TPU v7x, 32 devices: a whole 2x2x4 slice. The times are simulated.
32 devices in a mesh: ulysses: 2 (over x), blk: 16 (over z, y, core).
Axes of the slice: x: 2, y: 2, z: 4, core: 2. Of those that a mesh axis runs over, the one named last changes fastest.
Arguments:
- layer_input: bfloat16 [3, 3072, 768], P(None, ('ulysses', 'blk')), may hold values from -6 to 6
- query_key_value_weight: bfloat16 [768, 2304], P(('ulysses', 'blk')), may hold values from -0.21875 to 0.21875
- output_weight: bfloat16 [768, 768], P(('ulysses', 'blk')), may hold values from -1.75 to 1.75
- input_weight: bfloat16 [768, 3072], P(('ulysses', 'blk')), may hold values from -0.21875 to 0.21875
- down_weight: bfloat16 [3072, 768], P(('ulysses', 'blk')), may hold values from -0.109375 to 0.109375
- biases: bfloat16 [4, 768], P(None, ('ulysses', 'blk')), may hold values from -3 to 3
- hidden_unit_bias: bfloat16 [3072], P(('ulysses', 'blk')), may hold values from -3 to 3
- gains: bfloat16 [2, 768], P(None, ('ulysses', 'blk')), may hold values from 0.25 to 1.75
- shifts: bfloat16 [2, 768], P(None, ('ulysses', 'blk')), may hold values from -3 to 3
- cotangent: bfloat16 [3, 3072, 768], P(None, ('ulysses', 'blk')), may hold values from -6 to 6
- block_ids: int32 [3, 3072], replicated, may hold values from 0 to 23, never falling along the last dimension, each value on 1 to 256 neighbouring positions
- offsets: int32 [3], replicated, may hold values from 0 to 95
- pairing: int32 [12, 2], replicated, may hold values from 0 to 1, each once within a row
Outputs:
- hidden_out: bfloat16 [3, 3072, 768], P(None, ('ulysses', 'blk'))
- grad_input: bfloat16 [3, 3072, 768], P(None, ('ulysses', 'blk'))
- grad_w_qkv: float32 [768, 2304], P(('ulysses', 'blk'))
- grad_w_out: float32 [768, 768], P(('ulysses', 'blk'))
- grad_w_in: float32 [768, 3072], P(('ulysses', 'blk'))
- grad_w_down: float32 [3072, 768], P(('ulysses', 'blk'))
- grad_biases: float32 [4, 768], P(None, ('ulysses', 'blk'))
- grad_bias_in: float32 [3072], P(('ulysses', 'blk'))
- grad_gains: float32 [2, 768], P(None, ('ulysses', 'blk'))
- grad_shifts: float32 [2, 768], P(None, ('ulysses', 'blk'))
Inputs may be any that keep to these rules, and one draw needn't show every extreme that they name: `block_ids`: along each sequence the block numbers never fall, and no block holds more than 256 tokens. `pairing`: each row names every large block once.
All inputs are finite; a program needn't handle non-finite values.
Results may differ from a plain program's by a relative error of at most 0.019.
Values may be sent and summed in bfloat16 or wider, within the bound.
No kernel may reach another device: no remote copies, remote signals or barrier semaphores. Data moves between devices by JAX's collectives and lax.ppermute only.
A program may use at most 320 MiB of HBM per device.

v0:
```python
import jax
import jax.numpy as jnp
from jax import lax
from jax.sharding import PartitionSpec as P

H = 12
HD = 64


NEG_FILL = -1e30
NORM_EPS = 1e-12


def layer_norm(summed, gain_row, shift_row):
    average = jnp.mean(summed, axis=-1, keepdims=True)
    centred = summed - average
    inv_std = lax.rsqrt(jnp.mean(centred * centred, axis=-1, keepdims=True) + NORM_EPS)
    normed = centred * inv_std
    return (normed * gain_row + shift_row, normed, inv_std)


def norm_back(incoming, normed, inv_std, gain_row):
    scaled = incoming * gain_row
    return inv_std * (
        scaled
        - jnp.mean(scaled, axis=-1, keepdims=True)
        - normed * jnp.mean(scaled * normed, axis=-1, keepdims=True)
    )


def gelu_exact(inner_hidden):
    return jax.nn.gelu(inner_hidden, approximate=False)


def each_shard(step_fn, running, pieces):
    shards = pieces[0].shape[1]

    def one_turn(turn_idx, state):
        slices = tuple((lax.dynamic_slice_in_dim(member, turn_idx, 1, 1) for member in pieces))
        return step_fn(state, slices, turn_idx)

    return lax.fori_loop(0, shards, one_turn, running)


def per_device(
    layer_input,
    query_key_value_weight,
    output_weight,
    input_weight,
    down_weight,
    biases,
    hidden_unit_bias,
    gains,
    shifts,
    cotangent,
    block_ids,
    offsets,
    pairing,
):
    num_seqs, seq_rows, model_width = layer_input.shape
    narrow = lax.axis_size("ulysses")
    wide_size = lax.axis_size("blk")
    heads_here = H // narrow
    feat_here = heads_here * HD
    half_len = wide_size * seq_rows
    me_narrow = lax.axis_index("ulysses")
    me_wide = lax.axis_index("blk")
    score_scale = HD ** (-0.5)
    fetched = (
        lax.all_gather(query_key_value_weight, ("ulysses", "blk"), axis=0, tiled=True),
        lax.all_gather(output_weight, ("ulysses", "blk"), axis=0, tiled=True),
        lax.all_gather(input_weight, ("ulysses", "blk"), axis=0, tiled=True),
        lax.all_gather(down_weight, ("ulysses", "blk"), axis=0, tiled=True),
        lax.all_gather(biases, ("ulysses", "blk"), axis=1, tiled=True),
        lax.all_gather(hidden_unit_bias, ("ulysses", "blk"), axis=0, tiled=True),
        lax.all_gather(gains, ("ulysses", "blk"), axis=1, tiled=True),
        lax.all_gather(shifts, ("ulysses", "blk"), axis=1, tiled=True),
    )
    wq_all, wo_all, wi_all, wd_all, bias_all, bin_all, gain_all, shift_all = fetched
    bias_f = bias_all.astype(jnp.float32)
    gain_f = gain_all.astype(jnp.float32)
    shift_f = shift_all.astype(jnp.float32)
    projected_rows = jnp.einsum(
        "scd,de->sce", layer_input, wq_all, preferred_element_type=jnp.float32
    )
    query = (projected_rows[..., :model_width] + bias_f[0]).astype(jnp.bfloat16)
    key = projected_rows[..., model_width : 2 * model_width].astype(jnp.bfloat16)
    value = (projected_rows[..., 2 * model_width :] + bias_f[1]).astype(jnp.bfloat16)
    query_h, key_h, value_h = (
        lax.all_to_all(query[:, None], "ulysses", split_axis=3, concat_axis=1, tiled=True),
        lax.all_to_all(key[:, None], "ulysses", split_axis=3, concat_axis=1, tiled=True),
        lax.all_to_all(value[:, None], "ulysses", split_axis=3, concat_axis=1, tiled=True),
    )
    q_own = query_h.reshape(num_seqs, narrow, seq_rows, heads_here, HD)
    k_own = key_h.reshape(num_seqs, narrow, seq_rows, heads_here, HD)
    v_own = value_h.reshape(num_seqs, narrow, seq_rows, heads_here, HD)
    pair_here = lax.dynamic_slice_in_dim(pairing, me_narrow * heads_here, heads_here, 0)
    halves = jnp.arange(narrow, dtype=jnp.int32)
    pair_sel = pair_here.T
    chooser = pair_sel[:, None, :] == halves[None, :, None]
    chooser_bf = chooser.astype(jnp.bfloat16)
    chooser_int = chooser.astype(jnp.int32)
    chooser_q = jnp.transpose(chooser, (1, 0, 2))
    chooser_q_bf = chooser_q.astype(jnp.bfloat16)
    chooser_q_int = chooser_q.astype(jnp.int32)
    ids_grid = block_ids.reshape(num_seqs, narrow, wide_size, seq_rows)
    own_ids = lax.dynamic_index_in_dim(ids_grid, me_wide, 2, keepdims=False)
    iota_rows = jnp.arange(seq_rows, dtype=jnp.int32)
    own_pos = halves[:, None] * half_len + me_wide * seq_rows + iota_rows[None, :]
    own_valid = own_pos[None] >= offsets[:, None, None]

    def key_mask(first_row, shard_count):
        ids_rows = lax.dynamic_slice_in_dim(ids_grid, first_row, shard_count, 2)
        ids_sel = jnp.sum(
            chooser_int[None, :, :, :, None, None] * ids_rows[:, None, :, None, :, :], axis=2
        )
        slots = (first_row + jnp.arange(shard_count, dtype=jnp.int32))[
            :, None
        ] * seq_rows + iota_rows[None, :]
        positions = pair_sel[:, :, None, None] * half_len + slots[None, None]
        later = ids_sel[:, :, None] <= own_ids[:, :, :, None, None, None]
        return later & (positions[None, :, None] >= offsets[:, None, None, None, None, None])

    def query_mask(first_row, shard_count):
        ids_rows = lax.dynamic_slice_in_dim(ids_grid, first_row, shard_count, 2)
        ids_sel = jnp.sum(
            chooser_q_int[None, :, :, None, None, :] * ids_rows[:, None, :, :, :, None], axis=2
        )
        ids_sel = jnp.moveaxis(ids_sel, 2, 1)
        later = own_ids[:, None, :, None, None, :] <= ids_sel[..., None]
        return later & own_valid[:, None, :, None, None, :]

    def select_keys(member):
        shaped = member.reshape(member.shape[:4] + (heads_here, HD))
        return jnp.einsum(
            "sjuchd,auh->sjachd", shaped, chooser_bf, preferred_element_type=jnp.float32
        ).astype(jnp.bfloat16)

    def select_queries(member):
        shaped = member.reshape(member.shape[:4] + (heads_here, HD))
        return jnp.einsum(
            "sjachd,uah->sjuchd", shaped, chooser_q_bf, preferred_element_type=jnp.float32
        ).astype(jnp.bfloat16)

    def select_stats(stat):
        picked = jnp.where(chooser_q[None, None, :, :, None, :], stat[:, :, None], 0.0)
        return jnp.sum(picked, axis=3)

    def forward_step(running, pieces, first_row):
        maxima, totals, weighted = running
        key_rows, value_rows = pieces
        key_sel = select_keys(key_rows)
        value_sel = select_keys(value_rows)
        visible = key_mask(first_row, key_rows.shape[1])
        scores = (
            jnp.einsum("sachd,sjakhd->sachjk", q_own, key_sel, preferred_element_type=jnp.float32)
            * score_scale
        )
        new_max = jnp.maximum(maxima, jnp.max(jnp.where(visible, scores, NEG_FILL), axis=(4, 5)))
        exponent = jnp.exp(jnp.where(visible, scores - new_max[..., None, None], -jnp.inf))
        factor = jnp.exp(maxima - new_max)
        totals = totals * factor + jnp.sum(exponent, axis=(4, 5))
        weighted = weighted * factor[..., None] + jnp.einsum(
            "sachjk,sjakhd->sachd",
            exponent.astype(jnp.bfloat16),
            value_sel,
            preferred_element_type=jnp.float32,
        )
        return (new_max, totals, weighted)

    stat_shape = (num_seqs, narrow, seq_rows, heads_here)
    start_state = (
        jnp.full(stat_shape, NEG_FILL, jnp.float32),
        jnp.zeros(stat_shape, jnp.float32),
        jnp.zeros(stat_shape + (HD,), jnp.float32),
    )
    maxima, totals, weighted = each_shard(
        forward_step,
        start_state,
        (
            lax.all_gather(key_h[:, None], "blk", axis=1, tiled=True),
            lax.all_gather(value_h[:, None], "blk", axis=1, tiled=True),
        ),
    )
    totals_safe = jnp.maximum(totals, 1.0)
    attended = weighted / totals_safe[..., None]
    log_total = maxima + jnp.log(totals_safe)
    att_send = attended.astype(jnp.bfloat16).reshape(num_seqs, narrow, seq_rows, feat_here)
    att_tok = lax.all_to_all(att_send, "ulysses", split_axis=1, concat_axis=3, tiled=True).reshape(
        num_seqs, seq_rows, model_width
    )
    projected_att = (
        jnp.einsum("scd,de->sce", att_tok, wo_all, preferred_element_type=jnp.float32) + bias_f[2]
    )
    middle_activations, normed_one, inv_one = layer_norm(
        layer_input.astype(jnp.float32) + projected_att, gain_f[0], shift_f[0]
    )
    mid_low = middle_activations.astype(jnp.bfloat16)
    inner_hidden = jnp.einsum(
        "scd,df->scf", mid_low, wi_all, preferred_element_type=jnp.float32
    ) + bin_all.astype(jnp.float32)
    active_units, gelu_pull = jax.vjp(gelu_exact, inner_hidden)
    active_low = active_units.astype(jnp.bfloat16)
    feedforward_output = (
        jnp.einsum("scf,fd->scd", active_low, wd_all, preferred_element_type=jnp.float32)
        + bias_f[3]
    )
    second, normed_two, inv_two = layer_norm(
        middle_activations + feedforward_output, gain_f[1], shift_f[1]
    )
    hidden_out = second.astype(jnp.bfloat16)
    wq_back, wo_back, wi_back, wd_back = (
        lax.all_gather(query_key_value_weight, ("ulysses", "blk"), axis=0, tiled=True),
        lax.all_gather(output_weight, ("ulysses", "blk"), axis=0, tiled=True),
        lax.all_gather(input_weight, ("ulysses", "blk"), axis=0, tiled=True),
        lax.all_gather(down_weight, ("ulysses", "blk"), axis=0, tiled=True),
    )
    grad_out = cotangent.astype(jnp.float32)
    dgain_two = jnp.sum(grad_out * normed_two, axis=(0, 1))
    dshift_two = jnp.sum(grad_out, axis=(0, 1))
    dsecond = norm_back(grad_out, normed_two, inv_two, gain_f[1])
    dfeed = dsecond.astype(jnp.bfloat16)
    dbias_out = jnp.sum(dfeed.astype(jnp.float32), axis=(0, 1))
    dw_down = jnp.einsum("scf,scd->fd", active_low, dfeed, preferred_element_type=jnp.float32)
    dactive = jnp.einsum("scd,fd->scf", dfeed, wd_back, preferred_element_type=jnp.float32)
    dinner = gelu_pull(dactive)[0].astype(jnp.bfloat16)
    dbias_in = jnp.sum(dinner.astype(jnp.float32), axis=(0, 1))
    dw_in = jnp.einsum("scd,scf->df", mid_low, dinner, preferred_element_type=jnp.float32)
    dmid = dsecond + jnp.einsum("scf,df->scd", dinner, wi_back, preferred_element_type=jnp.float32)
    dgain_one = jnp.sum(dmid * normed_one, axis=(0, 1))
    dshift_one = jnp.sum(dmid, axis=(0, 1))
    dsum_one = norm_back(dmid, normed_one, inv_one, gain_f[0])
    dproj = dsum_one.astype(jnp.bfloat16)
    dbias_o = jnp.sum(dproj.astype(jnp.float32), axis=(0, 1))
    dw_out = jnp.einsum("scd,sce->de", att_tok, dproj, preferred_element_type=jnp.float32)
    datt = jnp.einsum("sce,de->scd", dproj, wo_back, preferred_element_type=jnp.float32).astype(
        jnp.bfloat16
    )
    dout_h = lax.all_to_all(
        datt.reshape(num_seqs, 1, seq_rows, model_width),
        "ulysses",
        split_axis=3,
        concat_axis=1,
        tiled=True,
    )
    dout_rows = dout_h.reshape(num_seqs, narrow, seq_rows, heads_here, HD)
    delta = jnp.sum(dout_rows.astype(jnp.float32) * attended, axis=-1)

    def query_grad_step(running, pieces, first_row):
        key_rows, value_rows = pieces
        key_sel = select_keys(key_rows)
        value_sel = select_keys(value_rows)
        visible = key_mask(first_row, key_rows.shape[1])
        scores = (
            jnp.einsum("sachd,sjakhd->sachjk", q_own, key_sel, preferred_element_type=jnp.float32)
            * score_scale
        )
        probabilities = jnp.exp(jnp.where(visible, scores - log_total[..., None, None], -jnp.inf))
        dprob = jnp.einsum(
            "sachd,sjakhd->sachjk", dout_rows, value_sel, preferred_element_type=jnp.float32
        )
        dscore = (probabilities * (dprob - delta[..., None, None])).astype(jnp.bfloat16)
        return running + jnp.einsum(
            "sachjk,sjakhd->sachd", dscore, key_sel, preferred_element_type=jnp.float32
        )

    zeros_rows = jnp.zeros(stat_shape + (HD,), jnp.float32)
    dquery = each_shard(
        query_grad_step,
        zeros_rows,
        (
            lax.all_gather(key_h[:, None], "blk", axis=1, tiled=True),
            lax.all_gather(value_h[:, None], "blk", axis=1, tiled=True),
        ),
    )
    dquery = (
        (dquery * score_scale).astype(jnp.bfloat16).reshape(num_seqs, narrow, seq_rows, feat_here)
    )
    stats_lse, stats_delta = (
        lax.all_gather(log_total[:, None], "blk", axis=1, tiled=True),
        lax.all_gather(delta[:, None], "blk", axis=1, tiled=True),
    )

    def key_grad_step(running, pieces, first_row):
        dkey_run, dvalue_run = running
        query_rows, dout_piece = pieces
        shard_count = query_rows.shape[1]
        query_sel = select_queries(query_rows)
        dout_sel = select_queries(dout_piece)
        lse_sel = select_stats(lax.dynamic_slice_in_dim(stats_lse, first_row, shard_count, 1))
        delta_sel = select_stats(lax.dynamic_slice_in_dim(stats_delta, first_row, shard_count, 1))
        visible = query_mask(first_row, shard_count)
        scores = (
            jnp.einsum("sjuqhd,sukhd->sjuqhk", query_sel, k_own, preferred_element_type=jnp.float32)
            * score_scale
        )
        probabilities = jnp.exp(jnp.where(visible, scores - lse_sel[..., None], -jnp.inf))
        dprob = jnp.einsum(
            "sjuqhd,sukhd->sjuqhk", dout_sel, v_own, preferred_element_type=jnp.float32
        )
        dscore = (probabilities * (dprob - delta_sel[..., None])).astype(jnp.bfloat16)
        dvalue_run = dvalue_run + jnp.einsum(
            "sjuqhk,sjuqhd->sukhd",
            probabilities.astype(jnp.bfloat16),
            dout_sel,
            preferred_element_type=jnp.float32,
        )
        dkey_run = dkey_run + jnp.einsum(
            "sjuqhk,sjuqhd->sukhd", dscore, query_sel, preferred_element_type=jnp.float32
        )
        return (dkey_run, dvalue_run)

    dkey, dvalue = each_shard(
        key_grad_step,
        (zeros_rows, zeros_rows),
        (
            lax.all_gather(query_h[:, None], "blk", axis=1, tiled=True),
            lax.all_gather(dout_h[:, None], "blk", axis=1, tiled=True),
        ),
    )
    dkey = (dkey * score_scale).astype(jnp.bfloat16).reshape(num_seqs, narrow, seq_rows, feat_here)
    dvalue = dvalue.astype(jnp.bfloat16).reshape(num_seqs, narrow, seq_rows, feat_here)
    dq_tok, dk_tok, dv_tok = (
        lax.all_to_all(dquery, "ulysses", split_axis=1, concat_axis=3, tiled=True),
        lax.all_to_all(dkey, "ulysses", split_axis=1, concat_axis=3, tiled=True),
        lax.all_to_all(dvalue, "ulysses", split_axis=1, concat_axis=3, tiled=True),
    )
    dprojected = jnp.concatenate([dq_tok, dk_tok, dv_tok], axis=3).reshape(
        num_seqs, seq_rows, 3 * model_width
    )
    dw_qkv = jnp.einsum("scd,sce->de", layer_input, dprojected, preferred_element_type=jnp.float32)
    grad_input = (
        dsum_one
        + jnp.einsum("sce,de->scd", dprojected, wq_back, preferred_element_type=jnp.float32)
    ).astype(jnp.bfloat16)
    dbias_q = jnp.sum(dq_tok.astype(jnp.float32), axis=(0, 1, 2))
    dbias_v = jnp.sum(dv_tok.astype(jnp.float32), axis=(0, 1, 2))
    dbiases = jnp.stack([dbias_q, dbias_v, dbias_o, dbias_out])
    dgains = jnp.stack([dgain_one, dgain_two])
    dshifts = jnp.stack([dshift_one, dshift_two])
    shares = (
        lax.psum_scatter(dw_qkv, ("ulysses", "blk"), scatter_dimension=0, tiled=True),
        lax.psum_scatter(dw_out, ("ulysses", "blk"), scatter_dimension=0, tiled=True),
        lax.psum_scatter(dw_in, ("ulysses", "blk"), scatter_dimension=0, tiled=True),
        lax.psum_scatter(dw_down, ("ulysses", "blk"), scatter_dimension=0, tiled=True),
        lax.psum_scatter(dbiases, ("ulysses", "blk"), scatter_dimension=1, tiled=True),
        lax.psum_scatter(dbias_in, ("ulysses", "blk"), scatter_dimension=0, tiled=True),
        lax.psum_scatter(dgains, ("ulysses", "blk"), scatter_dimension=1, tiled=True),
        lax.psum_scatter(dshifts, ("ulysses", "blk"), scatter_dimension=1, tiled=True),
    )
    return (
        hidden_out,
        grad_input,
        shares[0],
        shares[1],
        shares[2],
        shares[3],
        shares[4],
        shares[5],
        shares[6],
        shares[7],
    )


def solution(mesh):
    placed = (
        P(None, ("ulysses", "blk"), None),
        P(("ulysses", "blk"), None),
        P(("ulysses", "blk"), None),
        P(("ulysses", "blk"), None),
        P(("ulysses", "blk"), None),
        P(None, ("ulysses", "blk")),
        P(("ulysses", "blk")),
        P(None, ("ulysses", "blk")),
        P(None, ("ulysses", "blk")),
        P(None, ("ulysses", "blk"), None),
        P(),
        P(),
        P(),
    )
    return jax.shard_map(
        per_device,
        mesh=mesh,
        in_specs=placed,
        out_specs=(
            P(None, ("ulysses", "blk"), None),
            P(None, ("ulysses", "blk"), None),
            P(("ulysses", "blk"), None),
            P(("ulysses", "blk"), None),
            P(("ulysses", "blk"), None),
            P(("ulysses", "blk"), None),
            P(None, ("ulysses", "blk")),
            P(("ulysses", "blk")),
            P(None, ("ulysses", "blk")),
            P(None, ("ulysses", "blk")),
        ),
        check_vma=False,
    )
```

profile of v0, /device:TPU:8, one launch (start us, length us, event | category | flops | bytes accessed | tf_op | source)
XLA Modules:
  0.0 1238.7 jit_solution(13250866393834870120)
XLA Ops:
  8.0 38.4 %all-gather.6 = bf16[32,24,4]{1,2,0:T(4,128)(2,1)S(1)} all-gather(bf16[1,24,4]{1,2,0:T(4,128)(2,1)} %bitcast.479), channel_id=1, replica_groups=mesh['ulysses'=2,'blk'=16] {'ulysses','blk'}, dimensions={0}, use_global_device_ids=true | all-gather | bytes 6336 | tf_op jit(solution)/shard_map/all_gather | solution.py:74
  46.7 25.0 %all-gather.18.cloned.1.call-done = bf16[768,2304]{1,0:T(8,128)(2,1)} async-done(((bf16[24,2304]{1,0:T(8,128)(2,1)}), bf16[768,2304]{1,0:T(8,128)(2,1)}) %all-gather.18.cloned.1.call-update) | async-done | bytes 3538960 | tf_op jit(solution)/shard_map/all_gather | solution.py:70
  77.6 14.7 %all_to_all.129 = bf16[3,1,96,768]{2,0,1,3:T(4,128)(2,1)} all-to-all(bf16[3,1,96,768]{2,0,1,3:T(4,128)(2,1)S(1)} %copy.573), channel_id=1, replica_groups=mesh['ulysses'=2,'blk'=16] {'ulysses'}, dimensions={3} | all-to-all | bytes 884736 | tf_op jit(solution)/shard_map/all_to_all | solution.py:92
  97.9 13.2 %all_to_all.130 = bf16[3,1,96,768]{2,0,1,3:T(4,128)(2,1)S(1)} all-to-all(bf16[3,1,96,768]{2,0,1,3:T(4,128)(2,1)S(1)} %copy.565), channel_id=1, replica_groups=mesh['ulysses'=2,'blk'=16] {'ulysses'}, dimensions={3} | all-to-all | bytes 884736 | tf_op jit(solution)/shard_map/all_to_all | solution.py:91
  121.3 37.9 %all-gather.7 = bf16[32,24,2]{1,2,0:T(2,128)(2,1)S(1)} all-gather(bf16[1,24,2]{1,2,0:T(2,128)(2,1)S(1)} %bitcast.480), channel_id=1, replica_groups=mesh['ulysses'=2,'blk'=16] {'ulysses','blk'}, dimensions={0}, use_global_device_ids=true | all-gather | bytes 3168 | tf_op jit(solution)/shard_map/all_gather | solution.py:76
  159.5 36.5 %all-gather.8 = bf16[32,24,2]{1,2,0:T(2,128)(2,1)S(1)} all-gather(bf16[1,24,2]{1,2,0:T(2,128)(2,1)S(1)} %bitcast.481), channel_id=1, replica_groups=mesh['ulysses'=2,'blk'=16] {'ulysses','blk'}, dimensions={0}, use_global_device_ids=true | all-gather | bytes 3168 | tf_op jit(solution)/shard_map/all_gather | solution.py:77
  196.5 43.0 %all-reduce = bf16[3072]{0:T(1024)(128)(2,1)S(1)} all-reduce(bf16[3072]{0:T(1024)(128)(2,1)S(1)} %dynamic-update-slice), channel_id=1, replica_groups=mesh['ulysses'=2,'blk'=16] {'ulysses','blk'}, use_global_device_ids=true, to_apply=%add | all-reduce | flops 3072 | bytes 12288
  241.1 11.4 copy.579
  252.5 11.4 copy.578
  263.9 280.8 %while.54 = (s32[]{:T(128)}, f32[3,2,96,6]{2,3,1,0:T(8,128)S(1)}, f32[3,2,96,6]{2,3,1,0:T(8,128)S(1)}, f32[3,2,96,6,64]{2,4,3,1,0:T(8,128)}, s32[3,2,16,96]{3,1,...) while((s32[]{:T(128)}, f32[3,2,96,6]{2,3,1,0:T(8,128)S(1)}, ...), condition=%wide.region_4.5_spmd.clone.clone.clone, body=%wide.region_0.4_spmd.clone.clone.clone.sunk | while | flops 93482752 | bytes 18009740 | solution.py:42
  321.4 4.1 fusion.240
  409.2 4.1 fusion.240
  426.7 4.1 fusion.240
  461.8 4.1 fusion.240
  479.4 4.1 fusion.240
  551.0 7.0 all-to-all-done.3
  561.0 5.1 fusion.149
  567.9 9.0 multiply_convert_fusion
  577.0 4.7 fusion.166
  595.6 13.4 %all_to_all.131 = bf16[3,1,96,768]{2,0,1,3:T(4,128)(2,1)S(1)} all-to-all(bf16[3,1,96,768]{2,0,1,3:T(4,128)(2,1)} %copy.589), channel_id=1, replica_groups=mesh['ulysses'=2,'blk'=16] {'ulysses'}, dimensions={3} | all-to-all | bytes 884736 | tf_op jit(solution)/shard_map/all_to_all | solution.py:239
  612.4 7.9 convolution_bitcast_fusion.4
  625.0 19.5 %all-gather.3 = f32[3,32,96,6]{2,3,0,1:T(8,128)S(1)} all-gather(f32[3,2,96,6]{2,3,0,1:T(8,128)S(1)} %get-tuple-element.1628), channel_id=5, replica_groups=mesh['ulysses'=2,'blk'=16] {'blk'}, dimensions={1}, use_global_device_ids=true | all-gather | bytes 235008 | tf_op jit(solution)/shard_map/all_gather | solution.py:280
  645.4 6.8 convolution_bitcast_fusion.5
  656.8 173.5 %while.55 = (s32[]{:T(128)}, f32[3,2,96,6,64]{2,4,3,1,0:T(8,128)}, bf16[3,16,2,96,384]{3,4,2,0,1:T(8,128)(2,1)}, s32[3,2,16,96]{3,1,0,2:T(2,128)}, s32[3,2,96]{2...) while((s32[]{:T(128)}, f32[3,2,96,6,64]{2,4,3,1,0:T(8,128)}, ...), condition=%wide.region_16.17_spmd.clone.clone.clone, body=%wide.region_14.16_spmd.clone.clone.clone.sunk | while | flops 132725632 | bytes 12026231 | solution.py:42
  674.2 4.2 fusion.258
  685.1 4.1 fusion.258
  695.9 4.1 fusion.258
  706.8 4.1 fusion.258
  717.6 4.1 fusion.258
  728.5 4.1 fusion.258
  739.4 4.1 fusion.258
  750.2 4.1 fusion.258
  771.9 4.1 fusion.258
  782.7 4.1 fusion.258
  793.5 4.1 fusion.258
  804.4 4.1 fusion.258
  815.2 4.1 fusion.258
  826.2 4.1 fusion.258
  832.9 4.2 all-to-all-start.5
  837.1 18.8 %all-gather.5 = f32[3,32,96,6]{2,3,0,1:T(8,128)S(1)} all-gather(f32[3,2,96,6]{2,3,0,1:T(8,128)S(1)} %copy-done.25), channel_id=7, replica_groups=mesh['ulysses'=2,'blk'=16] {'blk'}, dimensions={1}, use_global_device_ids=true | all-gather | bytes 235008 | tf_op jit(solution)/shard_map/all_gather | solution.py:281
  856.8 217.0 %while.56 = (s32[]{:T(128)}, f32[3,2,96,6,64]{2,4,3,1,0:T(8,128)}, f32[3,2,96,6,64]{2,4,3,1,0:T(8,128)S(1)}, bf16[3,16,2,96,384]{3,4,2,1,0:T(8,128)(2,1)}, s32[3...) while((s32[]{:T(128)}, f32[3,2,96,6,64]{2,4,3,1,0:T(8,128)}, ...), condition=%wide.region_21.22_spmd.clone.clone.clone, body=%wide.region_17.21_spmd.clone.clone.clone.sunk | while | flops 175983696 | bytes 17430000 | solution.py:42
  1081.0 6.6 all-to-all-done.6
  1092.2 5.8 all-to-all-done.7
  1098.1 4.9 convolution_bitcast_fusion.6
  1103.0 8.0 copy.633
  1117.1 42.3 %all-reduce.5 = (f32[4,768]{1,0:T(4,128)S(1)}, f32[3072]{0:T(1024)S(1)}, f32[2,768]{1,0:T(2,128)S(1)}, f32[2,768]{1,0:T(2,128)S(1)}) all-reduce(f32[4,768]{1,0:T(4,128)S(1)} %pad_maximum_fusion, f32[3072]{0:T(1024)} %get-tuple-element.1636, ...), channel_id=12, replica_groups=mesh['ulysses'=2,'blk'=16] {'ulysses','blk'}, use_global_device_ids=true, to_apply=%region_30.31.clone | all-reduce | flops 9216 | bytes 73728
  1161.9 4.1 fusion.133
  1166.0 65.4 %reduce-scatter.16.cloned.1.call-done = f32[24,2304]{1,0:T(8,128)} async-done(((f32[768,2304]{1,0:T(8,128)}), f32[24,2304]{1,0:T(8,128)}) %reduce-scatter.16.cloned.1.call-update) | async-done | bytes 221200
  (1054 shorter events, 677.4 us)
Async XLA Ops:
  7.2 113.3 %copy-start = (s32[12,2]{0,1:T(2,128)S(1)}, s32[12,2]{0,1:T(2,128)}, u32[]{:S(2)}) copy-start(s32[12,2]{0,1:T(2,128)} %param.31) | copy-start | bytes 292
  7.2 64.5 %all-gather.18.cloned.1.call-start = ((), (), s32[]{:S(2)}) async-start(), calls=%async_computation.12 | async-start | bytes 3649536 | tf_op jit(solution)/shard_map/all_gather | solution.py:70
  7.9 233.2 %all-gather.28.cloned.1.call-start = ((), (), s32[]{:S(2)}) async-start(), calls=%async_computation.20 | async-start | bytes 7520256 | tf_op jit(solution)/shard_map/all_gather | solution.py:182
  95.5 19.1 %copy-start.28 = (s32[3,3072]{1,0:T(4,128)S(1)}, s32[3,3072]{1,0:T(4,128)}, u32[]{:S(2)}) copy-start(s32[3,3072]{1,0:T(4,128)} %param.29) | copy-start | bytes 110596
  95.5 157.0 %all-gather.26.cloned.1.call-start = ((), (), s32[]{:S(2)}) async-start(), calls=%async_computation.19 | async-start | bytes 7520256 | tf_op jit(solution)/shard_map/all_gather | solution.py:181
  97.8 23.5 %copy-start.35 = (bf16[2,24]{1,0:T(2,128)(2,1)S(1)}, bf16[2,24]{1,0:T(2,128)(2,1)}, u32[]{:S(2)}) copy-start(bf16[2,24]{1,0:T(2,128)(2,1)} %param.26) | copy-start | bytes 292
  97.8 61.6 %copy-start.36 = (bf16[2,24]{1,0:T(2,128)(2,1)S(1)}, bf16[2,24]{1,0:T(2,128)(2,1)}, u32[]{:S(2)}) copy-start(bf16[2,24]{1,0:T(2,128)(2,1)} %param.27) | copy-start | bytes 292
  97.8 98.4 %copy-start.38 = (bf16[96]{0:T(256)(128)(2,1)S(1)}, bf16[96]{0:T(256)(128)(2,1)}, u32[]{:S(2)}) copy-start(bf16[96]{0:T(256)(128)(2,1)} %param.25) | copy-start | bytes 580
  111.9 140.6 %copy-start.10 = (bf16[3,1,96,2,384]{4,3,2,0,1:T(2,128)(2,1)}, bf16[3,1,96,2,384]{4,3,2,0,1:T(2,128)(2,1)S(1)}, u32[]{:S(2)}) copy-start(bf16[3,1,96,2,384]{4,3,2,0,1:T(2,128)(2,1)S(1)} %copy.619) | copy-start | bytes 1327108
  112.8 445.9 %all-gather.20.cloned.1.call-start = ((), (), s32[]{:S(2)}) async-start(), calls=%async_computation.13 | async-start | bytes 1216512 | tf_op jit(solution)/shard_map/all_gather | solution.py:71
  113.4 447.6 %all-gather.22.cloned.1.call-start = ((), (), s32[]{:S(2)}) async-start(), calls=%async_computation.14 | async-start | bytes 4866048 | tf_op jit(solution)/shard_map/all_gather | solution.py:72
  114.0 462.9 %all-gather.24.cloned.1.call-start = ((), (), s32[]{:S(2)}) async-start(), calls=%async_computation.15 | async-start | bytes 4866048 | tf_op jit(solution)/shard_map/all_gather | solution.py:73
  116.8 123.3 %all-to-all-start.1 = ((bf16[3,1,96,768]{2,0,1,3:T(4,128)(2,1)}), bf16[3,1,96,768]{2,0,1,3:T(4,128)(2,1)S(1)}, u32[]{:S(2)}, u32[]{:S(2)}) async-start(bf16[3,1,96,768]{2,0,1,3:T(4,128)(2,1)} %copy.571), calls=%async_computation.1 | async-start | bytes 1572864 | tf_op jit(solution)/shard_map/all_to_all | solution.py:90
  120.4 736.4 %all-gather.30.cloned.1.call-start = ((), (), s32[]{:S(2)}) async-start(), calls=%async_computation.21 | async-start | bytes 10027008 | tf_op jit(solution)/shard_map/all_gather | solution.py:317
  252.5 11.4 copy-start.2
  544.7 14.0 %copy-start.16 = (bf16[3,96,768]{2,1,0:T(8,128)(2,1)S(1)}, bf16[3,96,768]{2,1,0:T(8,128)(2,1)}, u32[]{:S(2)}) copy-start(bf16[3,96,768]{2,1,0:T(8,128)(2,1)} %param.19) | copy-start | bytes 1327108
  547.2 10.8 all-to-all-start.3
  550.8 306.0 %all-gather.32.cloned.1.call-start = ((), (), s32[]{:S(2)}) async-start(), calls=%async_computation.22 | async-start | bytes 10027008 | tf_op jit(solution)/shard_map/all_gather | solution.py:318
  558.7 7.5 copy-start.11
  560.7 84.7 %copy-start.5 = (f32[3,96,768]{2,1,0:T(8,128)}, f32[3,96,768]{2,1,0:T(8,128)S(1)}, u32[]{:S(2)}) copy-start(f32[3,96,768]{2,1,0:T(8,128)S(1)} %get-tuple-element.1631) | copy-start | bytes 2654212
  560.7 84.6 %copy-start.26 = (f32[3,96]{1,0:T(4,128)}, f32[3,96]{1,0:T(4,128)S(1)}, u32[]{:S(2)}) copy-start(f32[3,96]{1,0:T(4,128)S(1)} %broadcast_multiply_fusion.7) | copy-start | bytes 3460
  561.0 84.4 %copy-start.29 = (f32[3,96]{1,0:T(4,128)}, f32[3,96]{1,0:T(4,128)S(1)}, u32[]{:S(2)}) copy-start(f32[3,96]{1,0:T(4,128)S(1)} %add_rsqrt_fusion.1) | copy-start | bytes 3460
  576.9 7.7 copy-start.15
  576.9 7.7 copy-start.37
  590.3 18.6 %copy-start.33 = (f32[3,96]{1,0:T(4,128)}, f32[3,96]{1,0:T(4,128)S(1)}, u32[]{:S(2)}) copy-start(f32[3,96]{1,0:T(4,128)S(1)} %broadcast_multiply_fusion.2) | copy-start | bytes 3460
  590.4 18.6 %copy-start.34 = (f32[3,96]{1,0:T(4,128)}, f32[3,96]{1,0:T(4,128)S(1)}, u32[]{:S(2)}) copy-start(f32[3,96]{1,0:T(4,128)S(1)} %broadcast_multiply_fusion.3) | copy-start | bytes 3460
  592.2 17.8 %copy-start.12 = (bf16[3,96,768]{2,1,0:T(8,128)(2,1)S(1)}, bf16[3,96,768]{2,1,0:T(8,128)(2,1)}, u32[]{:S(2)}) copy-start(bf16[3,96,768]{2,1,0:T(8,128)(2,1)} %copy-done.11) | copy-start | bytes 1327108
  609.9 556.1 %reduce-scatter.10.cloned.1.call-start = ((), (), s32[]{:S(2)}) async-start(), calls=%async_computation.16 | async-start | bytes 2433024 | tf_op jit(solution)/shard_map/reduce_scatter | solution.py:343
  612.1 553.9 %reduce-scatter.14.cloned.1.call-start = ((), (), s32[]{:S(2)}) async-start(), calls=%async_computation.18 | async-start | bytes 9732096 | tf_op jit(solution)/shard_map/reduce_scatter | solution.py:345
  620.3 545.8 %reduce-scatter.12.cloned.1.call-start = ((), (), s32[]{:S(2)}) async-start(), calls=%async_computation.17 | async-start | bytes 9732096 | tf_op jit(solution)/shard_map/reduce_scatter | solution.py:344
  830.3 6.7 copy-start.25
  830.3 26.4 %copy-start.31 = (s32[2,96]{1,0:T(2,128)S(1)}, s32[2,96]{1,0:T(2,128)}, u32[]{:S(2)}) copy-start(s32[2,96]{1,0:T(2,128)} %iota_add_fusion.2) | copy-start | bytes 2308
  832.9 243.4 %all-to-all-start.5 = ((bf16[3,2,96,384]{3,2,0,1:T(8,128)(2,1)}), bf16[3,2,96,384]{3,2,0,1:T(8,128)(2,1)}, u32[]{:S(2)}, u32[]{:S(2)}) async-start(bf16[3,2,96,384]{3,2,0,1:T(8,128)(2,1)} %copy.595), calls=%async_computation.5 | async-start | bytes 884736 | tf_op jit(solution)/shard_map/all_to_all | solution.py:324
  869.9 5.3 copy-start.24
  897.1 5.4 copy-start.24
  951.4 5.4 copy-start.24
  965.2 5.4 copy-start.24
  978.9 5.3 copy-start.24
  1019.5 5.4 copy-start.24
  1076.2 21.8 %copy-start.17 = (bf16[3,96,768]{2,1,0:T(8,128)(2,1)S(1)}, bf16[3,96,768]{2,1,0:T(8,128)(2,1)}, u32[]{:S(2)}) copy-start(bf16[3,96,768]{2,1,0:T(8,128)(2,1)} %param.19) | copy-start | bytes 1327108
  1076.2 11.4 all-to-all-start.6
  1087.6 10.4 all-to-all-start.7
  1091.1 140.3 %reduce-scatter.16.cloned.1.call-start = ((), (), s32[]{:S(2)}) async-start(), calls=%async_computation.23 | async-start | bytes 7299072
  1111.0 50.9 %copy-start.6 = (f32[3,96,768]{2,1,0:T(8,128)S(1)}, f32[3,96,768]{2,1,0:T(8,128)}, u32[]{:S(2)}) copy-start(f32[3,96,768]{2,1,0:T(8,128)} %copy-done.5) | copy-start | bytes 2654212
  1111.0 50.9 %copy-start.23 = (f32[3,96,768]{2,1,0:T(8,128)S(1)}, f32[3,96,768]{2,1,0:T(8,128)}, u32[]{:S(2)}) copy-start(f32[3,96,768]{2,1,0:T(8,128)} %copy-done.22) | copy-start | bytes 2654212
  1111.0 50.9 %copy-start.27 = (f32[3,96]{1,0:T(4,128)S(1)}, f32[3,96]{1,0:T(4,128)}, u32[]{:S(2)}) copy-start(f32[3,96]{1,0:T(4,128)} %copy-done.26) | copy-start | bytes 3460
  1111.0 50.9 %copy-start.30 = (f32[3,96]{1,0:T(4,128)S(1)}, f32[3,96]{1,0:T(4,128)}, u32[]{:S(2)}) copy-start(f32[3,96]{1,0:T(4,128)} %copy-done.29) | copy-start | bytes 3460
  1161.3 70.1 %copy-start.1 = (s32[12,2]{0,1:T(2,128)S(1)}, s32[12,2]{0,1:T(2,128)}, u32[]{:S(2)}) copy-start(s32[12,2]{0,1:T(2,128)} %param.31) | copy-start | bytes 292
  (85 other events, 279.0 us)
Sparse Core Ops, SparseCore 0:
  10.9 60.7 all-gather.17
  95.6 65.8 all-gather.27
  164.4 66.4 all-gather.25
  233.6 51.9 all-gather.19
  288.3 63.9 all-gather.21
  355.1 62.4 all-gather.23
  419.9 79.0 all-gather.29
  610.0 81.3 all-gather.31
  697.2 97.8 reduce-scatter.9
  802.5 134.6 reduce-scatter.13
  943.6 134.6 reduce-scatter.11
  1111.2 120.1 reduce-scatter.15
where the time goes:
time: 1260 us; the launch traced here: 1240 us
  matrix products  465 us (37%)
  blocking collectives  278 us (22%)
  local copies, waits for them, and re-layouts  204 us (16%)
  other arithmetic  142 us (11%)
  waiting for transfers between devices  112 us (9%)
  starting transfers between devices  19.2 us (2%)
  between operations  15.3 us (1%)
    unnamed x2, blocking collectives  85.4 us
    dot_general x64, matrix products, select_keys(): jnp.einsum('sjuchd,auh->sjachd', shaped, chooser_bf, preferred_element_ty...  79.4 us
    unnamed x13, waiting for transfers between devices  67.8 us
    dot_general x16, matrix products, query_grad_step(): jnp.einsum('sachjk,sjakhd->sachd', dscore, key_sel, preferred_element_typ...  65.3 us
    dot_general x16, matrix products, forward_step(): jnp.einsum('sachd,sjakhd->sachjk', q_own, key_sel, preferred_element_type...  65.1 us
    dynamic_slice x48, local copies, waits for them, and re-layouts, one_turn(): lax.dynamic_slice_in_dim(member, turn_idx, 1, 1)  64 us
    dot_general x16, matrix products, key_grad_step(): jnp.einsum('sjuqhk,sjuqhd->sukhd', dscore, query_sel, preferred_element_t...  58.8 us
    dot_general x16, matrix products, forward_step(): jnp.einsum('sachjk,sjakhd->sachd', exponent.astype(jnp.bfloat16), value_s...  57.1 us
  transfers between devices with their start and end apart: 17, of which 5 were waited for; matrix products, arithmetic and copies ran while one was open for 63% of the time, Pallas kernels for 0%

commit v1 on v0

v1 whole, which is shorter than its diff:
```python
import functools

import jax
import jax.numpy as jnp
from jax import lax
from jax.experimental import pallas as pl
from jax.experimental.pallas import tpu as pltpu
from jax.sharding import Mesh
from jax.sharding import PartitionSpec as P

H = 12
HD = 64
TP = 4
HG = H // TP
NORM_EPS = 1e-12
FILL = -1e30
FLOOR = -1e29
ALL = ("u", "r", "t")
BF = jnp.bfloat16
F32 = jnp.float32
VMEM_LIMIT = 56 * 1024 * 1024


def layer_norm(summed, gain_row, shift_row):
    average = jnp.mean(summed, axis=-1, keepdims=True)
    centred = summed - average
    inv_std = lax.rsqrt(jnp.mean(centred * centred, axis=-1, keepdims=True) + NORM_EPS)
    normed = centred * inv_std
    return (normed * gain_row + shift_row, normed, inv_std)


def norm_back(incoming, normed, inv_std, gain_row):
    scaled = incoming * gain_row
    return inv_std * (
        scaled
        - jnp.mean(scaled, axis=-1, keepdims=True)
        - normed * jnp.mean(scaled * normed, axis=-1, keepdims=True)
    )


def gelu_exact(inner_hidden):
    return jax.nn.gelu(inner_hidden, approximate=False)


def dot_nt(a, b):
    return lax.dot_general(a, b, (((1,), (1,)), ((), ())), preferred_element_type=F32)


def dot_nn(a, b):
    return lax.dot_general(a, b, (((1,), (0,)), ((), ())), preferred_element_type=F32)


def chunk_of(shards):
    return 8 if shards % 8 == 0 else shards


def forward_kernel(rows, shards, pair_ref, begin_ref, last_ref, q_ref, kv0, kv1, kv2, end_ref, att_ref, lse_ref, m_ref, l_ref, acc_ref):
    seq = pl.program_id(0)
    group = chunk_of(shards)
    nq = TP * rows
    width = group * rows
    for h, kv_ref in enumerate((kv0, kv1, kv2)):
        query = q_ref[:, 0, :, h * 128 : (h + 1) * 128].reshape(nq, 128)
        end = end_ref[0, h]
        begin = begin_ref[seq * HG + h]
        m_ref[...] = jnp.full_like(m_ref, FLOOR)
        l_ref[...] = jnp.zeros_like(l_ref)
        acc_ref[...] = jnp.zeros_like(acc_ref)

        def step(c, _):
            kv = kv_ref[0, pl.ds(c * group, group), 0].reshape(width, 128)
            spot = lax.broadcasted_iota(jnp.int32, (nq, width), 1) + c * width
            seen = (spot < end) & (spot >= begin)
            scores = jnp.where(seen, dot_nt(query, kv), FILL)
            old = m_ref[...]
            new = jnp.maximum(old, jnp.max(scores, axis=1, keepdims=True))
            weights = jnp.exp(scores - new)
            factor = jnp.exp(old - new)
            m_ref[...] = new
            l_ref[...] = l_ref[...] * factor + jnp.sum(weights, axis=1, keepdims=True)
            acc_ref[...] = acc_ref[...] * factor + dot_nn(weights.astype(BF), kv)
            return 0

        lax.fori_loop(0, pl.cdiv(last_ref[seq * HG + h], width), step, 0)
        total = jnp.maximum(l_ref[...], 1.0)
        lse_ref[0, h] = m_ref[...] + jnp.log(total)
        att = (acc_ref[...] / total).astype(BF)
        att_ref[:, 0, :, h * HD : (h + 1) * HD] = att[:, HD:].reshape(TP, rows, HD)


def query_kernel(rows, shards, pair_ref, begin_ref, last_ref, q_ref, kv0, kv1, kv2, end_ref, lse_ref, delta_ref, dout_ref, dq_ref, acc_ref):
    seq = pl.program_id(0)
    group = chunk_of(shards)
    nq = TP * rows
    width = group * rows
    for h, kv_ref in enumerate((kv0, kv1, kv2)):
        query = q_ref[:, 0, :, h * 128 : (h + 1) * 128].reshape(nq, 128)
        dout = dout_ref[:, 0, :, h * 128 : (h + 1) * 128].reshape(nq, 128)
        end = end_ref[0, h]
        lse = lse_ref[0, h]
        delta = delta_ref[0, h]
        begin = begin_ref[seq * HG + h]
        acc_ref[...] = jnp.zeros_like(acc_ref)

        def step(c, _):
            kv = kv_ref[0, pl.ds(c * group, group), 0].reshape(width, 128)
            spot = lax.broadcasted_iota(jnp.int32, (nq, width), 1) + c * width
            seen = (spot < end) & (spot >= begin)
            scores = jnp.where(seen, dot_nt(query, kv), FILL)
            prob = jnp.exp(scores - lse)
            dscore = (prob * (dot_nt(dout, kv) - delta)).astype(BF)
            acc_ref[...] += dot_nn(dscore, kv)
            return 0

        lax.fori_loop(0, pl.cdiv(last_ref[seq * HG + h], width), step, 0)
        dq = (acc_ref[...] * (HD**-0.5)).astype(BF)
        dq_ref[:, 0, :, h * HD : (h + 1) * HD] = dq[:, :HD].reshape(TP, rows, HD)


def key_kernel(rows, shards, pair_ref, begin_ref, first_ref, place_ref, q_ref, do_ref, kv0, kv1, kv2, stat_ref, dkv_ref, acc_ref):
    seq = pl.program_id(0)
    group = chunk_of(shards)
    nk = TP * rows
    width = group * rows
    start = place_ref[0]
    for h, kv_ref in enumerate((kv0, kv1, kv2)):
        kv = kv_ref[0, :, 0].reshape(nk, 128)
        begin = begin_ref[seq * HG + h]
        acc_ref[...] = jnp.zeros_like(acc_ref)

        def step(c, _):
            query = q_ref[pl.ds(c * group, group), 0, :, h * 128 : (h + 1) * 128].reshape(width, 128)
            dout = do_ref[pl.ds(c * group, group), 0, :, h * 128 : (h + 1) * 128].reshape(width, 128)
            stat = stat_ref[0, h, :, pl.ds(pl.multiple_of(c * width, 128), width)]
            lse, delta, end = stat[0:1], stat[1:2], stat[2:3].astype(jnp.int32)
            spot = lax.broadcasted_iota(jnp.int32, (nk, width), 0) + start
            seen = (spot < end) & (spot >= begin)
            scores = jnp.where(seen, dot_nt(kv, query), FILL)
            prob = jnp.exp(scores - lse)
            dscore = (prob * (dot_nt(kv, dout) - delta)).astype(BF)
            acc_ref[...] += dot_nn(dscore, query) + dot_nn(prob.astype(BF), dout)
            return 0

        lax.fori_loop(first_ref[seq * HG + h] // width, shards // group, step, 0)
        dkv_ref[:, 0, :, h * 128 : (h + 1) * 128] = acc_ref[...].astype(BF).reshape(TP, rows, 128)


def keys_spec(h, shards, rows):
    return pl.BlockSpec((1, shards, 1, rows, 128), lambda s, pair, *_: (pair[h], 0, s, 0, h))


def attend_forward(q_loc, kv, pair, begin, last, end_col):
    _, shards, seqs, rows, _ = kv.shape
    nq = TP * rows
    row_spec = pl.BlockSpec((TP, 1, rows, 384), lambda s, *_: (0, s, 0, 0))
    col_spec = pl.BlockSpec((1, HG, nq, 1), lambda s, *_: (s, 0, 0, 0))
    return pl.pallas_call(
        functools.partial(forward_kernel, rows, shards),
        grid_spec=pltpu.PrefetchScalarGridSpec(
            num_scalar_prefetch=3,
            grid=(seqs,),
            in_specs=[row_spec] + [keys_spec(h, shards, rows) for h in range(HG)] + [col_spec],
            out_specs=[pl.BlockSpec((TP, 1, rows, HG * HD), lambda s, *_: (0, s, 0, 0)), col_spec],
            scratch_shapes=[pltpu.VMEM((nq, 1), F32), pltpu.VMEM((nq, 1), F32), pltpu.VMEM((nq, 128), F32)],
        ),
        out_shape=[
            jax.ShapeDtypeStruct((TP, seqs, rows, HG * HD), BF),
            jax.ShapeDtypeStruct((seqs, HG, nq, 1), F32),
        ],
        compiler_params=pltpu.CompilerParams(vmem_limit_bytes=VMEM_LIMIT),
        name="attend_forward",
    )(pair, begin, last, q_loc, kv, kv, kv, end_col)


def attend_query(q_loc, kv, pair, begin, last, end_col, lse, delta, dout):
    _, shards, seqs, rows, _ = kv.shape
    nq = TP * rows
    row_spec = pl.BlockSpec((TP, 1, rows, 384), lambda s, *_: (0, s, 0, 0))
    col_spec = pl.BlockSpec((1, HG, nq, 1), lambda s, *_: (s, 0, 0, 0))
    return pl.pallas_call(
        functools.partial(query_kernel, rows, shards),
        grid_spec=pltpu.PrefetchScalarGridSpec(
            num_scalar_prefetch=3,
            grid=(seqs,),
            in_specs=[row_spec]
            + [keys_spec(h, shards, rows) for h in range(HG)]
            + [col_spec, col_spec, col_spec, row_spec],
            out_specs=pl.BlockSpec((TP, 1, rows, HG * HD), lambda s, *_: (0, s, 0, 0)),
            scratch_shapes=[pltpu.VMEM((nq, 128), F32)],
        ),
        out_shape=jax.ShapeDtypeStruct((TP, seqs, rows, HG * HD), BF),
        compiler_params=pltpu.CompilerParams(vmem_limit_bytes=VMEM_LIMIT),
        name="attend_query",
    )(pair, begin, last, q_loc, kv, kv, kv, end_col, lse, delta, dout)


def attend_key(q_all, do_all, kv, pair, begin, first, place, stats):
    _, shards, seqs, rows, _ = kv.shape
    nk = TP * rows
    all_spec = pl.BlockSpec((shards, 1, rows, 384), lambda s, *_: (0, s, 0, 0))

    def own_keys(h):
        return pl.BlockSpec((1, TP, 1, rows, 128), lambda s, pair, begin, first, place: (pair[h], place[1], s, 0, h))

    return pl.pallas_call(
        functools.partial(key_kernel, rows, shards),
        grid_spec=pltpu.PrefetchScalarGridSpec(
            num_scalar_prefetch=4,
            grid=(seqs,),
            in_specs=[all_spec, all_spec]
            + [own_keys(h) for h in range(HG)]
            + [pl.BlockSpec((1, HG, 8, shards * rows), lambda s, *_: (s, 0, 0, 0))],
            out_specs=pl.BlockSpec((TP, 1, rows, 384), lambda s, *_: (0, s, 0, 0)),
            scratch_shapes=[pltpu.VMEM((nk, 128), F32)],
        ),
        out_shape=jax.ShapeDtypeStruct((TP, seqs, rows, 384), BF),
        compiler_params=pltpu.CompilerParams(vmem_limit_bytes=VMEM_LIMIT),
        name="attend_key",
    )(pair, begin, first, place, q_all, do_all, kv, kv, kv, stats)


def ring_gather(piece, axis):
    size = lax.axis_size(axis)
    me = lax.axis_index(axis)
    out = jnp.zeros((size,) + piece.shape, piece.dtype)
    out = lax.dynamic_update_index_in_dim(out, piece, me, 0)
    for k in range(1, size):
        piece = lax.ppermute(piece, axis, [(i, (i + 1) % size) for i in range(size)])
        out = lax.dynamic_update_index_in_dim(out, piece, (me - k) % size, 0)
    return out


def per_device(layer_input, wqkv, wo, wi, wd, biases, hidden_bias, gains, shifts, cotangent, block_ids, offsets, pairing):
    seqs, rows, width = layer_input.shape
    devices = lax.axis_size(ALL)
    ring = lax.axis_size("r")
    shards = ring * TP
    half = shards * rows
    tokens = seqs * rows
    me_u, me_r, me_t = lax.axis_index("u"), lax.axis_index("r"), lax.axis_index("t")
    part = wqkv.shape[0]
    fpart = wd.shape[0]
    hidden = wi.shape[1]
    cols_in = hidden // width

    def rows_of(m):
        return [m[:, k * width : (k + 1) * width] for k in range(m.shape[1] // width)]

    small = jnp.concatenate([biases.reshape(-1), hidden_bias, gains.reshape(-1), shifts.reshape(-1)])
    small = jnp.zeros((16, width), BF).at[0, : small.shape[0]].set(small)
    counts = [tokens] + [part] * 3 + [part] + [part] * cols_in + [fpart, 16]
    packed = jnp.concatenate([layer_input.reshape(tokens, width)] + rows_of(wqkv) + [wo] + rows_of(wi) + [wd, small])
    everything = lax.all_gather(packed, ALL, axis=0, tiled=False)
    marks = [0]
    for n in counts:
        marks.append(marks[-1] + n)

    def piece(i):
        return everything[:, marks[i] : marks[i + 1]]

    x_all = piece(0).reshape(2, shards, seqs, rows, width)
    wq, wk, wv = (piece(1 + i).reshape(devices * part, width) for i in range(3))
    wo_all = piece(4).reshape(devices * part, width)
    wi_all = [piece(5 + i).reshape(devices * part, width) for i in range(cols_in)]
    wd_all = piece(5 + cols_in).reshape(devices * fpart, width)
    small_all = piece(6 + cols_in)[:, 0].astype(F32)
    bias_f = small_all[:, : 4 * part].reshape(devices, 4, part).transpose(1, 0, 2).reshape(4, width)
    bin_f = small_all[:, 4 * part : 4 * part + fpart].reshape(-1)
    at = 4 * part + fpart
    gain_f = small_all[:, at : at + 2 * part].reshape(devices, 2, part).transpose(1, 0, 2).reshape(2, width)
    shift_f = small_all[:, at + 2 * part : at + 4 * part].reshape(devices, 2, part).transpose(1, 0, 2).reshape(2, width)

    def heads_of(m):
        return lax.dynamic_slice_in_dim(m.reshape(m.shape[0], H, HD), me_t * HG, HG, 1)

    wq_h, wk_h, wv_h = heads_of(wq), heads_of(wk), heads_of(wv)
    bq_h, bv_h = heads_of(bias_f[0:1]), heads_of(bias_f[1:2])
    wq_pad = jnp.concatenate([wq_h, jnp.zeros_like(wq_h)], 2).reshape(width, HG * 128)
    wkv = jnp.concatenate([wk_h, wv_h], 2).reshape(width, HG * 128)
    bq_pad = jnp.concatenate([bq_h, jnp.zeros_like(bq_h)], 2).reshape(HG * 128)
    bkv = jnp.concatenate([jnp.zeros_like(bv_h), bv_h], 2).reshape(HG * 128)
    x_half = lax.dynamic_index_in_dim(x_all, me_u, 0, keepdims=False)
    kv = (jnp.einsum("urscd,de->ursce", x_all, wkv, preferred_element_type=F32) + bkv).astype(BF)
    q_all = ((jnp.einsum("rscd,de->rsce", x_half, wq_pad, preferred_element_type=F32) + bq_pad) * (HD**-0.5)).astype(BF)
    q_loc = lax.dynamic_slice_in_dim(q_all, me_r * TP, TP, 0)

    pair = lax.dynamic_slice_in_dim(lax.dynamic_index_in_dim(pairing, me_u, 1, keepdims=False), me_t * HG, HG, 0)
    ids = block_ids.reshape(seqs, 2, half)
    ids_own = lax.dynamic_index_in_dim(ids, me_u, 1, keepdims=False)
    ends = jnp.sum((ids[:, :, None, :] <= ids_own[:, None, :, None]).astype(jnp.int32), axis=-1)
    end_all = jnp.where((pair == 0)[None, :, None], ends[:, 0:1], ends[:, 1:2])
    end_loc = lax.dynamic_slice_in_dim(end_all, me_r * TP * rows, TP * rows, 2)
    begin = jnp.maximum(offsets[:, None] - pair[None, :] * half, 0).reshape(-1)
    last = end_loc[:, :, -1].reshape(-1)
    start = me_r * TP * rows
    first = jnp.sum((end_all <= start).astype(jnp.int32), axis=-1).reshape(-1)
    end_col = end_loc[..., None]

    att, lse = attend_forward(q_loc, kv, pair, begin, last, end_col)
    att_t = lax.all_to_all(att, "t", split_axis=0, concat_axis=0, tiled=True)
    att_tok = att_t.transpose(1, 2, 0, 3).reshape(tokens, width)

    x_own = layer_input.reshape(tokens, width)
    proj = dot_nn(att_tok, wo_all) + bias_f[2]
    mid, normed_one, inv_one = layer_norm(x_own.astype(F32) + proj, gain_f[0], shift_f[0])
    mid_low = mid.astype(BF)
    inner = jnp.concatenate([dot_nn(mid_low, w) for w in wi_all], axis=1) + bin_f
    active, gelu_pull = jax.vjp(gelu_exact, inner)
    active_low = active.astype(BF)
    feed = dot_nn(active_low, wd_all) + bias_f[3]
    second, normed_two, inv_two = layer_norm(mid + feed, gain_f[1], shift_f[1])
    hidden_out = second.astype(BF).reshape(seqs, rows, width)
    grad_out = cotangent.reshape(tokens, width).astype(F32)
    dgain_two = jnp.sum(grad_out * normed_two, axis=0)
    dshift_two = jnp.sum(grad_out, axis=0)
    dsecond = norm_back(grad_out, normed_two, inv_two, gain_f[1])
    dfeed = dsecond.astype(BF)
    dbias_out = jnp.sum(dfeed.astype(F32), axis=0)
    dactive = dot_nt(dfeed, wd_all)
    dinner = gelu_pull(dactive)[0].astype(BF)
    dbias_in = jnp.sum(dinner.astype(F32), axis=0)
    dmid = dsecond
    for k, w in enumerate(wi_all):
        dmid = dmid + dot_nt(dinner[:, k * width : (k + 1) * width], w)
    dgain_one = jnp.sum(dmid * normed_one, axis=0)
    dshift_one = jnp.sum(dmid, axis=0)
    dsum = norm_back(dmid, normed_one, inv_one, gain_f[0])
    dproj = dsum.astype(BF)
    dbias_o = jnp.sum(dproj.astype(F32), axis=0)
    datt = dot_nt(dproj, wo_all).astype(BF)

    def dot_tn(a, b):
        return lax.dot_general(a, b, (((0,), (0,)), ((), ())), preferred_element_type=F32).astype(BF)

    dwi = [dot_tn(mid_low, dinner[:, k * width : (k + 1) * width]).reshape(devices, part, width) for k in range(cols_in)]
    dwd = dot_tn(active_low, dfeed).reshape(devices, fpart, width)
    dwo = dot_tn(att_tok, dproj).reshape(devices, part, width)

    def shard_cols(v):
        return v.reshape(-1, devices, v.shape[-1] // devices).transpose(1, 0, 2).reshape(devices, -1)

    dsmall = jnp.concatenate(
        [
            shard_cols(jnp.stack([dbias_o, dbias_out])),
            shard_cols(dbias_in),
            shard_cols(jnp.stack([dgain_one, dgain_two])),
            shard_cols(jnp.stack([dshift_one, dshift_two])),
        ],
        axis=1,
    ).astype(BF)
    dsmall = jnp.zeros((devices, 16, width), BF).at[:, 0, : dsmall.shape[1]].set(dsmall)
    packed_grads = jnp.concatenate(dwi + [dwd, dwo, dsmall], axis=1)
    summed = lax.psum_scatter(packed_grads, ALL, scatter_dimension=0, tiled=False).astype(F32)
    at = cols_in * part
    grad_w_in = jnp.concatenate([summed[k * part : (k + 1) * part] for k in range(cols_in)], axis=1)
    grad_w_down = summed[at : at + fpart]
    grad_w_out = summed[at + fpart : at + fpart + part]
    flat = summed[at + fpart + part]
    grad_bo = flat[: 2 * part].reshape(2, part)
    grad_bin = flat[2 * part : 2 * part + fpart]
    at = 2 * part + fpart
    grad_gains = flat[at : at + 2 * part].reshape(2, part)
    grad_shifts = flat[at + 2 * part : at + 4 * part].reshape(2, part)

    datt_t = datt.reshape(seqs, rows, TP, HG * HD).transpose(2, 0, 1, 3)
    dout = lax.all_to_all(datt_t, "t", split_axis=0, concat_axis=0, tiled=True)
    spread = (TP, seqs, rows, HG, HD)
    delta = jnp.sum((dout.astype(F32) * att.astype(F32)).reshape(spread), axis=-1)
    delta = delta.transpose(1, 3, 0, 2).reshape(seqs, HG, TP * rows)
    dout_pad = jnp.pad(dout.reshape(spread), ((0, 0),) * 4 + ((HD, 0),)).reshape(TP, seqs, rows, HG * 128)
    dout_r = ring_gather(dout, "r")
    stat_r = ring_gather(jnp.stack([lse[..., 0], delta], axis=2), "r")
    dq = attend_query(q_loc, kv, pair, begin, last, end_col, lse, delta[..., None], dout_pad)
    do_all = jnp.pad(dout_r.reshape((shards,) + spread[1:]), ((0, 0),) * 4 + ((HD, 0),)).reshape(shards, seqs, rows, HG * 128)
    stats = stat_r.transpose(1, 2, 3, 0, 4).reshape(seqs, HG, 2, half)
    stats = jnp.concatenate([stats, end_all[:, :, None].astype(F32), jnp.zeros((seqs, HG, 5, half), F32)], axis=2)
    place = jnp.stack([start, me_r]).astype(jnp.int32)
    dkv = attend_key(q_all, do_all, kv, pair, begin, first, place, stats)

    is_own = jnp.repeat(pair == me_u, 128)[None]
    dq2 = dq.reshape(TP * tokens, HG * HD)
    dkv2 = dkv.reshape(TP * tokens, HG * 128)
    dkv_own = jnp.where(is_own, dkv2, 0).astype(BF)
    dkv_oth = jnp.where(is_own, 0, dkv2).astype(BF)
    wq_own = wq_h.reshape(width, HG * HD)
    from_own = (dot_nt(dq2, wq_own) + dot_nt(dkv_own, wkv)).astype(BF).reshape(TP, tokens, width)
    from_oth = dot_nt(dkv_oth, wkv).astype(BF).reshape(TP, tokens, width)
    swap = [(0, 1), (1, 0)]
    got_oth = lax.all_to_all(from_oth, "t", split_axis=0, concat_axis=0, tiled=True)
    got_own = lax.all_to_all(from_own, "t", split_axis=0, concat_axis=0, tiled=True)
    oth = lax.ppermute(jnp.sum(got_oth.astype(F32), axis=0).astype(BF), "u", swap)
    grad_input = dsum + jnp.sum(got_own.astype(F32), axis=0) + oth.astype(F32)
    grad_input = grad_input.astype(BF).reshape(seqs, rows, width)

    x_rows = lax.dynamic_slice_in_dim(x_all, me_r * TP, TP, 1).reshape(2, TP * tokens, width)
    x_mine = lax.dynamic_index_in_dim(x_rows, me_u, 0, keepdims=False)
    x_yours = lax.dynamic_index_in_dim(x_rows, 1 - me_u, 0, keepdims=False)

    def dot_tn32(a, b):
        return lax.dot_general(a, b, (((0,), (0,)), ((), ())), preferred_element_type=F32)

    dwq = dot_tn32(x_mine, dq2)
    dwkv = dot_tn32(x_mine, dkv_own) + dot_tn32(x_yours, dkv_oth)
    dbq = jnp.sum(dq2.astype(F32), axis=0)
    dbkv = jnp.sum(dkv2.astype(F32), axis=0)
    send = jnp.concatenate([dwq, dwkv], axis=1).astype(BF).reshape(devices, part, 576)
    extra = jnp.concatenate([dbq, dbkv]).astype(BF)
    send = jnp.concatenate([send, jnp.broadcast_to(extra, (devices, 8, 576))], axis=1)
    got = lax.all_to_all(send, ALL, split_axis=0, concat_axis=0, tiled=True)
    got = jnp.sum(got.astype(F32).reshape(2 * ring, TP, part + 8, 576), axis=0)
    got_q = got[:, :, :192].transpose(1, 0, 2).reshape(part + 8, width)
    got_kv = got[:, :, 192:].reshape(TP, part + 8, HG, 2, HD).transpose(3, 1, 0, 2, 4).reshape(2, part + 8, width)
    grad_w_qkv = jnp.concatenate([got_q[:part], got_kv[0, :part], got_kv[1, :part]], axis=1)
    mine = lax.axis_index(ALL) * part
    grad_bq = lax.dynamic_slice_in_dim(got_q[part], mine, part, 0)
    grad_bv = lax.dynamic_slice_in_dim(got_kv[1, part], mine, part, 0)
    grad_biases = jnp.concatenate([jnp.stack([grad_bq, grad_bv]), grad_bo])
    return (hidden_out, grad_input, grad_w_qkv, grad_w_out, grad_w_in, grad_w_down, grad_biases, grad_bin, grad_gains, grad_shifts)


def solution(mesh):
    wide = mesh.shape["blk"]
    grid = Mesh(mesh.devices.reshape(2, wide // TP, TP), ALL)
    rows2, cols1 = P(ALL, None), P(None, ALL)
    toks = P(None, ALL, None)
    return jax.shard_map(
        per_device,
        mesh=grid,
        in_specs=(toks, rows2, rows2, rows2, rows2, cols1, P(ALL), cols1, cols1, toks, P(), P(), P()),
        out_specs=(toks, toks, rows2, rows2, rows2, rows2, cols1, P(ALL), cols1, cols1),
        check_vma=False,
    )
```

time: 1260 us -> 611 us (0.48)
  the two profiles are of different devices: /device:TPU:8 before, /device:TPU:0 now
where the time goes in v1:
time: 611 us; the launch traced here: 600 us
  waiting for transfers between devices  250 us (41%)
  local copies, waits for them, and re-layouts  136 us (22%)
  matrix products  56 us (9%)
  starting transfers between devices  49.3 us (8%)
  other arithmetic  43 us (7%)
  Pallas kernels  38.5 us (6%)
  between operations  15.6 us (3%)
  blocking collectives  11.9 us (2%)
    all_gather x1, waiting for transfers between devices, per_device(): everything = lax.all_gather(packed, ALL, axis=0, tiled=False)  162 us
    ppermute x6, waiting for transfers between devices, ring_gather(): lax.ppermute(piece, axis, [(i, (i + 1) % size) for i in range(size)])  47.3 us
    all_to_all x1, starting transfers between devices, per_device(): got = lax.all_to_all(send, ALL, split_axis=0, concat_axis=0, tiled=True)  27.5 us
    unnamed x91, local copies, waits for them, and re-layouts  23.9 us
    slice x3, local copies, waits for them, and re-layouts, piece(): return everything[:, marks[i]:marks[i + 1]]  22 us
    ppermute x1, waiting for transfers between devices, per_device(): lax.ppermute(jnp.sum(got_oth.astype(F32), axis=0).astype(BF), 'u', swap)  19.7 us
    pallas_call x1, Pallas kernels, attend_key(): pl.pallas_call(functools.partial(key_kernel, rows, shards), grid_spec=plt...  18 us
    dot_general x9, matrix products, dot_nt(): lax.dot_general(a, b, (((1,), (1,)), ((), ())), preferred_element_type=F32)  14.3 us
  transfers between devices with their start and end apart: 13, of which 10 were waited for; matrix products, arithmetic and copies ran while one was open for 17% of the time, Pallas kernels for 5%

profile of v1, /device:TPU:0, one launch (start us, length us, event | category | flops | bytes accessed | tf_op | source)
XLA Modules:
  0.0 600.1 jit_solution(1797667592798914897)
XLA Ops:
  23.6 7.3 %convert_reduce_fusion = s32[3,2,1536]{2,1,0:T(2,128)S(1)} fusion(s32[3,1536]{1,0:T(4,128)S(1)} %bitcast.256, s32[3,2,1536]{2,1,0:T(2,128)S(1)} %le.23), kind=kLoop, calls=%fused_computation | loop fusion | flops 42458112 | bytes 92160 | tf_op jit(solution)/shard_map/reduce_sum | solution.py:290
  33.8 161.9 %all-gather.3.cloned.1.call-done = bf16[18944,768]{1,0:T(8,128)(2,1)} async-done(((bf16[592,768]{1,0:T(8,128)(2,1)}), bf16[18944,768]{1,0:T(8,128)(2,1)}) %all-gather.3.cloned.1.call-update) | async-done | bytes 29098000 | tf_op jit(solution)/shard_map/all_gather | solution.py:253
  197.0 6.5 %fusion.49 = (bf16[32,24,768]{2,1,0:T(8,128)(2,1)}, bf16[32,24,768]{2,1,0:T(8,128)(2,1)}, bf16[32,24,768]{2,1,0:T(8,128)(2,1)}, bf16[32,24,768]{2,1,0:T(8,128)(2...) fusion(bf16[32,592,768]{2,1,0:T(8,128)(2,1)} %bitcast.188), kind=kLoop, calls=%fused_computation.186 | loop fusion | bytes 18874368 | tf_op jit(solution)/shard_map/slice | solution.py:259
  203.6 10.6 %slice.314 = bf16[32,288,768]{2,1,0:T(8,128)(2,1)} slice(bf16[32,592,768]{2,1,0:T(8,128)(2,1)} %bitcast.189), slice={[0:32], [0:288], [0:768]} | slice | bytes 28311552 | tf_op jit(solution)/shard_map/slice | solution.py:259
  215.0 4.7 reshape_reshape.11
  219.7 4.7 reshape_reshape.10
  224.4 3.9 constant_dynamic-slice_fusion.4
  232.4 3.2 reshape_reshape.9
  235.7 2.4 constant_dynamic-slice_fusion.8
  238.7 7.1 %multiply_convert_fusion.q_ref = bf16[16,3,96,384]{3,2,1,0:T(8,128)(2,1)S(1)} fusion(f32[384]{0:T(512)S(1)} %pad_bitcast_fusion.1, bf16[768,384,1,1]{0,1,3,2:T(8,128)(2,1)S(1)} %bitcast.243, bf16[2,16,3,96,768]{4,3,2,1,0:T(8,128)(2,1)} %bitcast.191, s32[]{:T(128)S(6)} %select_n.106), kind=kOutput, calls=%fused_computation.4 | convolution fusion | flops 2723217408 | bytes 11208196 | tf_op jit(solution)/shard_map/rscd,de->rsce/dot_general | solution.py:284
  248.5 9.8 %add_convert_fusion.kv0.kv1.kv2 = bf16[2,16,3,96,384]{4,3,2,1,0:T(8,128)(2,1)} fusion(f32[384]{0:T(512)S(1)} %pad_bitcast_fusion, bf16[2,16,3,96,768]{4,3,2,1,0:T(8,128)(2,1)S(1)} %bitcast.195, bf16[768,384,1,1,1]{0,1,4,3,2:T(8,128)(2,1)S(1)} %bitcast.225), kind=kOutput, calls=%fused_computation.1 | convolution fusion | flops 5442895872 | bytes 21825024 | tf_op jit(solution)/shard_map/urscd,de->ursce/dot_general | solution.py:283
  258.3 11.2 %attend_forward.1 = (bf16[4,3,96,192]{3,2,1,0:T(8,128)(2,1)}, f32[3,3,384,1]{3,2,1,0:T(8,128)}) custom-call(s32[3]{0:T(128)} %copy-done.27, s32[9]{0:T(128)} %max.8.begin_ref, s32[9]{0:T(128)} %reshape_squeeze.3.last_ref, bf16[4,3,96,384]{3,2,1,0:T(8,128)(2,1)} %constant_dynamic-slice_fusion.6.q_ref, ...), custom_call_target="tpu_custom_call" | custom-call | tf_op jit(solution)/shard_map/attend_forward/pallas_call | solution.py:157
  269.5 3.5 all-to-all-start
  273.1 4.9 slice.333
  279.8 2.7 all-to-all-done
  290.0 8.1 %multiply_convert_fusion.1 = (bf16[288,3072]{1,0:T(8,128)(2,1)S(1)}, f32[288,3072]{1,0:T(8,128)S(1)}) fusion(f32[3072]{0:T(1024)S(1)} %add.229, f32[288,768]{1,0:T(8,128)S(1)} %fusion.61, f32[288,768]{1,0:T(8,128)S(1)} %fusion.60, f32[288,768]{1,0:T(8,128)S(1)} %fusion.59, f32[288,768]{1,0:T(8,128)S(1)} %fusion.58), kind=kLoop, calls=%fused_computation.13 | loop fusion | flops 61046784 | bytes 8859648 | tf_op jit(solution)/shard_map/convert_element_type | solution.py:309
  301.7 3.4 fusion.57
  313.1 4.4 convolution_convert_fusion
  324.0 2.5 constant_dynamic-update-slice_fusion.16
  330.0 4.9 constant_dynamic-update-slice_fusion.12
  340.2 11.9 %all_to_all.25 = bf16[4,3,96,192]{3,2,1,0:T(8,128)(2,1)S(1)} all-to-all(bf16[4,3,96,192]{3,2,1,0:T(8,128)(2,1)S(1)} %bitcast.229), channel_id=1, replica_groups=mesh['u'=2,'r'=4,'t'=4] {'t'}, dimensions={0} | all-to-all | bytes 884736 | tf_op jit(solution)/shard_map/all_to_all | solution.py:366
  352.1 5.5 collective-permute-start
  362.7 2.5 collective-permute-start.3
  365.1 10.9 %collective-permute-done = bf16[4,3,96,192]{3,2,1,0:T(8,128)(2,1)} collective-permute-done((bf16[4,3,96,192]{3,2,1,0:T(8,128)(2,1)S(1)}, bf16[4,3,96,192]{3,2,1,0:T(8,128)(2,1)}, u32[]{:S(2)}, u32[]{:S(2)}) %collective-permute-start) | collective-permute-done | bytes 442400 | tf_op jit(solution)/shard_map/ppermute | solution.py:228
  379.2 13.6 %collective-permute-done.4 = f32[3,3,2,384]{3,2,1,0:T(2,128)} collective-permute-done((f32[3,3,2,384]{3,2,1,0:T(2,128)S(1)}, f32[3,3,2,384]{3,2,1,0:T(2,128)}, u32[]{:S(2)}, u32[]{:S(2)}) %collective-permute-start.4) | collective-permute-done | bytes 27680 | tf_op jit(solution)/shard_map/ppermute | solution.py:228
  395.9 2.9 collective-permute-done.5
  407.4 19.9 %collective-permute-done.2 = bf16[4,3,96,192]{3,2,1,0:T(8,128)(2,1)} collective-permute-done((bf16[4,3,96,192]{3,2,1,0:T(8,128)(2,1)}, bf16[4,3,96,192]{3,2,1,0:T(8,128)(2,1)}, u32[]{:S(2)}, u32[]{:S(2)}) %collective-permute-start.2) | collective-permute-done | bytes 442400 | tf_op jit(solution)/shard_map/ppermute | solution.py:228
  430.7 3.6 pad.22
  434.3 6.7 %copy.206.do_ref = bf16[16,3,96,384]{3,2,1,0:T(8,128)(2,1)} copy(bf16[16,3,96,384]{2,3,1,0:T(8,128)(2,1)} %bitcast.196) | data formatting | bytes 7077888 | tf_op jit(solution)/shard_map/reshape | solution.py:374
  440.9 18.0 %attend_key.1 = bf16[4,3,96,384]{3,2,1,0:T(8,128)(2,1)} custom-call(s32[3]{0:T(128)} %copy-done.27, s32[9]{0:T(128)} %max.8.begin_ref, s32[9]{0:T(128)} %reshape.485.first_ref, s32[2]{0:T(128)} %pad_add_fusion.place_ref, bf16[16,3,96,384]{3,2,1,0:T(8,128)(2,1)} %copy-done.9, bf16[16,3,96,384]{3,2,1,0:T(8,128)(2,1)} %copy.206.do_ref, ...), custom_call_target="tpu_custom_call" | custom-call | tf_op jit(solution)/shard_map/attend_key/pallas_call | solution.py:205
  458.9 2.4 broadcast_select_fusion.1
  461.3 2.3 convolution_convert_fusion.1
  463.6 3.6 all-to-all-start.3
  467.2 4.2 constant_dynamic-slice_fusion.2
  471.4 2.9 broadcast_in_dim_reshape.3.delta_ref
  475.3 2.4 pad.21
  477.8 2.3 copy.205.dout_ref
  480.1 9.4 %attend_query.1 = bf16[4,3,96,192]{3,2,1,0:T(8,128)(2,1)} custom-call(s32[3]{0:T(128)} %copy-done.27, s32[9]{0:T(128)} %max.8.begin_ref, s32[9]{0:T(128)} %reshape_squeeze.3.last_ref, bf16[4,3,96,384]{3,2,1,0:T(8,128)(2,1)} %constant_dynamic-slice_fusion.6.q_ref, bf16[2,16,3,96,384]{4,3,2,1,0:T(8,128)(2,1)} %add_convert_fusion.kv0.kv1.kv2, ...), custom_call_target="tpu_custom_call" | custom-call | tf_op jit(solution)/shard_map/attend_query/pallas_call | solution.py:180
  491.2 2.3 fusion.9
  495.7 4.6 all-to-all-start.2
  500.3 2.8 constant_dynamic-slice_fusion.1
  503.2 3.9 copy.188
  507.3 2.3 convolution_convert_fusion.8
  509.7 2.9 fusion.12
  515.4 7.8 %all-to-all-done.2 = bf16[4,288,768]{2,1,0:T(8,128)(2,1)} async-done(((bf16[4,288,768]{2,1,0:T(8,128)(2,1)}), bf16[4,288,768]{2,1,0:T(8,128)(2,1)}, u32[]{:S(2)}, u32[]{:S(2)}) %all-to-all-start.2) | async-done | bytes 1769504 | tf_op jit(solution)/shard_map/all_to_all | solution.py:390
  523.1 27.5 %all-to-all-start.4 = ((bf16[32,32,576]{2,1,0:T(8,128)(2,1)}), bf16[32,32,576]{2,1,0:T(8,128)(2,1)}, u32[]{:S(2)}, u32[]{:S(2)}) async-start(bf16[32,32,576]{2,1,0:T(8,128)(2,1)} %pad_maximum_fusion), calls=%async_computation.4 | async-start | bytes 2621440 | tf_op jit(solution)/shard_map/all_to_all | solution.py:409
  554.7 19.7 %collective-permute-done.6 = bf16[288,768]{1,0:T(8,128)(2,1)S(1)} collective-permute-done((bf16[288,768]{1,0:T(8,128)(2,1)S(1)}, bf16[288,768]{1,0:T(8,128)(2,1)S(1)}, u32[]{:S(2)}, u32[]{:S(2)}) %collective-permute-start.6) | collective-permute-done | bytes 442400 | tf_op jit(solution)/shard_map/ppermute | solution.py:391
  575.3 8.1 %all-to-all-done.4 = bf16[32,32,576]{2,1,0:T(8,128)(2,1)} async-done(((bf16[32,32,576]{2,1,0:T(8,128)(2,1)}), bf16[32,32,576]{2,1,0:T(8,128)(2,1)}, u32[]{:S(2)}, u32[]{:S(2)}) %all-to-all-start.4) | async-done | bytes 1179680 | tf_op jit(solution)/shard_map/all_to_all | solution.py:409
  (278 shorter events, 110.2 us)
Async XLA Ops:
  7.2 188.5 %all-gather.3.cloned.1.call-start = ((), (), s32[]{:S(2)}) async-start(), calls=%async_computation.7 | async-start | bytes 30007296 | tf_op jit(solution)/shard_map/all_gather | solution.py:253
  18.4 1.0 copy-start.18
  20.1 183.4 %copy-start.27 = (s32[3]{0:T(128)}, s32[3]{0:T(128)S(1)}, u32[]{:S(2)}) copy-start(s32[3]{0:T(128)S(1)} %get-tuple-element.56.pair_ref) | copy-start | bytes 40
  203.6 10.7 %copy-start = (bf16[3,96,768]{2,1,0:T(8,128)(2,1)S(1)}, bf16[3,96,768]{2,1,0:T(8,128)(2,1)}, u32[]{:S(2)}) copy-start(bf16[3,96,768]{2,1,0:T(8,128)(2,1)} %param.26) | copy-start | bytes 1327108
  238.6 7.2 %copy-start.13 = (bf16[768,3,64]{0,2,1:T(8,128)(2,1)}, bf16[768,3,64]{0,2,1:T(8,128)(2,1)S(1)}, u32[]{:S(2)}) copy-start(bf16[768,3,64]{0,2,1:T(8,128)(2,1)S(1)} %copy.212) | copy-start | bytes 884740
  238.6 9.9 %slice-start = ((s8[14155776]{0:T(1024)(128)(4,1)}), s8[4194304]{0:T(1024)(128)(4,1)S(1)}, s32[]{:S(2)}) async-start(s8[14155776]{0:T(1024)(128)(4,1)} %bitcast.193), calls=%async_computation.8 | async-start | bytes 8388608
  238.7 9.9 %slice-start.1 = ((s8[14155776]{0:T(1024)(128)(4,1)}), s8[4194304]{0:T(1024)(128)(4,1)S(1)}, s32[]{:S(2)}) async-start(s8[14155776]{0:T(1024)(128)(4,1)} %bitcast.193), calls=%async_computation.9 | async-start | bytes 8388608
  238.7 9.9 %slice-start.2 = ((s8[14155776]{0:T(1024)(128)(4,1)}), s8[4194304]{0:T(1024)(128)(4,1)S(1)}, s32[]{:S(2)}) async-start(s8[14155776]{0:T(1024)(128)(4,1)} %bitcast.193), calls=%async_computation.10 | async-start | bytes 8388608
  238.7 9.9 %slice-start.3 = ((s8[14155776]{0:T(1024)(128)(4,1)}), s8[1572864]{0:T(1024)(128)(4,1)S(1)}, s32[]{:S(2)}) async-start(s8[14155776]{0:T(1024)(128)(4,1)} %bitcast.193), calls=%async_computation.11 | async-start | bytes 3145728
  238.7 9.8 %copy-start.15 = (bf16[768,3,128]{0,2,1:T(8,128)(2,1)S(1)}, bf16[768,3,128]{0,2,1:T(8,128)(2,1)}, u32[]{:S(2)}) copy-start(bf16[768,3,128]{0,2,1:T(8,128)(2,1)} %copy.160) | copy-start | bytes 1769476
  245.8 1.7 copy-start.9
  269.5 13.0 %all-to-all-start = ((bf16[4,3,96,192]{3,2,1,0:T(8,128)(2,1)}), bf16[4,3,96,192]{3,2,1,0:T(8,128)(2,1)S(1)}, u32[]{:S(2)}, u32[]{:S(2)}) async-start(bf16[4,3,96,192]{3,2,1,0:T(8,128)(2,1)} %get-tuple-element.36), calls=%async_computation | async-start | bytes 1179648 | tf_op jit(solution)/shard_map/all_to_all | solution.py:300
  273.0 314.0 %reduce-scatter.2.cloned.1.call-start = ((), (), s32[]{:S(2)}) async-start(), calls=%async_computation.6 | async-start | bytes 11759616 | tf_op jit(solution)/shard_map/reduce_scatter | solution.py:353
  277.9 7.4 %copy-start.21 = (bf16[3,96,768]{2,1,0:T(8,128)(2,1)S(1)}, bf16[3,96,768]{2,1,0:T(8,128)(2,1)}, u32[]{:S(2)}) copy-start(bf16[3,96,768]{2,1,0:T(8,128)(2,1)} %param.17) | copy-start | bytes 1327108
  285.4 3.0 copy-start.1
  286.0 2.9 copy-start.2
  286.5 3.0 copy-start.3
  289.5 8.7 %slice-start.4 = ((s8[4718592]{0:T(1024)(128)(4,1)}), s8[4194304]{0:T(1024)(128)(4,1)S(1)}, s32[]{:S(2)}) async-start(s8[4718592]{0:T(1024)(128)(4,1)} %bitcast.216), calls=%async_computation.12 | async-start | bytes 8388608
  290.0 8.2 %slice-start.5 = ((s8[4718592]{0:T(1024)(128)(4,1)}), s8[524288]{0:T(1024)(128)(4,1)S(1)}, s32[]{:S(2)}) async-start(s8[4718592]{0:T(1024)(128)(4,1)} %bitcast.216), calls=%async_computation.13 | async-start | bytes 1048576
  298.2 1.7 copy-start.19
  298.2 2.0 copy-start.12
  307.5 5.5 copy-start.20
  317.5 1.3 copy-start.4
  323.1 3.5 copy-start.24
  323.2 4.5 copy-start.23
  324.0 4.8 copy-start.22
  338.4 19.3 %copy-start.8 = (f32[3,3,384,1]{3,2,1,0:T(8,128)S(1)}, f32[3,3,384,1]{3,2,1,0:T(8,128)}, u32[]{:S(2)}) copy-start(f32[3,3,384,1]{3,2,1,0:T(8,128)} %get-tuple-element.37.lse_ref) | copy-start | bytes 41476
  352.1 26.0 %copy-start.5 = (bf16[4,3,96,192]{3,2,1,0:T(8,128)(2,1)}, bf16[4,3,96,192]{3,2,1,0:T(8,128)(2,1)S(1)}, u32[]{:S(2)}) copy-start(bf16[4,3,96,192]{3,2,1,0:T(8,128)(2,1)S(1)} %all_to_all.25) | copy-start | bytes 1327108
  352.1 23.9 %collective-permute-start = (bf16[4,3,96,192]{3,2,1,0:T(8,128)(2,1)S(1)}, bf16[4,3,96,192]{3,2,1,0:T(8,128)(2,1)}, u32[]{:S(2)}, u32[]{:S(2)}) collective-permute-start(bf16[4,3,96,192]{3,2,1,0:T(8,128)(2,1)S(1)} %all_to_all.25), channel_id=1, source_target_pairs={{0,4},{4,8},{8,12},{12,0},{1,5},{5,9},{9,13},{13,1},{2,6},{6,10},{... | collective-permute-start | bytes 1327112 | tf_op jit(solution)/shard_map/ppermute | solution.py:228
  362.7 13.9 %collective-permute-start.3 = (f32[3,3,2,384]{3,2,1,0:T(2,128)S(1)}, f32[3,3,2,384]{3,2,1,0:T(2,128)S(1)}, u32[]{:S(2)}, u32[]{:S(2)}) collective-permute-start(f32[3,3,2,384]{3,2,1,0:T(2,128)S(1)} %get-tuple-element.88), channel_id=1, source_target_pairs={{0,4},{4,8},{8,12},{12,0},{1,5},{5,9},{9,13},{13,1},{2,6},{6,10},{... | collective-permute-start | bytes 82952 | tf_op jit(solution)/shard_map/ppermute | solution.py:228
  376.0 23.9 %collective-permute-start.1 = (bf16[4,3,96,192]{3,2,1,0:T(8,128)(2,1)}, bf16[4,3,96,192]{3,2,1,0:T(8,128)(2,1)}, u32[]{:S(2)}, u32[]{:S(2)}) collective-permute-start(bf16[4,3,96,192]{3,2,1,0:T(8,128)(2,1)} %collective-permute-done), channel_id=1, source_target_pairs={{0,4},{4,8},{8,12},{12,0},{1,5},{5,9},{9,13},{13,1},{2,6},{6,10},{... | collective-permute-start | bytes 1327112 | tf_op jit(solution)/shard_map/ppermute | solution.py:228
  376.6 16.3 %collective-permute-start.4 = (f32[3,3,2,384]{3,2,1,0:T(2,128)S(1)}, f32[3,3,2,384]{3,2,1,0:T(2,128)}, u32[]{:S(2)}, u32[]{:S(2)}) collective-permute-start(f32[3,3,2,384]{3,2,1,0:T(2,128)S(1)} %collective-permute-done.3), channel_id=1, source_target_pairs={{0,4},{4,8},{8,12},{12,0},{1,5},{5,9},{9,13},{13,1},{2,6},{6,10},{... | collective-permute-start | bytes 82952 | tf_op jit(solution)/shard_map/ppermute | solution.py:228
  392.9 6.0 collective-permute-start.5
  399.9 27.5 %collective-permute-start.2 = (bf16[4,3,96,192]{3,2,1,0:T(8,128)(2,1)}, bf16[4,3,96,192]{3,2,1,0:T(8,128)(2,1)}, u32[]{:S(2)}, u32[]{:S(2)}) collective-permute-start(bf16[4,3,96,192]{3,2,1,0:T(8,128)(2,1)} %collective-permute-done.1), channel_id=1, source_target_pairs={{0,4},{4,8},{8,12},{12,0},{1,5},{5,9},{9,13},{13,1},{2,6},{6,10},{... | collective-permute-start | bytes 1327112 | tf_op jit(solution)/shard_map/ppermute | solution.py:228
  440.9 18.0 %copy-start.28 = (pred[384]{0:T(512)(128)(4,1)S(1)}, pred[384]{0:T(512)(128)(4,1)}, u32[]{:S(2)}) copy-start(pred[384]{0:T(512)(128)(4,1)} %broadcast_bitcast_fusion) | copy-start | bytes 1156
  440.9 20.4 %copy-start.16 = (bf16[768,3,128]{0,2,1:T(8,128)(2,1)S(1)}, bf16[768,3,128]{0,2,1:T(8,128)(2,1)}, u32[]{:S(2)}) copy-start(bf16[768,3,128]{0,2,1:T(8,128)(2,1)} %copy.160) | copy-start | bytes 1769476
  461.3 2.3 copy-start.25
  463.6 32.1 %all-to-all-start.3 = ((bf16[4,288,768]{2,1,0:T(8,128)(2,1)}), bf16[4,288,768]{2,1,0:T(8,128)(2,1)S(1)}, u32[]{:S(2)}, u32[]{:S(2)}) async-start(bf16[4,288,768]{2,1,0:T(8,128)(2,1)} %bitcast.231), calls=%async_computation.3 | async-start | bytes 3538944 | tf_op jit(solution)/shard_map/all_to_all | solution.py:389
  467.2 7.1 %copy-start.6 = (bf16[4,3,96,192]{3,2,1,0:T(8,128)(2,1)S(1)}, bf16[4,3,96,192]{3,2,1,0:T(8,128)(2,1)}, u32[]{:S(2)}) copy-start(bf16[4,3,96,192]{3,2,1,0:T(8,128)(2,1)} %copy-done.5) | copy-start | bytes 1327108
  480.1 9.4 %copy-start.14 = (bf16[768,3,64]{0,2,1:T(8,128)(2,1)S(1)}, bf16[768,3,64]{0,2,1:T(8,128)(2,1)}, u32[]{:S(2)}) copy-start(bf16[768,3,64]{0,2,1:T(8,128)(2,1)} %copy-done.13) | copy-start | bytes 884740
  489.4 1.8 copy-start.11
  489.4 1.8 copy-start.17
  495.7 27.4 %all-to-all-start.2 = ((bf16[4,288,768]{2,1,0:T(8,128)(2,1)}), bf16[4,288,768]{2,1,0:T(8,128)(2,1)}, u32[]{:S(2)}, u32[]{:S(2)}) async-start(bf16[4,288,768]{2,1,0:T(8,128)(2,1)} %bitcast.211), calls=%async_computation.2 | async-start | bytes 3538944 | tf_op jit(solution)/shard_map/all_to_all | solution.py:390
  500.3 6.7 %copy-start.10 = (bf16[4,3,96,192]{3,2,1,0:T(8,128)(2,1)S(1)}, bf16[4,3,96,192]{3,2,1,0:T(8,128)(2,1)}, u32[]{:S(2)}) copy-start(bf16[4,3,96,192]{3,2,1,0:T(8,128)(2,1)} %attend_query.1) | copy-start | bytes 1327108
  507.2 5.4 copy-start.7
  507.2 5.4 copy-start.26
  523.1 60.3 %all-to-all-start.4 = ((bf16[32,32,576]{2,1,0:T(8,128)(2,1)}), bf16[32,32,576]{2,1,0:T(8,128)(2,1)}, u32[]{:S(2)}, u32[]{:S(2)}) async-start(bf16[32,32,576]{2,1,0:T(8,128)(2,1)} %pad_maximum_fusion), calls=%async_computation.4 | async-start | bytes 2621440 | tf_op jit(solution)/shard_map/all_to_all | solution.py:409
  551.1 23.3 %collective-permute-start.6 = (bf16[288,768]{1,0:T(8,128)(2,1)S(1)}, bf16[288,768]{1,0:T(8,128)(2,1)S(1)}, u32[]{:S(2)}, u32[]{:S(2)}) collective-permute-start(bf16[288,768]{1,0:T(8,128)(2,1)S(1)} %reduce_sum.222), channel_id=1, source_target_pairs={{0,16},{16,0},{1,17},{17,1},{2,18},{18,2},{3,19},{19,3},{4,20},{20... | collective-permute-start | bytes 1327112 | tf_op jit(solution)/shard_map/ppermute | solution.py:391
Sparse Core Ops, SparseCore 0:
  19.5 176.1 all-gather.2
  337.2 177.3 reduce-scatter.1

commit v2 on v1

v2 whole, which is shorter than its diff:
```python
import functools

import jax
import jax.numpy as jnp
from jax import lax
from jax.experimental import pallas as pl
from jax.experimental.pallas import tpu as pltpu
from jax.sharding import Mesh
from jax.sharding import PartitionSpec as P

H = 12
HD = 64
TP = 4
HG = H // TP
NORM_EPS = 1e-12
FILL = -1e30
FLOOR = -1e29
ALL = ("u", "r", "y", "c")
BF = jnp.bfloat16
F32 = jnp.float32
VMEM_LIMIT = 56 * 1024 * 1024


def split_three(v):
    high = v.astype(BF)
    v = v - high.astype(F32)
    middle = v.astype(BF)
    return high, middle, (v - middle.astype(F32)).astype(BF)


def dot_nt(a, b):
    return lax.dot_general(a, b, (((1,), (1,)), ((), ())), preferred_element_type=F32)


def dot_nn(a, b):
    return lax.dot_general(a, b, (((1,), (0,)), ((), ())), preferred_element_type=F32)


def dot_tn(a, b):
    return lax.dot_general(a, b, (((0,), (0,)), ((), ())), preferred_element_type=F32)


def lanes_like(shape):
    return lax.broadcasted_iota(jnp.int32, shape, len(shape) - 1)


def chooser(h, kind, depth):
    at = HD + kind * 3 * HG + 3 * h
    lane = lanes_like((depth, 128))
    return jnp.where((lane >= at) & (lane < at + 3), -1.0, 0.0).astype(BF)


def chunk_of(shards):
    return 16 if shards % 16 == 0 else shards


def key_spots(first, count, begin, end_row):
    spot = lax.broadcasted_iota(jnp.int32, (count, 1), 0) + first
    return jnp.where(spot >= begin, spot, 1 << 30) < end_row


def forward_kernel(rows, shards, pair_ref, begin_ref, last_ref, q_ref, kv0, kv1, kv2, end_ref, att_ref, m_ref, l_ref, acc_ref):
    seq = pl.program_id(0)
    group = chunk_of(shards)
    nq = TP * rows
    width = group * rows
    for h in range(HG):
        m_ref[h] = jnp.full((1, nq), FLOOR, F32)
        l_ref[h] = jnp.zeros((1, nq), F32)
        acc_ref[h] = jnp.zeros((128, nq), F32)

    def step(c, _):
        for h, kv_ref in enumerate((kv0, kv1, kv2)):
            query = q_ref[:, 0, :, h * 128 : (h + 1) * 128].reshape(nq, 128)
            kv = kv_ref[0, pl.ds(c * group, group), 0].reshape(width, 128)
            seen = key_spots(c * width, width, begin_ref[seq * HG + h], end_ref[0, h])
            scores = jnp.where(seen, dot_nt(kv, query), FILL)
            old = m_ref[h]
            new = jnp.maximum(old, jnp.max(scores, axis=0, keepdims=True))
            weights = jnp.exp(scores - new)
            factor = jnp.exp(old - new)
            m_ref[h] = new
            l_ref[h] = l_ref[h] * factor + jnp.sum(weights, axis=0, keepdims=True)
            acc_ref[h] = acc_ref[h] * factor + dot_tn(kv, weights.astype(BF))
        return 0

    trips = [pl.cdiv(last_ref[seq * HG + h], width) for h in range(HG)]
    lax.fori_loop(0, functools.reduce(jnp.maximum, trips), step, 0)
    turn = lax.broadcasted_iota(jnp.int32, (HD, nq), 0)
    notes = jnp.zeros((HD, nq), F32)
    for h in range(HG):
        total = jnp.maximum(l_ref[h], 1.0)
        for p, value in enumerate(split_three(m_ref[h] + jnp.log(total))):
            notes = jnp.where(turn == 3 * HG + 3 * h + p, value.astype(F32), notes)
        att = (acc_ref[h] / total)[HD:].T.astype(BF)
        att_ref[:, 0, :, h * HD : (h + 1) * HD] = att.reshape(TP, rows, HD)
    att_ref[:, 0, :, HG * HD :] = notes.T.astype(BF).reshape(TP, rows, HD)


def output_gradient(load_ref, h, count):
    dout = load_ref[:, 0, :, h * HD : (h + 1) * HD].reshape(count, HD)
    return jnp.concatenate([jnp.zeros_like(dout), dout], axis=1)


def query_kernel(rows, shards, pair_ref, begin_ref, last_ref, q_ref, kv0, kv1, kv2, end_ref, load_ref, dq_ref, acc_ref):
    seq = pl.program_id(0)
    group = chunk_of(shards)
    nq = TP * rows
    width = group * rows
    notes = load_ref[:, 0, :, 128:].reshape(nq, 128)
    acc_ref[...] = jnp.zeros_like(acc_ref)

    def step(c, _):
        for h, kv_ref in enumerate((kv0, kv1, kv2)):
            query = q_ref[:, 0, :, h * 128 : (h + 1) * 128].reshape(nq, 128)
            kv = kv_ref[0, pl.ds(c * group, group), 0].reshape(width, 128)
            seen = key_spots(c * width, width, begin_ref[seq * HG + h], end_ref[0, h])
            query = jnp.concatenate([query, notes], axis=1)
            dout = jnp.concatenate([output_gradient(load_ref, h, nq), notes], axis=1)
            scores = dot_nt(jnp.concatenate([kv, chooser(h, 1, width)], axis=1), query)
            prob = jnp.exp(jnp.where(seen, scores, FILL))
            dprob = dot_nt(jnp.concatenate([kv, chooser(h, 0, width)], axis=1), dout)
            acc_ref[h] += dot_tn(kv, (prob * dprob).astype(BF))
        return 0

    trips = [pl.cdiv(last_ref[seq * HG + h], width) for h in range(HG)]
    lax.fori_loop(0, functools.reduce(jnp.maximum, trips), step, 0)
    for h in range(HG):
        dq = (acc_ref[h][:HD] * (HD**-0.5)).T.astype(BF)
        dq_ref[:, 0, :, h * HD : (h + 1) * HD] = dq.reshape(TP, rows, HD)


def key_kernel(rows, pair_ref, begin_ref, reach_ref, place_ref, q_ref, load_ref, kv0, kv1, kv2, end_ref, old_ref, dkv_ref):
    seq = pl.program_id(0)
    span = TP * rows
    start = place_ref[0]
    reach = [reach_ref[seq * HG + h] for h in range(HG)]
    needed = functools.reduce(jnp.maximum, reach) > start

    @pl.when(needed)
    def _():
        notes = load_ref[:, 0, :, 128:].reshape(span, 128)
        for h, kv_ref in enumerate((kv0, kv1, kv2)):
            lanes = slice(h * 128, (h + 1) * 128)
            kv = kv_ref[0, :, 0].reshape(span, 128)
            query = q_ref[:, 0, :, lanes].reshape(span, 128)
            dout = output_gradient(load_ref, h, span)
            seen = key_spots(start, span, begin_ref[seq * HG + h], end_ref[0, h])
            scores = dot_nt(jnp.concatenate([kv, chooser(h, 1, span)], axis=1), jnp.concatenate([query, notes], axis=1))
            prob = jnp.exp(jnp.where(seen, scores, FILL))
            dprob = dot_nt(jnp.concatenate([kv, chooser(h, 0, span)], axis=1), jnp.concatenate([dout, notes], axis=1))
            sides = jnp.concatenate([(prob * dprob).astype(BF), prob.astype(BF)], axis=1)
            new = dot_nn(sides, jnp.concatenate([query, dout], axis=0))
            dkv_ref[:, 0, :, lanes] = old_ref[:, 0, :, lanes] + new.reshape(TP, rows, 128)

    @pl.when(jnp.logical_not(needed))
    def _():
        dkv_ref[...] = old_ref[...]


def project_kernel(seqs, rows, fresh, spot_ref, *refs):
    pieces, w_ref, bias_ref = refs[:8], refs[8], refs[9]
    kv_out, q_out, kv_tmp, q_tmp, kv_sem, q_sem = refs[10 if fresh else 12 :]
    keys = HG * 128
    tokens = seqs * rows
    me_u, me_y, me_c, source = (spot_ref[i] for i in range(4))
    for which in range(2):
        core = me_c if which == 0 else 1 - me_c
        x = jnp.concatenate([pieces[which * 4 + i][...] for i in range(4)], axis=0)
        if which == 0:
            q_tmp[...] = jnp.zeros_like(q_tmp)
        kv = (dot_nn(x, w_ref[:, :keys]) + bias_ref[0:1, :keys]).astype(BF)
        for i in range(4):
            p, q = i // 2, i % 2
            x_rel = jnp.where(core == 0, q, p)
            y_rel = jnp.where(core == 0, p, q)
            shard = jnp.bitwise_xor(me_y, y_rel) * 2 + core
            slot = which * 4 + i
            kv_tmp[slot] = kv[i * tokens : (i + 1) * tokens].reshape(seqs, rows, keys)
            spot = kv_out.at[jnp.bitwise_xor(me_u, x_rel), source, shard]
            pltpu.make_async_copy(kv_tmp.at[slot], spot, kv_sem.at[slot]).start()
        second = jnp.where(core == 0, x[2 * tokens : 3 * tokens], x[tokens : 2 * tokens])
        for y_rel, part in enumerate((x[:tokens], second)):
            query = (dot_nn(part, w_ref[:, keys:]) + bias_ref[0:1, keys:]) * (HD**-0.5)
            slot = which * 2 + y_rel
            query = query.astype(BF)
            for h in range(HG):
                q_tmp[slot, :, :, h * 128 : h * 128 + HD] = query[:, h * HD : (h + 1) * HD].reshape(seqs, rows, HD)
            shard = jnp.bitwise_xor(me_y, y_rel) * 2 + core
            pltpu.make_async_copy(q_tmp.at[slot], q_out.at[source, shard], q_sem.at[slot]).start()
    for slot in range(8):
        pltpu.make_async_copy(kv_tmp.at[slot], kv_out.at[0, 0, 0], kv_sem.at[slot]).wait()
    for slot in range(4):
        pltpu.make_async_copy(q_tmp.at[slot], q_out.at[0, 0], q_sem.at[slot]).wait()


def project(pieces, weight, bias, spot, buffers, ring, seqs, rows):
    keys = HG * 128
    width = weight.shape[0]
    tokens = seqs * rows
    extra = [] if buffers is None else list(buffers)
    anywhere = pl.BlockSpec(memory_space=pl.ANY)
    local = pl.BlockSpec(memory_space=pltpu.VMEM)
    return pl.pallas_call(
        functools.partial(project_kernel, seqs, rows, not extra),
        in_specs=[pl.BlockSpec(memory_space=pltpu.SMEM)] + [local] * 10 + [anywhere] * len(extra),
        out_specs=[anywhere, anywhere],
        scratch_shapes=[
            pltpu.VMEM((8, seqs, rows, keys), BF),
            pltpu.VMEM((4, seqs, rows, keys), BF),
            pltpu.SemaphoreType.DMA((8,)),
            pltpu.SemaphoreType.DMA((4,)),
        ],
        out_shape=[
            jax.ShapeDtypeStruct((2, ring, TP, seqs, rows, keys), BF),
            jax.ShapeDtypeStruct((ring, TP, seqs, rows, keys), BF),
        ],
        input_output_aliases={11: 0, 12: 1} if extra else {},
        compiler_params=pltpu.CompilerParams(vmem_limit_bytes=VMEM_LIMIT),
        cost_estimate=pl.CostEstimate(flops=12 * tokens * width * keys * 2, bytes_accessed=12 << 20, transcendentals=0),
        name="project",
    )(spot, *pieces, weight, bias, *extra)


def keys_spec(h, shards, rows):
    return pl.BlockSpec((1, shards, 1, rows, 128), lambda s, pair, *_: (pair[h], 0, s, 0, h))


def attend_forward(q_loc, kv, pair, begin, last, end_row_own):
    _, shards, seqs, rows, _ = kv.shape
    nq = TP * rows
    row_spec = pl.BlockSpec((TP, 1, rows, 384), lambda s, *_: (0, s, 0, 0))
    end_spec = pl.BlockSpec((1, HG, 1, nq), lambda s, *_: (s, 0, 0, 0))
    return pl.pallas_call(
        functools.partial(forward_kernel, rows, shards),
        grid_spec=pltpu.PrefetchScalarGridSpec(
            num_scalar_prefetch=3,
            grid=(seqs,),
            in_specs=[row_spec] + [keys_spec(h, shards, rows) for h in range(HG)] + [end_spec],
            out_specs=pl.BlockSpec((TP, 1, rows, 256), lambda s, *_: (0, s, 0, 0)),
            scratch_shapes=[pltpu.VMEM((HG, 1, nq), F32), pltpu.VMEM((HG, 1, nq), F32), pltpu.VMEM((HG, 128, nq), F32)],
        ),
        out_shape=jax.ShapeDtypeStruct((TP, seqs, rows, 256), BF),
        compiler_params=pltpu.CompilerParams(vmem_limit_bytes=VMEM_LIMIT),
        cost_estimate=pl.CostEstimate(flops=4 * 9 * nq * shards * rows * 128, bytes_accessed=12 << 20, transcendentals=0),
        name="attend_forward",
    )(pair, begin, last, q_loc, kv, kv, kv, end_row_own)


def attend_query(q_loc, kv, pair, begin, last, end_row_own, load):
    _, shards, seqs, rows, _ = kv.shape
    nq = TP * rows
    row_spec = pl.BlockSpec((TP, 1, rows, 384), lambda s, *_: (0, s, 0, 0))
    end_spec = pl.BlockSpec((1, HG, 1, nq), lambda s, *_: (s, 0, 0, 0))
    return pl.pallas_call(
        functools.partial(query_kernel, rows, shards),
        grid_spec=pltpu.PrefetchScalarGridSpec(
            num_scalar_prefetch=3,
            grid=(seqs,),
            in_specs=[row_spec]
            + [keys_spec(h, shards, rows) for h in range(HG)]
            + [end_spec, pl.BlockSpec((TP, 1, rows, 256), lambda s, *_: (0, s, 0, 0))],
            out_specs=pl.BlockSpec((TP, 1, rows, HG * HD), lambda s, *_: (0, s, 0, 0)),
            scratch_shapes=[pltpu.VMEM((HG, 128, nq), F32)],
        ),
        out_shape=jax.ShapeDtypeStruct((TP, seqs, rows, HG * HD), BF),
        compiler_params=pltpu.CompilerParams(vmem_limit_bytes=VMEM_LIMIT),
        cost_estimate=pl.CostEstimate(flops=6 * 9 * nq * shards * rows * 128, bytes_accessed=12 << 20, transcendentals=0),
        name="attend_query",
    )(pair, begin, last, q_loc, kv, kv, kv, end_row_own, load)


def attend_key(q_all, load, kv, pair, begin, reach, place, end_row, old):
    _, shards, seqs, rows, _ = kv.shape

    def own_keys(h):
        return pl.BlockSpec((1, TP, 1, rows, 128), lambda s, pair, begin, reach, place: (pair[h], place[1], s, 0, h))

    total = pl.BlockSpec((TP, 1, rows, 384), lambda s, *_: (0, s, 0, 0))
    return pl.pallas_call(
        functools.partial(key_kernel, rows),
        grid_spec=pltpu.PrefetchScalarGridSpec(
            num_scalar_prefetch=4,
            grid=(seqs,),
            in_specs=[
                pl.BlockSpec((TP, 1, rows, 384), lambda s, pair, begin, reach, place: (place[2], s, 0, 0)),
                pl.BlockSpec((TP, 1, rows, 256), lambda s, *_: (0, s, 0, 0)),
            ]
            + [own_keys(h) for h in range(HG)]
            + [pl.BlockSpec((1, HG, 1, TP * rows), lambda s, *_: (s, 0, 0, 0)), total],
            out_specs=total,
        ),
        out_shape=jax.ShapeDtypeStruct((TP, seqs, rows, 384), F32),
        input_output_aliases={10: 0},
        compiler_params=pltpu.CompilerParams(vmem_limit_bytes=VMEM_LIMIT),
        cost_estimate=pl.CostEstimate(flops=8 * 9 * (TP * rows) ** 2 * 128, bytes_accessed=8 << 20, transcendentals=0),
        name="attend_key",
    )(pair, begin, reach, place, q_all, load, kv, kv, kv, end_row, old)


def norm_parts(summed):
    centred = summed - jnp.mean(summed, axis=1, keepdims=True)
    inv_std = lax.rsqrt(jnp.mean(centred * centred, axis=1, keepdims=True) + NORM_EPS)
    return centred * inv_std, inv_std


def dense_kernel(fold, att_ref, x_ref, cot_ref, order_ref, dense_ref, out_ref, load_ref, dsum_ref, keep_ref, send_ref, w, note, grad, grad_note, act, slope, turn, in_sem, out_sem):
    tokens, width = x_ref.shape
    blocks = 2 * fold + 1

    def fetch(b):
        wide = pl.ds(b * width, width) if b < blocks else pl.ds(blocks * width, 128)
        return pltpu.make_async_copy(dense_ref.at[:, wide], w.at[b] if b < blocks else note, in_sem.at[b])

    def ship(b, side):
        wide = pl.ds(b * width, width) if b < blocks else pl.ds(blocks * width, 128)
        rows = pl.ds(side * (width // 2), width // 2)
        source = grad.at[b, rows] if b < blocks else grad_note.at[rows]
        return pltpu.make_async_copy(source, (send_ref if side else keep_ref).at[:, wide], out_sem.at[2 * b + side])

    def start_ship(b):
        ship(b, 0).start()
        ship(b, 1).start()

    for b in [0, blocks] + list(range(1, blocks)):
        fetch(b).start()
    att = jnp.concatenate([att_ref[t, :, : HG * HD] for t in range(TP)], axis=1)
    row = lax.broadcasted_iota(jnp.int32, (width, width), 0)
    turn[...] = (row == order_ref[0:1]).astype(F32).astype(BF)

    def turned(v):
        return dot_nn(v, turn[...]).astype(BF)

    fetch(0).wait()
    fetch(blocks).wait()
    vec = note[...].astype(F32).T
    gain_one, gain_two, shift_one, shift_two = (vec[i : i + 1] for i in range(2, 6))
    normed_one, inv_one = norm_parts(x_ref[...].astype(F32) + dot_nn(att, w[0]) + vec[0:1])
    mid = normed_one * gain_one + shift_one
    mid_low = mid.astype(BF)
    feed = mid + vec[1:2]
    for k in range(fold):
        fetch(1 + k).wait()
        inner = dot_nn(mid_low, w[1 + k]) + vec[6 + k : 7 + k]
        spread = 0.5 + 0.5 * lax.erf(inner * (0.5**0.5))
        act[k] = (inner * spread).astype(BF)
        slope[k] = spread + inner * (jnp.exp(-0.5 * inner * inner) * 0.3989422804014327)
    for k in range(fold):
        fetch(1 + fold + k).wait()
        feed = feed + dot_nn(act[k], w[1 + fold + k])
    normed_two, inv_two = norm_parts(feed)
    out_ref[...] = (normed_two * gain_two + shift_two).astype(BF)
    grad_out = cot_ref[...].astype(F32)

    def back(incoming, normed, inv_std, gain):
        scaled = incoming * gain
        along = jnp.mean(scaled * normed, axis=1, keepdims=True)
        return inv_std * (scaled - jnp.mean(scaled, axis=1, keepdims=True) - normed * along)

    def total(v):
        return jnp.sum(v, axis=0, keepdims=True)

    dsecond = back(grad_out, normed_two, inv_two, gain_two)
    dfeed = dsecond.astype(BF)
    sums = [None, total(dfeed.astype(F32)), None, total(grad_out * normed_two), None, total(grad_out)]
    dmid = dsecond
    mid_turned = turned(mid_low)
    for k in range(fold):
        dinner = (dot_nt(dfeed, w[1 + fold + k]) * slope[k]).astype(BF)
        sums.append(total(dinner.astype(F32)))
        grad[k] = dot_tn(mid_turned, dinner).astype(BF)
        start_ship(k)
        grad[fold + k] = dot_tn(turned(act[k]), dfeed).astype(BF)
        start_ship(fold + k)
        dmid = dmid + dot_nt(dinner, w[1 + k])
    dsum = back(dmid, normed_one, inv_one, gain_one)
    dsum_ref[...] = dsum
    dproj = dsum.astype(BF)
    sums[0], sums[2], sums[4] = total(dproj.astype(F32)), total(dmid * normed_one), total(dmid)
    datt = dot_nt(dproj, w[0]).astype(BF)
    product = datt.astype(F32) * att.astype(F32)
    high = product.astype(BF)
    rest = (product - high.astype(F32)).astype(BF)
    feature = lax.broadcasted_iota(jnp.int32, (width, 128), 0)
    lane = lanes_like((width, 128))
    third = lanes_like((tokens, HD)) % 3
    for t in range(TP):
        of_head = ((feature // HD == t * HG + lane // 3) & (lane < 3 * HG)).astype(F32).astype(BF)
        delta = (dot_nn(high, of_head) + dot_nn(rest, of_head))[:, :HD]
        one, two, three = (v.astype(F32) for v in split_three(delta))
        notes = jnp.where(third == 0, one, jnp.where(third == 1, two, three))
        load_ref[t, :, : HG * HD] = datt[:, t * HG * HD : (t + 1) * HG * HD]
        load_ref[t, :, HG * HD :] = (notes + att_ref[t, :, HG * HD :].astype(F32)).astype(BF)
    grad[2 * fold] = dot_tn(turned(att), dproj).astype(BF)
    start_ship(2 * fold)
    table = jnp.concatenate(sums + [jnp.zeros((128 - len(sums), width), F32)], axis=0)
    grad_note[...] = dot_nn(table.astype(BF), turn[...]).T.astype(BF)
    start_ship(blocks)
    for b in range(blocks + 1):
        ship(b, 0).wait()
        ship(b, 1).wait()


def dense_layers(att, x, cotangent, order, dense, fold):
    tokens, width = x.shape
    blocks = 2 * fold + 1
    local = pl.BlockSpec(memory_space=pltpu.VMEM)
    anywhere = pl.BlockSpec(memory_space=pl.ANY)
    return pl.pallas_call(
        functools.partial(dense_kernel, fold),
        in_specs=[local, local, local, local, anywhere],
        out_specs=[local, local, local, anywhere, anywhere],
        out_shape=[
            jax.ShapeDtypeStruct((tokens, width), BF),
            jax.ShapeDtypeStruct((TP, tokens, 256), BF),
            jax.ShapeDtypeStruct((tokens, width), F32),
            jax.ShapeDtypeStruct((width // 2, blocks * width + 128), BF),
            jax.ShapeDtypeStruct((width // 2, blocks * width + 128), BF),
        ],
        scratch_shapes=[
            pltpu.VMEM((blocks, width, width), BF),
            pltpu.VMEM((width, 128), BF),
            pltpu.VMEM((blocks, width, width), BF),
            pltpu.VMEM((width, 128), BF),
            pltpu.VMEM((fold, tokens, width), BF),
            pltpu.VMEM((fold, tokens, width), F32),
            pltpu.VMEM((width, width), BF),
            pltpu.SemaphoreType.DMA((blocks + 1,)),
            pltpu.SemaphoreType.DMA((2 * blocks + 2,)),
        ],
        compiler_params=pltpu.CompilerParams(vmem_limit_bytes=VMEM_LIMIT),
        cost_estimate=pl.CostEstimate(flops=54 * tokens * width * width, bytes_accessed=24 << 20, transcendentals=0),
        name="dense_layers",
    )(att, x, cotangent, order, dense)


def tail_kernel(rows, part, spot_ref, dq_ref, dkv_ref, w_ref, *refs):
    pieces, (keep_ref, send_ref, dw_ref) = refs[:8], refs[8:]
    me_y, me_c = spot_ref[1], spot_ref[2]
    lane = lanes_like((1, HG * 128))
    is_own = jnp.zeros((1, HG * 128), jnp.int32)
    for h in range(HG):
        is_own = jnp.where(lane // 128 == h, spot_ref[3 + h], is_own)
    tokens, width = pieces[0].shape
    own_side, oth_side, near_x, far_x = [], [], [], []
    sum_q = sum_kv = 0.0
    for which, out_ref in enumerate((keep_ref, send_ref)):
        core = me_c if which == 0 else 1 - me_c
        middle = [pieces[4 * which + i][...] for i in (1, 2)]
        for y_rel in range(2):
            shard = jnp.bitwise_xor(me_y, y_rel) * 2 + core
            dq = dq_ref[shard].reshape(tokens, HG * HD)
            dkv = dkv_ref[shard].reshape(tokens, HG * 128)
            own = jnp.concatenate([jnp.where(is_own == 1, dkv, 0.0).astype(BF), dq], axis=1)
            oth = jnp.where(is_own == 1, 0.0, dkv).astype(BF)
            sum_q = sum_q + jnp.sum(dq.astype(F32), axis=0, keepdims=True)
            sum_kv = sum_kv + jnp.sum(dkv.astype(BF).astype(F32), axis=0, keepdims=True)
            to_own = dot_nt(own, w_ref[:, : HG * (128 + HD)]).astype(BF)
            to_oth = dot_nt(oth, w_ref[:, : HG * 128]).astype(BF)
            for x_rel, value in enumerate((to_own, to_oth)):
                out_ref[jnp.where(core == 0, x_rel, y_rel), jnp.where(core == 0, y_rel, x_rel)] = value
            own_side.append(own)
            oth_side.append(oth)
            first, last = pieces[4 * which][...], pieces[4 * which + 3][...]
            one = jnp.where(core == 0, middle[0], middle[1])
            two = jnp.where(core == 0, middle[1], middle[0])
            near_x.append(first if y_rel == 0 else two)
            far_x.append(one if y_rel == 0 else last)
    near = dot_tn(jnp.concatenate(near_x, axis=0), jnp.concatenate(own_side, axis=0))
    far = dot_tn(jnp.concatenate(far_x, axis=0), jnp.concatenate(oth_side, axis=0))
    dw_ref[:, : HG * 128] = (near[:, : HG * 128] + far).astype(BF)
    dw_ref[:, HG * 128 : HG * (128 + HD)] = near[:, HG * 128 :].astype(BF)
    values = [sum_q[:, h * HD : (h + 1) * HD] for h in range(HG)]
    values += [sum_kv[:, h * 128 + HD : (h + 1) * 128] for h in range(HG)]
    values = jnp.concatenate(values + [jnp.zeros((128 - 2 * HG, HD), F32)], axis=0).astype(BF)
    inside = lax.broadcasted_iota(jnp.int32, (width, 128), 0) % part
    place = (inside == lanes_like((width, 128))).astype(F32).astype(BF)
    dw_ref[:, HG * (128 + HD) :] = dot_nn(place, values).astype(BF)


def tail(spot, dq, dkv, weight, pieces, part):
    _, seqs, rows, _ = dq.shape
    tokens, width = pieces[0].shape
    local = pl.BlockSpec(memory_space=pltpu.VMEM)
    return pl.pallas_call(
        functools.partial(tail_kernel, rows, part),
        in_specs=[pl.BlockSpec(memory_space=pltpu.SMEM)] + [local] * 11,
        out_specs=[local, local, local],
        out_shape=[
            jax.ShapeDtypeStruct((2, 2, tokens, width), BF),
            jax.ShapeDtypeStruct((2, 2, tokens, width), BF),
            jax.ShapeDtypeStruct((width, 640), BF),
        ],
        compiler_params=pltpu.CompilerParams(vmem_limit_bytes=VMEM_LIMIT),
        cost_estimate=pl.CostEstimate(flops=16 * tokens * width * 480, bytes_accessed=16 << 20, transcendentals=0),
        name="tail",
    )(spot, dq, dkv, weight, *pieces)


def assemble_kernel(got_ref, grad_ref, note_ref):
    width = grad_ref.shape[1] // 3
    for t in range(TP):
        total = got_ref[0, t].astype(F32)
        for i in range(1, got_ref.shape[0]):
            total = total + got_ref[i, t].astype(F32)
        at = t * HG * HD
        grad_ref[:, at : at + HG * HD] = total[:, HG * 128 : HG * (128 + HD)]
        for h in range(HG):
            for j in range(2):
                to = (1 + j) * width + at + h * HD
                grad_ref[:, to : to + HD] = total[:, h * 128 + j * HD : h * 128 + (j + 1) * HD]
        note_ref[t] = total[:, HG * (128 + HD) :]


def assemble(got):
    _, _, part, _ = got.shape
    local = pl.BlockSpec(memory_space=pltpu.VMEM)
    return pl.pallas_call(
        assemble_kernel,
        in_specs=[local],
        out_specs=[local, local],
        out_shape=[
            jax.ShapeDtypeStruct((part, 3 * H * HD), F32),
            jax.ShapeDtypeStruct((TP, part, HD), F32),
        ],
        compiler_params=pltpu.CompilerParams(vmem_limit_bytes=VMEM_LIMIT),
        name="assemble",
    )(got)


def swap_on(axis):
    return lambda v: lax.ppermute(v, axis, [(0, 1), (1, 0)])


def crossing(first):
    pairs = []
    for u in range(2):
        for y in range(2):
            for c in range(2):
                along_u = (c == 0) == first
                to = (1 - u, y, c) if along_u else (u, 1 - y, c)
                pairs.append(((u * 2 + y) * 2 + c, (to[0] * 2 + to[1]) * 2 + to[2]))
    return lambda v: lax.ppermute(v, ("u", "y", "c"), pairs)


def after(v, *earlier):
    return lax.optimization_barrier((v,) + earlier)[0]


def add(a, b):
    return (a.astype(F32) + b.astype(F32)).astype(BF)


def pick(v, index, axis):
    return lax.dynamic_index_in_dim(v, index, axis, keepdims=False)


def put(buffer, v, index):
    return lax.dynamic_update_index_in_dim(buffer, v, index, 0)


def per_device(layer_input, wqkv, wo, wi, wd, biases, hidden_bias, gains, shifts, cotangent, block_ids, offsets, pairing):
    seqs, rows, width = layer_input.shape
    devices = lax.axis_size(ALL)
    ring = lax.axis_size("r")
    shards = ring * TP
    half = shards * rows
    tokens = seqs * rows
    me_u, me_r, me_y, me_c = (lax.axis_index(a) for a in ALL)
    me_t = me_y * 2 + me_c
    part = wqkv.shape[0]
    hidden = wi.shape[1]
    fold = hidden // width
    swap_u, swap_c = swap_on("u"), swap_on("c")
    cross_one, cross_two = crossing(True), crossing(False)
    forward = [(i, (i + 1) % ring) for i in range(ring)]

    notes = [biases[2:].T, gains.T, shifts.T, hidden_bias.reshape(fold, part).T]
    notes = jnp.concatenate(notes + [jnp.zeros((part, 128 - 6 - fold), BF)], axis=1)
    wi_turned = wi.reshape(part, devices, fold, part).transpose(0, 2, 1, 3).reshape(part, hidden)
    wd_cols = [wd[k * part : (k + 1) * part] for k in range(fold)]
    dense = lax.all_gather(jnp.concatenate([wo, wi_turned] + wd_cols + [notes], axis=1), ALL, axis=0, tiled=True)

    by_head = wqkv.reshape(part, 3, TP, HG, HD)
    blocks_kv = by_head[:, 1:].transpose(2, 0, 3, 1, 4).reshape(TP, part, HG * 128)
    blocks_q = by_head[:, 0].transpose(1, 0, 2, 3).reshape(TP, part, HG * HD)
    ends = jnp.pad(biases[:2].T, ((0, 0), (0, HD - 2)))
    blocks = jnp.concatenate([blocks_kv, blocks_q, jnp.broadcast_to(ends, (TP, part, HD))], axis=2)
    blocks = lax.all_to_all(blocks, ("y", "c"), split_axis=0, concat_axis=0, tiled=True)
    column = put(jnp.zeros((ring,) + blocks.shape, BF), blocks, me_r)
    for k in range(1, ring):
        got = lax.ppermute(blocks, "r", [(i, (i + k) % ring) for i in range(ring)])
        column = put(column, got, (me_r - k) % ring)
    both = jnp.zeros((2,) + column.shape, BF)
    w_here = put(put(both, column, me_u), swap_u(column), 1 - me_u).reshape(width, 640)
    b_heads = w_here[:, 576:578].astype(F32)
    b_heads = lax.dynamic_slice_in_dim(b_heads, me_t * HG * HD, HG * HD, 0).T
    b_kv = jnp.concatenate([jnp.zeros((HG, HD), F32), b_heads[1].reshape(HG, HD)], axis=1).reshape(-1)
    b_here = jnp.concatenate([b_kv, b_heads[0], jnp.zeros((HD,), F32)])
    b_here = jnp.broadcast_to(b_here, (8, 640))

    x_own = layer_input.reshape(tokens, width)
    piece = x_own
    stages = []
    for k in range(ring):
        if k == 1:
            piece, column = lax.optimization_barrier((piece, column))
        if k:
            piece = lax.ppermute(piece, "r", forward)
        if k >= 2:
            piece, stages[k - 2] = lax.optimization_barrier((piece, stages[k - 2]))
        one = cross_one(piece)
        two = cross_two(piece)
        if k == 1:
            one, w_here = lax.optimization_barrier((one, w_here))
        three = cross_two(one)
        if k >= 2:
            three, stages[k - 1] = lax.optimization_barrier((three, stages[k - 1]))
        mine = [piece, one, two, three]
        theirs = [swap_c(m) for m in mine]
        if k == 0:
            x_near = (mine, theirs)
        spot = jnp.stack([me_u, me_y, me_c, (me_r - k) % ring]).astype(jnp.int32)
        stages.append(project(mine + theirs, w_here, b_here, spot, stages[-1] if stages else None, ring, seqs, rows))
    buffers = stages[-1]
    kv = buffers[0].reshape(2, shards, seqs, rows, HG * 128)
    q_all = buffers[1].reshape(shards, seqs, rows, HG * 128)
    q_loc = lax.dynamic_slice_in_dim(q_all, me_r * TP, TP, 0)

    pair = lax.dynamic_slice_in_dim(pick(pairing, me_u, 1), me_t * HG, HG, 0)
    ids = block_ids.reshape(seqs, 2, half)
    ids_own = pick(ids, me_u, 1)
    ends = jnp.sum((ids[:, :, None, :] <= ids_own[:, None, :, None]).astype(jnp.int32), axis=-1)
    end_all = jnp.where((pair == 0)[None, :, None], ends[:, 0:1], ends[:, 1:2])
    end_loc = lax.dynamic_slice_in_dim(end_all, me_r * TP * rows, TP * rows, 2)
    begin = jnp.maximum(offsets[:, None] - pair[None, :] * half, 0).reshape(-1)
    last = end_loc[:, :, -1].reshape(-1)
    start = me_r * TP * rows
    end_ring = end_all.reshape(seqs, HG, ring, TP * rows)
    end_row_own = end_loc[:, :, None]

    att = attend_forward(q_loc, kv, pair, begin, last, end_row_own)
    att = lax.all_to_all(att, ("y", "c"), split_axis=0, concat_axis=0, tiled=True).reshape(TP, tokens, 256)

    index = jnp.arange(width, dtype=jnp.int32)
    inner_at, index = index % part, index // part
    r_rel, index = index % ring, index // ring
    s_rel, f_rel, c_rel = index % 2, index // 2 % 2, index // 4
    core = me_c ^ c_rel
    to_u = me_u ^ jnp.where(core == 0, f_rel, s_rel)
    to_y = me_y ^ jnp.where(core == 0, s_rel, f_rel)
    order = (((to_u * ring + (me_r + r_rel) % ring) * 2 + to_y) * 2 + core) * part + inner_at
    order = jnp.broadcast_to(order.astype(jnp.int32), (8, width))
    hidden_out, load, dsum, stay, leave = dense_layers(att, x_own, cotangent.reshape(tokens, width), order, dense, fold)
    hidden_out = hidden_out.reshape(seqs, rows, width)
    came = swap_c(leave)
    cut = width // 4
    high, low = add(stay[cut:], came[cut:]), add(stay[:cut], came[:cut])
    high_first = high
    cut = width // 8
    load = load.reshape(TP, seqs, rows, 256)
    load = lax.all_to_all(load, ("y", "c"), split_axis=0, concat_axis=0, tiled=True)
    came = cross_one(after(high_first, load))
    place = jnp.stack([start, me_r])
    dkv = jnp.zeros((TP, seqs, rows, HG * 128), F32)
    moving = load
    done = []
    for k in range(ring):
        if k >= 2:
            moving, done[k - 2] = lax.optimization_barrier((moving, done[k - 2]))
        if k == 2:
            moving, dq = lax.optimization_barrier((moving, dq))
        if k:
            moving = lax.ppermute(moving, "r", forward)
        source = (me_r - k) % ring
        ends_k = pick(end_ring, source, 2)
        where = jnp.concatenate([place, source[None]]).astype(jnp.int32)
        before = done[-1] if done else dkv
        if k == ring - 2:
            high2, low2 = add(low[cut:], came[cut:]), add(low[:cut], came[:cut])
            stay = add(low2, cross_two(high2))
            before = after(before, high2)
        done.append(attend_key(q_all, moving, kv, pair, begin, ends_k[:, :, -1].reshape(-1), where, ends_k[:, :, None], before))
        if k == 0:
            dq = attend_query(q_loc, kv, pair, begin, last, end_row_own, after(load, high))

    summed = stay[:part].astype(F32)
    for j in range(1, ring):
        along = [(i, (i + j) % ring) for i in range(ring)]
        summed = summed + lax.ppermute(stay[j * part : (j + 1) * part], "r", along).astype(F32)
    grad_w_in = summed[:, :hidden].reshape(part, fold, devices, part).transpose(0, 2, 1, 3).reshape(part, hidden)
    grad_w_down = jnp.concatenate([summed[:, hidden + k * width : hidden + (k + 1) * width] for k in range(fold)], axis=0)
    grad_w_out = summed[:, 2 * hidden : 2 * hidden + width]
    flat = summed[:, 2 * hidden + width : 2 * hidden + width + 6 + fold].T
    grad_bo, grad_gains, grad_shifts, grad_bin = flat[0:2], flat[2:4], flat[4:6], flat[6:].reshape(-1)


    spot = jnp.concatenate([jnp.stack([me_u, me_y, me_c]), (pair == me_u).astype(jnp.int32)])
    keep, send, dw = tail(spot.astype(jnp.int32), dq, done[-1], w_here, x_near[0] + x_near[1], part)
    keep = add(keep, swap_c(send))
    dw = after(dw, keep)
    got = lax.all_to_all(dw.reshape(devices, part, 640), ALL, split_axis=0, concat_axis=0, tiled=True)
    came = cross_one(keep[1])
    final = cross_two(add(keep[0, 1], came[1]))
    grad_input = dsum + keep[0, 0].astype(F32) + came[0].astype(F32) + final.astype(F32)
    grad_input = grad_input.astype(BF).reshape(seqs, rows, width)
    grad_w_qkv, note = assemble(after(got, final).reshape(2 * ring, TP, part, 640))
    at = lax.axis_index(ALL) * part
    grad_bq = lax.dynamic_slice_in_dim(note[:, :HG].reshape(width), at, part, 0)
    grad_bv = lax.dynamic_slice_in_dim(note[:, HG : 2 * HG].reshape(width), at, part, 0)
    grad_biases = jnp.concatenate([jnp.stack([grad_bq, grad_bv]), grad_bo])
    return (hidden_out, grad_input, grad_w_qkv, grad_w_out, grad_w_in, grad_w_down, grad_biases, grad_bin, grad_gains, grad_shifts)


def solution(mesh):
    wide = mesh.shape["blk"]
    grid = Mesh(mesh.devices.reshape(2, wide // TP, 2, TP // 2), ALL)
    rows2, cols1 = P(ALL, None), P(None, ALL)
    toks = P(None, ALL, None)
    return jax.shard_map(
        per_device,
        mesh=grid,
        in_specs=(toks, rows2, rows2, rows2, rows2, cols1, P(ALL), cols1, cols1, toks, P(), P(), P()),
        out_specs=(toks, toks, rows2, rows2, rows2, rows2, cols1, P(ALL), cols1, cols1),
        check_vma=False,
    )
```

time: 611 us -> 407 us (0.67)
  the two profiles are of different devices: /device:TPU:0 before, /device:TPU:8 now
where the time goes in v2:
time: 407 us; the launch traced here: 399 us
  waiting for transfers between devices  124 us (30%)
  Pallas kernels  116 us (29%)
  starting transfers between devices  74.6 us (18%)
  local copies, waits for them, and re-layouts  39.1 us (10%)
  other arithmetic  29.7 us (7%)
  between operations  15.3 us (4%)
    ppermute x3, waiting for transfers between devices, per_device(): piece = lax.ppermute(piece, 'r', forward)  34.6 us
    ppermute x3, waiting for transfers between devices, per_device(): lax.ppermute(stay[j * part:(j + 1) * part], 'r', along).astype(F32)  31.3 us
    pallas_call x4, Pallas kernels, attend_key(): pl.pallas_call(functools.partial(key_kernel, rows), grid_spec=pltpu.Prefe...  28.9 us
    pallas_call x1, Pallas kernels, dense_layers(): pl.pallas_call(functools.partial(dense_kernel, fold), in_specs=[local, lo...  25.1 us
    pallas_call x4, Pallas kernels, project(): pl.pallas_call(functools.partial(project_kernel, seqs, rows, not extra),...  23.1 us
    ppermute x16, starting transfers between devices, crossing(): return lambda v: lax.ppermute(v, ('u', 'y', 'c'), pairs)  20.1 us
    ppermute x19, starting transfers between devices, swap_on(): return lambda v: lax.ppermute(v, axis, [(0, 1), (1, 0)])  17.1 us
    ppermute x3, waiting for transfers between devices, per_device(): got = lax.ppermute(blocks, 'r', [(i, (i + k) % ring) for i in range(ring)])  16 us
  transfers between devices with their start and end apart: 52, of which 17 were waited for; matrix products, arithmetic and copies ran while one was open for 15% of the time, Pallas kernels for 22%

profile of v2, /device:TPU:8, one launch (start us, length us, event | category | flops | bytes accessed | tf_op | source)
XLA Modules:
  0.0 399.1 jit_solution(9942006710013830871)
XLA Ops:
  9.0 2.1 reshape.137
  15.4 3.3 all-to-all-start
  20.3 3.4 all-to-all-done
  28.4 8.1 %collective-permute-done = bf16[4,24,640]{2,1,0:T(8,128)(2,1)S(1)} collective-permute-done((bf16[4,24,640]{2,1,0:T(8,128)(2,1)S(1)}, bf16[4,24,640]{2,1,0:T(8,128)(2,1)S(1)}, u32[]{:S(2)}, u32[]{:S(2)}) %collective-permute-start) | collective-permute-done | bytes 122912 | tf_op jit(solution)/shard_map/ppermute | solution.py:592
  36.5 5.8 %collective-permute-done.1 = bf16[4,24,640]{2,1,0:T(8,128)(2,1)S(1)} collective-permute-done((bf16[4,24,640]{2,1,0:T(8,128)(2,1)S(1)}, bf16[4,24,640]{2,1,0:T(8,128)(2,1)S(1)}, u32[]{:S(2)}, u32[]{:S(2)}) %collective-permute-start.1) | collective-permute-done | bytes 122912 | tf_op jit(solution)/shard_map/ppermute | solution.py:592
  42.3 2.1 collective-permute-done.2
  49.3 15.4 %collective-permute-done.3.refs_0_ = bf16[288,768]{1,0:T(8,128)(2,1)} collective-permute-done((bf16[288,768]{1,0:T(8,128)(2,1)S(1)}, bf16[288,768]{1,0:T(8,128)(2,1)}, u32[]{:S(2)}, u32[]{:S(2)}) %collective-permute-start.3) | collective-permute-done | bytes 442400 | tf_op jit(solution)/shard_map/ppermute | solution.py:609
  66.1 3.0 collective-permute-done.12
  69.1 5.8 %collective-permute-start.10 = (bf16[288,768]{1,0:T(8,128)(2,1)S(1)}, bf16[288,768]{1,0:T(8,128)(2,1)S(1)}, u32[]{:S(2)}, u32[]{:S(2)}) collective-permute-start(bf16[288,768]{1,0:T(8,128)(2,1)S(1)} %collective-permute-done.6.refs_2_), channel_id=1, source_target_pairs={{0,1},{1,0},{2,3},{3,2},{4,5},{5,4},{6,7},{7,6},{8,9},{9,8},{10,11... | collective-permute-start | bytes 1327112 | tf_op jit(solution)/shard_map/ppermute | solution.py:532
  75.1 6.4 %collective-permute-start.11 = (bf16[288,768]{1,0:T(8,128)(2,1)}, bf16[288,768]{1,0:T(8,128)(2,1)S(1)}, u32[]{:S(2)}, u32[]{:S(2)}) collective-permute-start(bf16[288,768]{1,0:T(8,128)(2,1)} %collective-permute-done.7.refs_3_), channel_id=1, source_target_pairs={{0,1},{1,0},{2,3},{3,2},{4,5},{5,4},{6,7},{7,6},{8,9},{9,8},{10,11... | collective-permute-start | bytes 1327112 | tf_op jit(solution)/shard_map/ppermute | solution.py:532
  86.2 5.7 %project.4 = (bf16[2,4,4,3,96,384]{5,4,3,2,1,0:T(8,128)(2,1)}, bf16[4,4,3,96,384]{4,3,2,1,0:T(8,128)(2,1)}) custom-call(s32[4]{0:T(128)} %get-tuple-element.179.spot_ref, bf16[288,768]{1,0:T(8,128)(2,1)} %bitcast.137, bf16[288,768]{1,0:T(8,128)(2,1)} %copy-done.11, bf16[288,768]{1,0:T(8,128)(2,1)} %copy-done.12, ...), custom_call_target="tpu_custom_call" | custom-call | flops 2038431744 | bytes 12582912 | tf_op jit(solution)/shard_map/project/pallas_call | solution.py:204
  92.0 19.2 %collective-permute-done.4.refs_0_ = bf16[288,768]{1,0:T(8,128)(2,1)} collective-permute-done((bf16[288,768]{1,0:T(8,128)(2,1)}, bf16[288,768]{1,0:T(8,128)(2,1)}, u32[]{:S(2)}, u32[]{:S(2)}) %collective-permute-start.4) | collective-permute-done | bytes 442400 | tf_op jit(solution)/shard_map/ppermute | solution.py:609
  113.7 2.6 collective-permute-start.13
  116.3 3.4 collective-permute-done.14.refs_1_
  119.7 7.5 %convert_reduce_fusion = s32[3,2,1536]{2,1,0:T(2,128)S(1)} fusion(s32[3,1536]{1,0:T(4,128)S(1)} %bitcast.149, s32[3,2,1536]{2,1,0:T(2,128)S(1)} %le.17), kind=kLoop, calls=%fused_computation | loop fusion | flops 42458112 | bytes 92160 | tf_op jit(solution)/shard_map/reduce_sum | solution.py:633
  127.2 2.1 collective-permute-start.26
  130.3 5.9 %project.5 = (bf16[2,4,4,3,96,384]{5,4,3,2,1,0:T(8,128)(2,1)}, bf16[4,4,3,96,384]{4,3,2,1,0:T(8,128)(2,1)}) custom-call(s32[4]{0:T(128)} %get-tuple-element.178.spot_ref, bf16[288,768]{1,0:T(8,128)(2,1)} %collective-permute-done.3.refs_0_, bf16[288,768]{1,0:T(8,128)(2,1)} %copy-done.17, ...), custom_call_target="tpu_custom_call", output_to_operand_aliasing={{0}: (11, {}), {1}: (12, {})} | custom-call | flops 2038431744 | bytes 12582912 | tf_op jit(solution)/shard_map/project/pallas_call | solution.py:204
  139.4 9.2 %collective-permute-done.23.refs_1_ = bf16[288,768]{1,0:T(8,128)(2,1)S(1)} collective-permute-done((bf16[288,768]{1,0:T(8,128)(2,1)S(1)}, bf16[288,768]{1,0:T(8,128)(2,1)S(1)}, u32[]{:S(2)}, u32[]{:S(2)}) %collective-permute-start.23) | collective-permute-done | bytes 442400 | tf_op jit(solution)/shard_map/ppermute | solution.py:543
  151.9 5.7 %project.6 = (bf16[2,4,4,3,96,384]{5,4,3,2,1,0:T(8,128)(2,1)}, bf16[4,4,3,96,384]{4,3,2,1,0:T(8,128)(2,1)}) custom-call(s32[4]{0:T(128)} %get-tuple-element.144.spot_ref, bf16[288,768]{1,0:T(8,128)(2,1)} %collective-permute-done.4.refs_0_, bf16[288,768]{1,0:T(8,128)(2,1)} %copy-done.16, ...), custom_call_target="tpu_custom_call", output_to_operand_aliasing={{0}: (11, {}), {1}: (12, {})} | custom-call | flops 2038431744 | bytes 12582912 | tf_op jit(solution)/shard_map/project/pallas_call | solution.py:204
  160.5 5.8 %project.7 = (bf16[2,4,4,3,96,384]{5,4,3,2,1,0:T(8,128)(2,1)}, bf16[4,4,3,96,384]{4,3,2,1,0:T(8,128)(2,1)}) custom-call(s32[4]{0:T(128)} %get-tuple-element.180.spot_ref, bf16[288,768]{1,0:T(8,128)(2,1)} %copy-done.15, bf16[288,768]{1,0:T(8,128)(2,1)} %copy-done.19, ...), custom_call_target="tpu_custom_call", output_to_operand_aliasing={{0}: (11, {}), {1}: (12, {})} | custom-call | flops 2038431744 | bytes 12582912 | tf_op jit(solution)/shard_map/project/pallas_call | solution.py:204
  166.3 2.2 constant_dynamic-slice_fusion.5.q_ref
  168.5 13.8 %attend_forward.1 = bf16[4,3,96,256]{3,2,1,0:T(8,128)(2,1)} custom-call(s32[3]{0:T(128)} %copy-done.34, s32[9]{0:T(128)} %max.8.begin_ref, s32[9]{0:T(128)} %reshape_squeeze.18.last_ref, bf16[4,3,96,384]{3,2,1,0:T(8,128)(2,1)} %constant_dynamic-slice_fusion.5.q_ref, bf16[2,16,3,96,384]{4,3,2,1,0:T(8,128)(2,1)} %bitcast.102, ...), custom_call_target="tpu_custom_call" | custom-call | flops 2717908992 | bytes 12582912 | tf_op jit(solution)/shard_map/attend_forward/pallas_call | solution.py:234
  182.3 3.9 all-to-all-start.1
  186.2 9.2 %all-to-all-done.1 = bf16[4,3,96,256]{3,2,1,0:T(8,128)(2,1)S(1)} async-done(((bf16[4,3,96,256]{3,2,1,0:T(8,128)(2,1)}), bf16[4,3,96,256]{3,2,1,0:T(8,128)(2,1)S(1)}, u32[]{:S(2)}, u32[]{:S(2)}) %all-to-all-start.1) | async-done | bytes 589856 | tf_op jit(solution)/shard_map/all_to_all | solution.py:643
  196.3 25.1 %dense_layers.1 = (bf16[288,768]{1,0:T(8,128)(2,1)}, bf16[4,288,256]{2,1,0:T(8,128)(2,1)}, f32[288,768]{1,0:T(8,128)}, bf16[384,7040]{1,0:T(8,128)(2,1)}, bf16[384,7040]{1,0:T(8,128)(2,1)}) custom-call(bf16[4,288,256]{2,1,0:T(8,128)(2,1)} %bitcast.136, bf16[288,768]{1,0:T(8,128)(2,1)} %bitcast.138, bf16[288,768]{1,0:T(8,128)(2,1)} %bitcast.150, ...), custom_call_target="tpu_custom_call" | custom-call | flops 9172942848 | bytes 25165824 | tf_op jit(solution)/shard_map/dense_layers/pallas_call | solution.py:409
  221.5 3.5 all-to-all-start.2
  225.0 5.7 %collective-permute-done.36 = bf16[384,7040]{1,0:T(8,128)(2,1)} collective-permute-done((bf16[384,7040]{1,0:T(8,128)(2,1)}, bf16[384,7040]{1,0:T(8,128)(2,1)}, u32[]{:S(2)}, u32[]{:S(2)}) %collective-permute-start.36) | collective-permute-done | bytes 5406752 | tf_op jit(solution)/shard_map/ppermute | solution.py:532
  230.7 5.9 %add_convert_fusion = (bf16[192,7040]{1,0:T(8,128)(2,1)S(1)}, bf16[192,7040]{1,0:T(8,128)(2,1)}) fusion(bf16[384,7040]{1,0:T(8,128)(2,1)} %collective-permute-done.36, bf16[384,7040]{1,0:T(8,128)(2,1)} %get-tuple-element.71), kind=kLoop, calls=%fused_computation.1 | loop fusion | flops 10813440 | bytes 16220160 | tf_op jit(solution)/shard_map/convert_element_type | solution.py:551
  236.7 2.5 collective-permute-start.39
  239.4 2.6 collective-permute-start.35
  245.7 7.2 %attend_key.4.old_ref = f32[4,3,96,384]{3,2,1,0:T(8,128)} custom-call(s32[3]{0:T(128)} %copy-done.34, s32[9]{0:T(128)} %max.8.begin_ref, s32[9]{0:T(128)} %reshape_squeeze.20.reach_ref, s32[3]{0:T(128)} %get-tuple-element.177.place_ref, bf16[16,3,96,384]{3,2,1,0:T(8,128)(2,1)} %bitcast.121, ...), custom_call_target="tpu_custom_call", output_to_operand_aliasing={{}: (10, {})} | custom-call | flops 1358954496 | bytes 8388608 | tf_op jit(solution)/shard_map/attend_key/pallas_call | solution.py:280
  252.9 14.2 %attend_query.1.dq_ref = bf16[4,3,96,192]{3,2,1,0:T(8,128)(2,1)} custom-call(s32[3]{0:T(128)} %copy-done.34, s32[9]{0:T(128)} %max.8.begin_ref, s32[9]{0:T(128)} %reshape_squeeze.18.last_ref, bf16[4,3,96,384]{3,2,1,0:T(8,128)(2,1)} %constant_dynamic-slice_fusion.5.q_ref, bf16[2,16,3,96,384]{4,3,2,1,0:T(8,128)(2,1)} %bitcast.108, ...), custom_call_target="tpu_custom_call" | custom-call | flops 4076863488 | bytes 12582912 | tf_op jit(solution)/shard_map/attend_query/pallas_call | solution.py:255
  267.1 2.3 collective-permute-start.37
  270.0 2.7 add_convert_fusion.5
  274.8 7.2 %attend_key.5.old_ref = f32[4,3,96,384]{3,2,1,0:T(8,128)} custom-call(s32[3]{0:T(128)} %copy-done.34, s32[9]{0:T(128)} %max.8.begin_ref, s32[9]{0:T(128)} %reshape_squeeze.22.reach_ref, s32[3]{0:T(128)} %get-tuple-element.175.place_ref, bf16[16,3,96,384]{3,2,1,0:T(8,128)(2,1)} %bitcast.122, ...), custom_call_target="tpu_custom_call", output_to_operand_aliasing={{}: (10, {})} | custom-call | flops 1358954496 | bytes 8388608 | tf_op jit(solution)/shard_map/attend_key/pallas_call | solution.py:280
  285.8 7.2 %attend_key.6.old_ref = f32[4,3,96,384]{3,2,1,0:T(8,128)} custom-call(s32[3]{0:T(128)} %copy-done.34, s32[9]{0:T(128)} %max.8.begin_ref, s32[9]{0:T(128)} %reshape_squeeze.23.reach_ref, s32[3]{0:T(128)} %get-tuple-element.140.place_ref, bf16[16,3,96,384]{3,2,1,0:T(8,128)(2,1)} %bitcast.123, ...), custom_call_target="tpu_custom_call", output_to_operand_aliasing={{}: (10, {})} | custom-call | flops 1358954496 | bytes 8388608 | tf_op jit(solution)/shard_map/attend_key/pallas_call | solution.py:280
  293.0 5.4 %collective-permute-done.38.load_ref = bf16[4,3,96,256]{3,2,1,0:T(8,128)(2,1)} collective-permute-done((bf16[4,3,96,256]{3,2,1,0:T(8,128)(2,1)S(1)}, bf16[4,3,96,256]{3,2,1,0:T(8,128)(2,1)}, u32[]{:S(2)}, u32[]{:S(2)}) %collective-permute-start.38) | collective-permute-done | bytes 589856 | tf_op jit(solution)/shard_map/ppermute | solution.py:674
  298.5 7.2 %attend_key.7.dkv_ref = f32[4,3,96,384]{3,2,1,0:T(8,128)} custom-call(s32[3]{0:T(128)} %copy-done.34, s32[9]{0:T(128)} %max.8.begin_ref, s32[9]{0:T(128)} %reshape_squeeze.21.reach_ref, s32[3]{0:T(128)} %get-tuple-element.176.place_ref, bf16[16,3,96,384]{3,2,1,0:T(8,128)(2,1)} %bitcast.124, ...), custom_call_target="tpu_custom_call", output_to_operand_aliasing={{}: (10, {})} | custom-call | flops 1358954496 | bytes 8388608 | tf_op jit(solution)/shard_map/attend_key/pallas_call | solution.py:280
  305.7 9.0 %tail.1 = (bf16[2,2,288,768]{3,2,1,0:T(8,128)(2,1)}, bf16[2,2,288,768]{3,2,1,0:T(8,128)(2,1)}, bf16[768,640]{1,0:T(8,128)(2,1)}) custom-call(s32[6]{0:T(128)} %pad_add_fusion.5.spot_ref, bf16[4,3,96,192]{3,2,1,0:T(8,128)(2,1)} %attend_query.1.dq_ref, f32[4,3,96,384]{3,2,1,0:T(8,128)} %attend_key.7.dkv_ref, bf16[768,640]{1,0:T(8,128)(2,1)} %bitcast.130, ...), custom_call_target="tpu_custom_call" | custom-call | flops 1698693120 | bytes 16777216 | tf_op jit(solution)/shard_map/tail/pallas_call | solution.py:485
  314.7 2.3 add_convert_fusion.3
  319.3 4.6 %collective-permute-start.45 = (bf16[24,7040]{1,0:T(8,128)(2,1)S(1)}, bf16[24,7040]{1,0:T(8,128)(2,1)S(1)}, u32[]{:S(2)}, u32[]{:S(2)}) collective-permute-start(bf16[24,7040]{1,0:T(8,128)(2,1)S(1)} %get-tuple-element.150), channel_id=1, source_target_pairs={{0,8},{4,12},{8,0},{12,4},{1,9},{5,13},{9,1},{13,5},{2,10},{6,14},... | collective-permute-start | bytes 1013768 | tf_op jit(solution)/shard_map/ppermute | solution.py:690
  324.4 6.7 %all-to-all-start.3 = ((bf16[32,24,640]{2,1,0:T(8,128)(2,1)}), bf16[32,24,640]{2,1,0:T(8,128)(2,1)}, u32[]{:S(2)}, u32[]{:S(2)}) async-start(bf16[32,24,640]{2,1,0:T(8,128)(2,1)} %bitcast.44), calls=%async_computation.3 | async-start | bytes 1966080 | tf_op jit(solution)/shard_map/all_to_all | solution.py:702
  332.7 27.2 %collective-permute-done.45 = bf16[24,7040]{1,0:T(8,128)(2,1)S(1)} collective-permute-done((bf16[24,7040]{1,0:T(8,128)(2,1)S(1)}, bf16[24,7040]{1,0:T(8,128)(2,1)S(1)}, u32[]{:S(2)}, u32[]{:S(2)}) %collective-permute-start.45) | collective-permute-done | bytes 337952 | tf_op jit(solution)/shard_map/ppermute | solution.py:690
  359.9 4.1 %collective-permute-done.46 = bf16[24,7040]{1,0:T(8,128)(2,1)S(1)} collective-permute-done((bf16[24,7040]{1,0:T(8,128)(2,1)S(1)}, bf16[24,7040]{1,0:T(8,128)(2,1)S(1)}, u32[]{:S(2)}, u32[]{:S(2)}) %collective-permute-start.46) | collective-permute-done | bytes 337952 | tf_op jit(solution)/shard_map/ppermute | solution.py:690
  366.3 3.2 collective-permute-start.42
  371.7 2.1 reshape.145
  373.8 2.4 copy.113
  376.2 4.1 %reshape.146 = f32[24,3072]{1,0:T(8,128)} reshape(f32[24,32,4,24]{3,2,1,0:T(4,128)} %copy.113) | data formatting | bytes 589824 | tf_op jit(solution)/shard_map/reshape | solution.py:691
  (258 shorter events, 67.2 us)
Async XLA Ops:
  7.2 188.2 %all-gather.2.cloned.1.call-start = ((), (), s32[]{:S(2)}) async-start(), calls=%async_computation.4 | async-start | bytes 11151360 | tf_op jit(solution)/shard_map/all_gather | solution.py:582
  15.4 8.3 %all-to-all-start = ((bf16[4,24,640]{2,1,0:T(8,128)(2,1)}), bf16[4,24,640]{2,1,0:T(8,128)(2,1)S(1)}, u32[]{:S(2)}, u32[]{:S(2)}) async-start(bf16[4,24,640]{2,1,0:T(8,128)(2,1)} %pad_maximum_fusion.1), calls=%async_computation | async-start | bytes 245760 | tf_op jit(solution)/shard_map/all_to_all | solution.py:589
  18.7 28.8 %collective-permute-start.5 = (bf16[288,768]{1,0:T(8,128)(2,1)S(1)}, bf16[288,768]{1,0:T(8,128)(2,1)S(1)}, u32[]{:S(2)}, u32[]{:S(2)}) collective-permute-start(bf16[288,768]{1,0:T(8,128)(2,1)S(1)} %bitcast.140), channel_id=1, source_target_pairs={{0,16},{1,3},{2,18},{3,1},{16,0},{17,19},{18,2},{19,17},{4,20},{5,... | collective-permute-start | bytes 1327112 | tf_op jit(solution)/shard_map/ppermute | solution.py:543
  23.7 12.8 %collective-permute-start = (bf16[4,24,640]{2,1,0:T(8,128)(2,1)S(1)}, bf16[4,24,640]{2,1,0:T(8,128)(2,1)S(1)}, u32[]{:S(2)}, u32[]{:S(2)}) collective-permute-start(bf16[4,24,640]{2,1,0:T(8,128)(2,1)S(1)} %all-to-all-done), channel_id=1, source_target_pairs={{0,4},{4,8},{8,12},{12,0},{1,5},{5,9},{9,13},{13,1},{2,6},{6,10},{... | collective-permute-start | bytes 368648 | tf_op jit(solution)/shard_map/ppermute | solution.py:592
  25.3 17.0 %collective-permute-start.1 = (bf16[4,24,640]{2,1,0:T(8,128)(2,1)S(1)}, bf16[4,24,640]{2,1,0:T(8,128)(2,1)S(1)}, u32[]{:S(2)}, u32[]{:S(2)}) collective-permute-start(bf16[4,24,640]{2,1,0:T(8,128)(2,1)S(1)} %all-to-all-done), channel_id=1, source_target_pairs={{0,8},{4,12},{8,0},{12,4},{1,9},{5,13},{9,1},{13,5},{2,10},{6,14},... | collective-permute-start | bytes 368648 | tf_op jit(solution)/shard_map/ppermute | solution.py:592
  26.3 18.1 %collective-permute-start.2 = (bf16[4,24,640]{2,1,0:T(8,128)(2,1)S(1)}, bf16[4,24,640]{2,1,0:T(8,128)(2,1)S(1)}, u32[]{:S(2)}, u32[]{:S(2)}) collective-permute-start(bf16[4,24,640]{2,1,0:T(8,128)(2,1)S(1)} %all-to-all-done), channel_id=1, source_target_pairs={{0,12},{4,0},{8,4},{12,8},{1,13},{5,1},{9,5},{13,9},{2,14},{6,2},{... | collective-permute-start | bytes 368648 | tf_op jit(solution)/shard_map/ppermute | solution.py:592
  44.5 20.2 %collective-permute-start.3 = (bf16[288,768]{1,0:T(8,128)(2,1)S(1)}, bf16[288,768]{1,0:T(8,128)(2,1)}, u32[]{:S(2)}, u32[]{:S(2)}) collective-permute-start(bf16[288,768]{1,0:T(8,128)(2,1)S(1)} %bitcast.141), channel_id=1, source_target_pairs={{0,4},{4,8},{8,12},{12,0},{1,5},{5,9},{9,13},{13,1},{2,6},{6,10},{... | collective-permute-start | bytes 1327112 | tf_op jit(solution)/shard_map/ppermute | solution.py:609
  44.5 21.5 %collective-permute-start.6 = (bf16[288,768]{1,0:T(8,128)(2,1)S(1)}, bf16[288,768]{1,0:T(8,128)(2,1)S(1)}, u32[]{:S(2)}, u32[]{:S(2)}) collective-permute-start(bf16[288,768]{1,0:T(8,128)(2,1)S(1)} %bitcast.142), channel_id=1, source_target_pairs={{0,2},{1,17},{2,0},{3,19},{16,18},{17,1},{18,16},{19,3},{4,6},{5,2... | collective-permute-start | bytes 1327112 | tf_op jit(solution)/shard_map/ppermute | solution.py:543
  44.9 38.4 %collective-permute-start.8 = (bf16[288,768]{1,0:T(8,128)(2,1)S(1)}, bf16[288,768]{1,0:T(8,128)(2,1)}, u32[]{:S(2)}, u32[]{:S(2)}) collective-permute-start(bf16[288,768]{1,0:T(8,128)(2,1)S(1)} %bitcast.143), channel_id=1, source_target_pairs={{0,1},{1,0},{2,3},{3,2},{4,5},{5,4},{6,7},{7,6},{8,9},{9,8},{10,11... | collective-permute-start | bytes 1327112 | tf_op jit(solution)/shard_map/ppermute | solution.py:532
  45.8 23.3 %collective-permute-start.12 = (bf16[4,4,24,640]{3,2,1,0:T(8,128)(2,1)S(1)}, bf16[4,4,24,640]{3,2,1,0:T(8,128)(2,1)S(1)}, u32[]{:S(2)}, u32[]{:S(2)}) collective-permute-start(bf16[4,4,24,640]{3,2,1,0:T(8,128)(2,1)S(1)} %bitcast_dynamic-update-slice_fusion.2), channel_id=1, source_target_pairs={{0,16},{16,0},{1,17},{17,1},{2,18},{18,2},{3,19},{19,3},{4,20},{20... | collective-permute-start | bytes 1474568 | tf_op jit(solution)/shard_map/ppermute | solution.py:532
  47.6 27.6 %collective-permute-start.7 = (bf16[288,768]{1,0:T(8,128)(2,1)S(1)}, bf16[288,768]{1,0:T(8,128)(2,1)}, u32[]{:S(2)}, u32[]{:S(2)}) collective-permute-start(bf16[288,768]{1,0:T(8,128)(2,1)S(1)} %collective-permute-done.5.refs_1_), channel_id=1, source_target_pairs={{0,2},{1,17},{2,0},{3,19},{16,18},{17,1},{18,16},{19,3},{4,6},{5,2... | collective-permute-start | bytes 1327112 | tf_op jit(solution)/shard_map/ppermute | solution.py:543
  64.7 16.9 %collective-permute-start.16 = (bf16[288,768]{1,0:T(8,128)(2,1)}, bf16[288,768]{1,0:T(8,128)(2,1)S(1)}, u32[]{:S(2)}, u32[]{:S(2)}) collective-permute-start(bf16[288,768]{1,0:T(8,128)(2,1)} %collective-permute-done.3.refs_0_), channel_id=1, source_target_pairs={{0,16},{1,3},{2,18},{3,1},{16,0},{17,19},{18,2},{19,17},{4,20},{5,... | collective-permute-start | bytes 1327112 | tf_op jit(solution)/shard_map/ppermute | solution.py:543
  66.0 17.3 %collective-permute-start.9 = (bf16[288,768]{1,0:T(8,128)(2,1)S(1)}, bf16[288,768]{1,0:T(8,128)(2,1)}, u32[]{:S(2)}, u32[]{:S(2)}) collective-permute-start(bf16[288,768]{1,0:T(8,128)(2,1)S(1)} %collective-permute-done.5.refs_1_), channel_id=1, source_target_pairs={{0,1},{1,0},{2,3},{3,2},{4,5},{5,4},{6,7},{7,6},{8,9},{9,8},{10,11... | collective-permute-start | bytes 1327112 | tf_op jit(solution)/shard_map/ppermute | solution.py:532
  69.1 15.2 %collective-permute-start.10 = (bf16[288,768]{1,0:T(8,128)(2,1)S(1)}, bf16[288,768]{1,0:T(8,128)(2,1)S(1)}, u32[]{:S(2)}, u32[]{:S(2)}) collective-permute-start(bf16[288,768]{1,0:T(8,128)(2,1)S(1)} %collective-permute-done.6.refs_2_), channel_id=1, source_target_pairs={{0,1},{1,0},{2,3},{3,2},{4,5},{5,4},{6,7},{7,6},{8,9},{9,8},{10,11... | collective-permute-start | bytes 1327112 | tf_op jit(solution)/shard_map/ppermute | solution.py:532
  75.1 10.3 %collective-permute-start.11 = (bf16[288,768]{1,0:T(8,128)(2,1)}, bf16[288,768]{1,0:T(8,128)(2,1)S(1)}, u32[]{:S(2)}, u32[]{:S(2)}) collective-permute-start(bf16[288,768]{1,0:T(8,128)(2,1)} %collective-permute-done.7.refs_3_), channel_id=1, source_target_pairs={{0,1},{1,0},{2,3},{3,2},{4,5},{5,4},{6,7},{7,6},{8,9},{9,8},{10,11... | collective-permute-start | bytes 1327112 | tf_op jit(solution)/shard_map/ppermute | solution.py:532
  81.6 29.6 %collective-permute-start.4 = (bf16[288,768]{1,0:T(8,128)(2,1)}, bf16[288,768]{1,0:T(8,128)(2,1)}, u32[]{:S(2)}, u32[]{:S(2)}) collective-permute-start(bf16[288,768]{1,0:T(8,128)(2,1)} %collective-permute-done.3.refs_0_), channel_id=1, source_target_pairs={{0,4},{4,8},{8,12},{12,0},{1,5},{5,9},{9,13},{13,1},{2,6},{6,10},{... | collective-permute-start | bytes 1327112 | tf_op jit(solution)/shard_map/ppermute | solution.py:609
  83.3 29.9 %collective-permute-start.17 = (bf16[288,768]{1,0:T(8,128)(2,1)}, bf16[288,768]{1,0:T(8,128)(2,1)}, u32[]{:S(2)}, u32[]{:S(2)}) collective-permute-start(bf16[288,768]{1,0:T(8,128)(2,1)} %collective-permute-done.3.refs_0_), channel_id=1, source_target_pairs={{0,2},{1,17},{2,0},{3,19},{16,18},{17,1},{18,16},{19,3},{4,6},{5,2... | collective-permute-start | bytes 1327112 | tf_op jit(solution)/shard_map/ppermute | solution.py:543
  83.3 30.3 %collective-permute-start.19 = (bf16[288,768]{1,0:T(8,128)(2,1)}, bf16[288,768]{1,0:T(8,128)(2,1)}, u32[]{:S(2)}, u32[]{:S(2)}) collective-permute-start(bf16[288,768]{1,0:T(8,128)(2,1)} %collective-permute-done.3.refs_0_), channel_id=1, source_target_pairs={{0,1},{1,0},{2,3},{3,2},{4,5},{5,4},{6,7},{7,6},{8,9},{9,8},{10,11... | collective-permute-start | bytes 1327112 | tf_op jit(solution)/shard_map/ppermute | solution.py:532
  84.4 31.9 %collective-permute-start.18 = (bf16[288,768]{1,0:T(8,128)(2,1)}, bf16[288,768]{1,0:T(8,128)(2,1)}, u32[]{:S(2)}, u32[]{:S(2)}) collective-permute-start(bf16[288,768]{1,0:T(8,128)(2,1)} %copy-done.17), channel_id=1, source_target_pairs={{0,2},{1,17},{2,0},{3,19},{16,18},{17,1},{18,16},{19,3},{4,6},{5,2... | collective-permute-start | bytes 1327112 | tf_op jit(solution)/shard_map/ppermute | solution.py:543
  111.2 8.5 %collective-permute-start.14 = (bf16[288,768]{1,0:T(8,128)(2,1)}, bf16[288,768]{1,0:T(8,128)(2,1)S(1)}, u32[]{:S(2)}, u32[]{:S(2)}) collective-permute-start(bf16[288,768]{1,0:T(8,128)(2,1)} %collective-permute-done.4.refs_0_), channel_id=1, source_target_pairs={{0,16},{1,3},{2,18},{3,1},{16,0},{17,19},{18,2},{19,17},{4,20},{5,... | collective-permute-start | bytes 1327112 | tf_op jit(solution)/shard_map/ppermute | solution.py:543
  113.1 14.1 %collective-permute-start.20 = (bf16[288,768]{1,0:T(8,128)(2,1)}, bf16[288,768]{1,0:T(8,128)(2,1)S(1)}, u32[]{:S(2)}, u32[]{:S(2)}) collective-permute-start(bf16[288,768]{1,0:T(8,128)(2,1)} %copy-done.17), channel_id=1, source_target_pairs={{0,1},{1,0},{2,3},{3,2},{4,5},{5,4},{6,7},{7,6},{8,9},{9,8},{10,11... | collective-permute-start | bytes 1327112 | tf_op jit(solution)/shard_map/ppermute | solution.py:532
  113.2 16.2 %collective-permute-start.21 = (bf16[288,768]{1,0:T(8,128)(2,1)}, bf16[288,768]{1,0:T(8,128)(2,1)S(1)}, u32[]{:S(2)}, u32[]{:S(2)}) collective-permute-start(bf16[288,768]{1,0:T(8,128)(2,1)} %collective-permute-done.17.refs_2_), channel_id=1, source_target_pairs={{0,1},{1,0},{2,3},{3,2},{4,5},{5,4},{6,7},{7,6},{8,9},{9,8},{10,11... | collective-permute-start | bytes 1327112 | tf_op jit(solution)/shard_map/ppermute | solution.py:532
  113.7 22.5 %collective-permute-start.13 = (bf16[288,768]{1,0:T(8,128)(2,1)}, bf16[288,768]{1,0:T(8,128)(2,1)S(1)}, u32[]{:S(2)}, u32[]{:S(2)}) collective-permute-start(bf16[288,768]{1,0:T(8,128)(2,1)} %collective-permute-done.4.refs_0_), channel_id=1, source_target_pairs={{0,4},{4,8},{8,12},{12,0},{1,5},{5,9},{9,13},{13,1},{2,6},{6,10},{... | collective-permute-start | bytes 1327112 | tf_op jit(solution)/shard_map/ppermute | solution.py:609
  116.3 13.2 %collective-permute-start.22 = (bf16[288,768]{1,0:T(8,128)(2,1)}, bf16[288,768]{1,0:T(8,128)(2,1)S(1)}, u32[]{:S(2)}, u32[]{:S(2)}) collective-permute-start(bf16[288,768]{1,0:T(8,128)(2,1)} %collective-permute-done.18.refs_3_), channel_id=1, source_target_pairs={{0,1},{1,0},{2,3},{3,2},{4,5},{5,4},{6,7},{7,6},{8,9},{9,8},{10,11... | collective-permute-start | bytes 1327112 | tf_op jit(solution)/shard_map/ppermute | solution.py:532
  119.7 16.4 %collective-permute-start.15 = (bf16[288,768]{1,0:T(8,128)(2,1)S(1)}, bf16[288,768]{1,0:T(8,128)(2,1)S(1)}, u32[]{:S(2)}, u32[]{:S(2)}) collective-permute-start(bf16[288,768]{1,0:T(8,128)(2,1)S(1)} %collective-permute-done.14.refs_1_), channel_id=1, source_target_pairs={{0,2},{1,17},{2,0},{3,19},{16,18},{17,1},{18,16},{19,3},{4,6},{5,2... | collective-permute-start | bytes 1327112 | tf_op jit(solution)/shard_map/ppermute | solution.py:543
  127.2 11.0 %collective-permute-start.26 = (bf16[288,768]{1,0:T(8,128)(2,1)}, bf16[288,768]{1,0:T(8,128)(2,1)}, u32[]{:S(2)}, u32[]{:S(2)}) collective-permute-start(bf16[288,768]{1,0:T(8,128)(2,1)} %collective-permute-done.4.refs_0_), channel_id=1, source_target_pairs={{0,2},{1,17},{2,0},{3,19},{16,18},{17,1},{18,16},{19,3},{4,6},{5,2... | collective-permute-start | bytes 1327112 | tf_op jit(solution)/shard_map/ppermute | solution.py:543
  129.3 9.4 %collective-permute-start.27 = (bf16[288,768]{1,0:T(8,128)(2,1)}, bf16[288,768]{1,0:T(8,128)(2,1)}, u32[]{:S(2)}, u32[]{:S(2)}) collective-permute-start(bf16[288,768]{1,0:T(8,128)(2,1)} %collective-permute-done.4.refs_0_), channel_id=1, source_target_pairs={{0,1},{1,0},{2,3},{3,2},{4,5},{5,4},{6,7},{7,6},{8,9},{9,8},{10,11... | collective-permute-start | bytes 1327112 | tf_op jit(solution)/shard_map/ppermute | solution.py:532
  136.2 12.4 %collective-permute-start.23 = (bf16[288,768]{1,0:T(8,128)(2,1)S(1)}, bf16[288,768]{1,0:T(8,128)(2,1)S(1)}, u32[]{:S(2)}, u32[]{:S(2)}) collective-permute-start(bf16[288,768]{1,0:T(8,128)(2,1)S(1)} %collective-permute-done.13.refs_0_), channel_id=1, source_target_pairs={{0,16},{1,3},{2,18},{3,1},{16,0},{17,19},{18,2},{19,17},{4,20},{5,... | collective-permute-start | bytes 1327112 | tf_op jit(solution)/shard_map/ppermute | solution.py:543
  138.2 13.0 %collective-permute-start.28 = (bf16[288,768]{1,0:T(8,128)(2,1)S(1)}, bf16[288,768]{1,0:T(8,128)(2,1)}, u32[]{:S(2)}, u32[]{:S(2)}) collective-permute-start(bf16[288,768]{1,0:T(8,128)(2,1)S(1)} %collective-permute-done.14.refs_1_), channel_id=1, source_target_pairs={{0,1},{1,0},{2,3},{3,2},{4,5},{5,4},{6,7},{7,6},{8,9},{9,8},{10,11... | collective-permute-start | bytes 1327112 | tf_op jit(solution)/shard_map/ppermute | solution.py:532
  138.2 13.2 %collective-permute-start.29 = (bf16[288,768]{1,0:T(8,128)(2,1)}, bf16[288,768]{1,0:T(8,128)(2,1)}, u32[]{:S(2)}, u32[]{:S(2)}) collective-permute-start(bf16[288,768]{1,0:T(8,128)(2,1)} %collective-permute-done.26.refs_2_), channel_id=1, source_target_pairs={{0,1},{1,0},{2,3},{3,2},{4,5},{5,4},{6,7},{7,6},{8,9},{9,8},{10,11... | collective-permute-start | bytes 1327112 | tf_op jit(solution)/shard_map/ppermute | solution.py:532
  138.7 13.0 %collective-permute-start.24 = (bf16[288,768]{1,0:T(8,128)(2,1)S(1)}, bf16[288,768]{1,0:T(8,128)(2,1)}, u32[]{:S(2)}, u32[]{:S(2)}) collective-permute-start(bf16[288,768]{1,0:T(8,128)(2,1)S(1)} %collective-permute-done.13.refs_0_), channel_id=1, source_target_pairs={{0,2},{1,17},{2,0},{3,19},{16,18},{17,1},{18,16},{19,3},{4,6},{5,2... | collective-permute-start | bytes 1327112 | tf_op jit(solution)/shard_map/ppermute | solution.py:543
  138.7 13.2 %collective-permute-start.30 = (bf16[288,768]{1,0:T(8,128)(2,1)S(1)}, bf16[288,768]{1,0:T(8,128)(2,1)}, u32[]{:S(2)}, u32[]{:S(2)}) collective-permute-start(bf16[288,768]{1,0:T(8,128)(2,1)S(1)} %collective-permute-done.15.refs_3_), channel_id=1, source_target_pairs={{0,1},{1,0},{2,3},{3,2},{4,5},{5,4},{6,7},{7,6},{8,9},{9,8},{10,11... | collective-permute-start | bytes 1327112 | tf_op jit(solution)/shard_map/ppermute | solution.py:532
  148.6 9.1 %collective-permute-start.25 = (bf16[288,768]{1,0:T(8,128)(2,1)S(1)}, bf16[288,768]{1,0:T(8,128)(2,1)}, u32[]{:S(2)}, u32[]{:S(2)}) collective-permute-start(bf16[288,768]{1,0:T(8,128)(2,1)S(1)} %collective-permute-done.23.refs_1_), channel_id=1, source_target_pairs={{0,2},{1,17},{2,0},{3,19},{16,18},{17,1},{18,16},{19,3},{4,6},{5,2... | collective-permute-start | bytes 1327112 | tf_op jit(solution)/shard_map/ppermute | solution.py:543
  182.3 13.2 %all-to-all-start.1 = ((bf16[4,3,96,256]{3,2,1,0:T(8,128)(2,1)}), bf16[4,3,96,256]{3,2,1,0:T(8,128)(2,1)S(1)}, u32[]{:S(2)}, u32[]{:S(2)}) async-start(bf16[4,3,96,256]{3,2,1,0:T(8,128)(2,1)} %attend_forward.1), calls=%async_computation.1 | async-start | bytes 1179648 | tf_op jit(solution)/shard_map/all_to_all | solution.py:643
  221.4 9.3 %collective-permute-start.36 = (bf16[384,7040]{1,0:T(8,128)(2,1)}, bf16[384,7040]{1,0:T(8,128)(2,1)}, u32[]{:S(2)}, u32[]{:S(2)}) collective-permute-start(bf16[384,7040]{1,0:T(8,128)(2,1)} %get-tuple-element.72), channel_id=1, source_target_pairs={{0,1},{1,0},{2,3},{3,2},{4,5},{5,4},{6,7},{7,6},{8,9},{9,8},{10,11... | collective-permute-start | bytes 16220168 | tf_op jit(solution)/shard_map/ppermute | solution.py:532
  221.5 15.2 %all-to-all-start.2 = ((bf16[4,3,96,256]{3,2,1,0:T(8,128)(2,1)}), bf16[4,3,96,256]{3,2,1,0:T(8,128)(2,1)S(1)}, u32[]{:S(2)}, u32[]{:S(2)}) async-start(bf16[4,3,96,256]{3,2,1,0:T(8,128)(2,1)} %bitcast.135), calls=%async_computation.2 | async-start | bytes 1179648 | tf_op jit(solution)/shard_map/all_to_all | solution.py:662
  236.7 33.4 %collective-permute-start.39 = (bf16[192,7040]{1,0:T(8,128)(2,1)}, bf16[192,7040]{1,0:T(8,128)(2,1)}, u32[]{:S(2)}, u32[]{:S(2)}) collective-permute-start(bf16[192,7040]{1,0:T(8,128)(2,1)} %get-tuple-element.77), channel_id=1, source_target_pairs={{0,16},{1,3},{2,18},{3,1},{16,0},{17,19},{18,2},{19,17},{4,20},{5,... | collective-permute-start | bytes 8110088 | tf_op jit(solution)/shard_map/ppermute | solution.py:543
  239.4 13.5 %collective-permute-start.35 = (bf16[4,3,96,256]{3,2,1,0:T(8,128)(2,1)S(1)}, bf16[4,3,96,256]{3,2,1,0:T(8,128)(2,1)}, u32[]{:S(2)}, u32[]{:S(2)}) collective-permute-start(bf16[4,3,96,256]{3,2,1,0:T(8,128)(2,1)S(1)} %all-to-all-done.2.load_ref), channel_id=1, source_target_pairs={{0,4},{4,8},{8,12},{12,0},{1,5},{5,9},{9,13},{13,1},{2,6},{6,10},{... | collective-permute-start | bytes 1769480 | tf_op jit(solution)/shard_map/ppermute | solution.py:674
  267.1 16.0 %collective-permute-start.37 = (bf16[4,3,96,256]{3,2,1,0:T(8,128)(2,1)}, bf16[4,3,96,256]{3,2,1,0:T(8,128)(2,1)S(1)}, u32[]{:S(2)}, u32[]{:S(2)}) collective-permute-start(bf16[4,3,96,256]{3,2,1,0:T(8,128)(2,1)} %collective-permute-done.35.load_ref), channel_id=1, source_target_pairs={{0,4},{4,8},{8,12},{12,0},{1,5},{5,9},{9,13},{13,1},{2,6},{6,10},{... | collective-permute-start | bytes 1769480 | tf_op jit(solution)/shard_map/ppermute | solution.py:674
  272.8 42.0 %collective-permute-start.43 = (bf16[96,7040]{1,0:T(8,128)(2,1)}, bf16[96,7040]{1,0:T(8,128)(2,1)}, u32[]{:S(2)}, u32[]{:S(2)}) collective-permute-start(bf16[96,7040]{1,0:T(8,128)(2,1)} %add_convert_fusion.5), channel_id=1, source_target_pairs={{0,2},{1,17},{2,0},{3,19},{16,18},{17,1},{18,16},{19,3},{4,6},{5,2... | collective-permute-start | bytes 4055048 | tf_op jit(solution)/shard_map/ppermute | solution.py:543
  283.2 15.3 %collective-permute-start.38 = (bf16[4,3,96,256]{3,2,1,0:T(8,128)(2,1)S(1)}, bf16[4,3,96,256]{3,2,1,0:T(8,128)(2,1)}, u32[]{:S(2)}, u32[]{:S(2)}) collective-permute-start(bf16[4,3,96,256]{3,2,1,0:T(8,128)(2,1)S(1)} %collective-permute-done.37.load_ref), channel_id=1, source_target_pairs={{0,4},{4,8},{8,12},{12,0},{1,5},{5,9},{9,13},{13,1},{2,6},{6,10},{... | collective-permute-start | bytes 1769480 | tf_op jit(solution)/shard_map/ppermute | solution.py:674
  314.7 9.2 %collective-permute-start.40 = (bf16[2,2,288,768]{3,2,1,0:T(8,128)(2,1)}, bf16[2,2,288,768]{3,2,1,0:T(8,128)(2,1)S(1)}, u32[]{:S(2)}, u32[]{:S(2)}) collective-permute-start(bf16[2,2,288,768]{3,2,1,0:T(8,128)(2,1)} %get-tuple-element.80), channel_id=1, source_target_pairs={{0,1},{1,0},{2,3},{3,2},{4,5},{5,4},{6,7},{7,6},{8,9},{9,8},{10,11... | collective-permute-start | bytes 5308424 | tf_op jit(solution)/shard_map/ppermute | solution.py:532
  318.0 14.8 %collective-permute-start.44 = (bf16[24,7040]{1,0:T(8,128)(2,1)}, bf16[24,7040]{1,0:T(8,128)(2,1)S(1)}, u32[]{:S(2)}, u32[]{:S(2)}) collective-permute-start(bf16[24,7040]{1,0:T(8,128)(2,1)} %get-tuple-element.148), channel_id=1, source_target_pairs={{0,4},{4,8},{8,12},{12,0},{1,5},{5,9},{9,13},{13,1},{2,6},{6,10},{... | collective-permute-start | bytes 1013768 | tf_op jit(solution)/shard_map/ppermute | solution.py:690
  319.3 40.6 %collective-permute-start.45 = (bf16[24,7040]{1,0:T(8,128)(2,1)S(1)}, bf16[24,7040]{1,0:T(8,128)(2,1)S(1)}, u32[]{:S(2)}, u32[]{:S(2)}) collective-permute-start(bf16[24,7040]{1,0:T(8,128)(2,1)S(1)} %get-tuple-element.150), channel_id=1, source_target_pairs={{0,8},{4,12},{8,0},{12,4},{1,9},{5,13},{9,1},{13,5},{2,10},{6,14},... | collective-permute-start | bytes 1013768 | tf_op jit(solution)/shard_map/ppermute | solution.py:690
  323.9 40.2 %collective-permute-start.46 = (bf16[24,7040]{1,0:T(8,128)(2,1)S(1)}, bf16[24,7040]{1,0:T(8,128)(2,1)S(1)}, u32[]{:S(2)}, u32[]{:S(2)}) collective-permute-start(bf16[24,7040]{1,0:T(8,128)(2,1)S(1)} %get-tuple-element.149), channel_id=1, source_target_pairs={{0,12},{4,0},{8,4},{12,8},{1,13},{5,1},{9,5},{13,9},{2,14},{6,2},{... | collective-permute-start | bytes 1013768 | tf_op jit(solution)/shard_map/ppermute | solution.py:690
  324.4 63.7 %all-to-all-start.3 = ((bf16[32,24,640]{2,1,0:T(8,128)(2,1)}), bf16[32,24,640]{2,1,0:T(8,128)(2,1)}, u32[]{:S(2)}, u32[]{:S(2)}) async-start(bf16[32,24,640]{2,1,0:T(8,128)(2,1)} %bitcast.44), calls=%async_computation.3 | async-start | bytes 1966080 | tf_op jit(solution)/shard_map/all_to_all | solution.py:702
  331.2 34.1 %collective-permute-start.41 = (bf16[2,288,768]{2,1,0:T(8,128)(2,1)S(1)}, bf16[2,288,768]{2,1,0:T(8,128)(2,1)S(1)}, u32[]{:S(2)}, u32[]{:S(2)}) collective-permute-start(bf16[2,288,768]{2,1,0:T(8,128)(2,1)S(1)} %slice_bitcast_fusion), channel_id=1, source_target_pairs={{0,16},{1,3},{2,18},{3,1},{16,0},{17,19},{18,2},{19,17},{4,20},{5,... | collective-permute-start | bytes 2654216 | tf_op jit(solution)/shard_map/ppermute | solution.py:543
  366.3 19.8 %collective-permute-start.42 = (bf16[288,768]{1,0:T(8,128)(2,1)}, bf16[288,768]{1,0:T(8,128)(2,1)}, u32[]{:S(2)}, u32[]{:S(2)}) collective-permute-start(bf16[288,768]{1,0:T(8,128)(2,1)} %fusion), channel_id=1, source_target_pairs={{0,2},{1,17},{2,0},{3,19},{16,18},{17,1},{18,16},{19,3},{4,6},{5,2... | collective-permute-start | bytes 1327112 | tf_op jit(solution)/shard_map/ppermute | solution.py:543
  (44 other events, 415.5 us)
Sparse Core Ops, SparseCore 0:
  13.9 123.0 all-gather.1

commit v3 on v2

--- a/solution.py
+++ b/solution.py
@@ -497,6 +497,54 @@
     )(spot, dq, dkv, weight, *pieces)
 
 
+def finish_kernel(fold, *refs):
+    blocks, (in_ref, down_ref, out_ref, note_ref) = refs[:-4], refs[-4:]
+    part, width = out_ref.shape
+    hidden = fold * width
+    piece = width // fold
+
+    def total(at, size):
+        value = blocks[0][:, at : at + size].astype(F32)
+        for block in blocks[1:]:
+            value = value + block[:, at : at + size].astype(F32)
+        return value
+
+    row = lax.broadcasted_iota(jnp.int32, (piece, width), 0)
+    for k in range(fold):
+        target = row // part * (fold * part) + k * part + row % part
+        move = (lanes_like((piece, width)) == target).astype(F32).astype(BF)
+        value = total(k * width, width)
+        high = value.astype(BF)
+        rest = (value - high.astype(F32)).astype(BF)
+        for o in range(fold):
+            cols = slice(o * piece, (o + 1) * piece)
+            placed = dot_nn(high[:, cols], move) + dot_nn(rest[:, cols], move)
+            to = slice(o * width, (o + 1) * width)
+            in_ref[:, to] = placed if k == 0 else in_ref[:, to] + placed
+        down_ref[k] = total(hidden + k * width, width)
+    out_ref[...] = total(2 * hidden, width)
+    note_ref[...] = total(2 * hidden + width, 128)
+
+
+def finish(blocks, fold, width):
+    part = blocks[0].shape[0]
+    local = pl.BlockSpec(memory_space=pltpu.VMEM)
+    return pl.pallas_call(
+        functools.partial(finish_kernel, fold),
+        in_specs=[local] * len(blocks),
+        out_specs=[local] * 4,
+        out_shape=[
+            jax.ShapeDtypeStruct((part, fold * width), F32),
+            jax.ShapeDtypeStruct((fold, part, width), F32),
+            jax.ShapeDtypeStruct((part, width), F32),
+            jax.ShapeDtypeStruct((part, 128), F32),
+        ],
+        compiler_params=pltpu.CompilerParams(vmem_limit_bytes=VMEM_LIMIT),
+        cost_estimate=pl.CostEstimate(flops=1 << 27, bytes_accessed=2 << 20, transcendentals=0),
+        name="finish",
+    )(*blocks)
+
+
 def assemble_kernel(got_ref, grad_ref, note_ref):
     width = grad_ref.shape[1] // 3
     for t in range(TP):
@@ -579,7 +627,7 @@
     notes = jnp.concatenate(notes + [jnp.zeros((part, 128 - 6 - fold), BF)], axis=1)
     wi_turned = wi.reshape(part, devices, fold, part).transpose(0, 2, 1, 3).reshape(part, hidden)
     wd_cols = [wd[k * part : (k + 1) * part] for k in range(fold)]
-    dense = lax.all_gather(jnp.concatenate([wo, wi_turned] + wd_cols + [notes], axis=1), ALL, axis=0, tiled=True)
+    dense_own = jnp.concatenate([wo, wi_turned] + wd_cols + [notes], axis=1)
 
     by_head = wqkv.reshape(part, 3, TP, HG, HD)
     blocks_kv = by_head[:, 1:].transpose(2, 0, 3, 1, 4).reshape(TP, part, HG * 128)
@@ -591,6 +639,9 @@
     for k in range(1, ring):
         got = lax.ppermute(blocks, "r", [(i, (i + k) % ring) for i in range(ring)])
         column = put(column, got, (me_r - k) % ring)
+    early = (cross_one(layer_input.reshape(tokens, width)), cross_two(layer_input.reshape(tokens, width)))
+    column = after(column, *early)
+    dense = lax.all_gather(after(dense_own, column), ALL, axis=0, tiled=True)
     both = jnp.zeros((2,) + column.shape, BF)
     w_here = put(put(both, column, me_u), swap_u(column), 1 - me_u).reshape(width, 640)
     b_heads = w_here[:, 576:578].astype(F32)
@@ -609,8 +660,7 @@
             piece = lax.ppermute(piece, "r", forward)
         if k >= 2:
             piece, stages[k - 2] = lax.optimization_barrier((piece, stages[k - 2]))
-        one = cross_one(piece)
-        two = cross_two(piece)
+        one, two = early if k == 0 else (cross_one(piece), cross_two(piece))
         if k == 1:
             one, w_here = lax.optimization_barrier((one, w_here))
         three = cross_two(one)
@@ -688,20 +738,19 @@
     for j in range(1, ring):
         along = [(i, (i + j) % ring) for i in range(ring)]
         summed = summed + lax.ppermute(stay[j * part : (j + 1) * part], "r", along).astype(F32)
-    grad_w_in = summed[:, :hidden].reshape(part, fold, devices, part).transpose(0, 2, 1, 3).reshape(part, hidden)
-    grad_w_down = jnp.concatenate([summed[:, hidden + k * width : hidden + (k + 1) * width] for k in range(fold)], axis=0)
-    grad_w_out = summed[:, 2 * hidden : 2 * hidden + width]
-    flat = summed[:, 2 * hidden + width : 2 * hidden + width + 6 + fold].T
-    grad_bo, grad_gains, grad_shifts, grad_bin = flat[0:2], flat[2:4], flat[4:6], flat[6:].reshape(-1)
-
-
     spot = jnp.concatenate([jnp.stack([me_u, me_y, me_c]), (pair == me_u).astype(jnp.int32)])
     keep, send, dw = tail(spot.astype(jnp.int32), dq, done[-1], w_here, x_near[0] + x_near[1], part)
     keep = add(keep, swap_c(send))
     dw = after(dw, keep)
     got = lax.all_to_all(dw.reshape(devices, part, 640), ALL, split_axis=0, concat_axis=0, tiled=True)
     came = cross_one(keep[1])
-    final = cross_two(add(keep[0, 1], came[1]))
+    onward = add(keep[0, 1], came[1])
+    final = cross_two(onward)
+    grad_w_in, grad_w_down, grad_w_out, flat = finish([after(summed, onward)], fold, width)
+    grad_w_down = grad_w_down.reshape(fold * part, width)
+    flat = flat[:, : 6 + fold].T
+    grad_bo, grad_gains, grad_shifts, grad_bin = flat[0:2], flat[2:4], flat[4:6], flat[6:].reshape(-1)
+
     grad_input = dsum + keep[0, 0].astype(F32) + came[0].astype(F32) + final.astype(F32)
     grad_input = grad_input.astype(BF).reshape(seqs, rows, width)
     grad_w_qkv, note = assemble(after(got, final).reshape(2 * ring, TP, part, 640))

time: 407 us -> 385 us (0.946)
  waiting for transfers between devices: 124 us -> 112 us
  local copies, waits for them, and re-layouts: 39.1 us -> 27.6 us
    ppermute x3, waiting for transfers between devices: 34.6 us -> 7.48 us  [per_device(): piece = lax.ppermute(piece, 'r', forward)]
    ppermute x16, waiting for transfers between devices: 13.2 us -> 33.9 us  [crossing(): return lambda v: lax.ppermute(v, ('u', 'y', 'c'), pairs)]
    ppermute x3, waiting for transfers between devices: 16 us -> 9.66 us  [per_device(): got = lax.ppermute(blocks, 'r', [(i, (i + k) % ring) for i in range(ring)])]
    reshape x2 -> x0, local copies, waits for them, and re-layouts: 6.2 us -> none  [per_device(): summed[:, :hidden].reshape(part, fold, devices, part).transpose(0, 2, 1, 3)]
    ppermute x3, waiting for transfers between devices: 6.59 us -> 12.6 us  [per_device(): moving = lax.ppermute(moving, 'r', forward)]
  transfers between devices with their start and end apart: 52 -> 52, of which waited for: 17 -> 20; matrix products, arithmetic and copies ran while one was open for 15% -> 14% of each run, Pallas kernels for 22% -> 25%
where the time goes in v3:
time: 385 us; the launch traced here: 378 us
  Pallas kernels  120 us (31%)
  waiting for transfers between devices  112 us (29%)
  starting transfers between devices  73 us (19%)
  other arithmetic  30.7 us (8%)
  local copies, waits for them, and re-layouts  27.6 us (7%)
  between operations  15.1 us (4%)
    ppermute x16, waiting for transfers between devices, crossing(): return lambda v: lax.ppermute(v, ('u', 'y', 'c'), pairs)  33.9 us
    ppermute x3, waiting for transfers between devices, per_device(): lax.ppermute(stay[j * part:(j + 1) * part], 'r', along).astype(F32)  31.7 us
    pallas_call x4, Pallas kernels, attend_key(): pl.pallas_call(functools.partial(key_kernel, rows), grid_spec=pltpu.Prefe...  28.9 us
    pallas_call x1, Pallas kernels, dense_layers(): pl.pallas_call(functools.partial(dense_kernel, fold), in_specs=[local, lo...  25.2 us
    pallas_call x4, Pallas kernels, project(): pl.pallas_call(functools.partial(project_kernel, seqs, rows, not extra),...  22.9 us
    ppermute x19, starting transfers between devices, swap_on(): return lambda v: lax.ppermute(v, axis, [(0, 1), (1, 0)])  18.5 us
    ppermute x16, starting transfers between devices, crossing(): return lambda v: lax.ppermute(v, ('u', 'y', 'c'), pairs)  18.5 us
    pallas_call x1, Pallas kernels, attend_query(): pl.pallas_call(functools.partial(query_kernel, rows, shards), grid_spec=p...  14.2 us
  transfers between devices with their start and end apart: 52, of which 20 were waited for; matrix products, arithmetic and copies ran while one was open for 14% of the time, Pallas kernels for 25%

profile of v3, /device:TPU:8, one launch (start us, length us, event | category | flops | bytes accessed | tf_op | source)
XLA Modules:
  0.0 378.1 jit_solution(1135817666070871061)
XLA Ops:
  13.6 3.3 all-to-all-start
  26.6 5.7 %collective-permute-done = bf16[4,24,640]{2,1,0:T(8,128)(2,1)S(1)} collective-permute-done((bf16[4,24,640]{2,1,0:T(8,128)(2,1)S(1)}, bf16[4,24,640]{2,1,0:T(8,128)(2,1)S(1)}, u32[]{:S(2)}, u32[]{:S(2)}) %collective-permute-start) | collective-permute-done | bytes 122912 | tf_op jit(solution)/shard_map/ppermute | solution.py:640
  32.2 2.3 collective-permute-done.1
  40.2 5.9 %collective-permute-done.7.refs_3_ = bf16[288,768]{1,0:T(8,128)(2,1)} collective-permute-done((bf16[288,768]{1,0:T(8,128)(2,1)S(1)}, bf16[288,768]{1,0:T(8,128)(2,1)}, u32[]{:S(2)}, u32[]{:S(2)}) %collective-permute-start.7) | collective-permute-done | bytes 442400 | tf_op jit(solution)/shard_map/ppermute | solution.py:591
  46.1 11.4 %collective-permute-start.10 = (bf16[288,768]{1,0:T(8,128)(2,1)S(1)}, bf16[288,768]{1,0:T(8,128)(2,1)}, u32[]{:S(2)}, u32[]{:S(2)}) collective-permute-start(bf16[288,768]{1,0:T(8,128)(2,1)S(1)} %collective-permute-done.4.refs_2_), channel_id=1, source_target_pairs={{0,1},{1,0},{2,3},{3,2},{4,5},{5,4},{6,7},{7,6},{8,9},{9,8},{10,11... | collective-permute-start | bytes 1327112 | tf_op jit(solution)/shard_map/ppermute | solution.py:580
  61.2 5.7 %project.4 = (bf16[2,4,4,3,96,384]{5,4,3,2,1,0:T(8,128)(2,1)}, bf16[4,4,3,96,384]{4,3,2,1,0:T(8,128)(2,1)}) custom-call(s32[4]{0:T(128)} %get-tuple-element.188.spot_ref, bf16[288,768]{1,0:T(8,128)(2,1)} %bitcast.140, bf16[288,768]{1,0:T(8,128)(2,1)} %copy-done.8, bf16[288,768]{1,0:T(8,128)(2,1)} %copy-done.9, ...), custom_call_target="tpu_custom_call" | custom-call | flops 2038431744 | bytes 12582912 | tf_op jit(solution)/shard_map/project/pallas_call | solution.py:204
  66.9 7.5 %collective-permute-done.6.refs_0_ = bf16[288,768]{1,0:T(8,128)(2,1)S(1)} collective-permute-done((bf16[288,768]{1,0:T(8,128)(2,1)}, bf16[288,768]{1,0:T(8,128)(2,1)S(1)}, u32[]{:S(2)}, u32[]{:S(2)}) %collective-permute-start.6) | collective-permute-done | bytes 442400 | tf_op jit(solution)/shard_map/ppermute | solution.py:660
  77.1 2.8 collective-permute-start.13
  80.0 5.4 %collective-permute-done.18.refs_3_ = bf16[288,768]{1,0:T(8,128)(2,1)S(1)} collective-permute-done((bf16[288,768]{1,0:T(8,128)(2,1)}, bf16[288,768]{1,0:T(8,128)(2,1)S(1)}, u32[]{:S(2)}, u32[]{:S(2)}) %collective-permute-start.18) | collective-permute-done | bytes 442400 | tf_op jit(solution)/shard_map/ppermute | solution.py:591
  85.4 3.8 collective-permute-start.22
  91.9 7.8 %convert_reduce_fusion = s32[3,2,1536]{2,1,0:T(2,128)S(1)} fusion(s32[3,1536]{1,0:T(4,128)S(1)} %bitcast.150, s32[3,2,1536]{2,1,0:T(2,128)S(1)} %le.17), kind=kLoop, calls=%fused_computation | loop fusion | flops 42458112 | bytes 92160 | tf_op jit(solution)/shard_map/reduce_sum | solution.py:683
  100.5 5.7 %project.5 = (bf16[2,4,4,3,96,384]{5,4,3,2,1,0:T(8,128)(2,1)}, bf16[4,4,3,96,384]{4,3,2,1,0:T(8,128)(2,1)}) custom-call(s32[4]{0:T(128)} %get-tuple-element.187.spot_ref, bf16[288,768]{1,0:T(8,128)(2,1)} %collective-permute-done.5.refs_0_, bf16[288,768]{1,0:T(8,128)(2,1)} %collective-permute-done.16.refs_1_, ...), custom_call_target="tpu_custom_call", output_to_operand_aliasing={{0}: (11, {}), {1}: (12, {})} | custom-call | flops 2038431744 | bytes 12582912 | tf_op jit(solution)/shard_map/project/pallas_call | solution.py:204
  108.2 7.3 %collective-permute-done.26.refs_2_ = bf16[288,768]{1,0:T(8,128)(2,1)} collective-permute-done((bf16[288,768]{1,0:T(8,128)(2,1)S(1)}, bf16[288,768]{1,0:T(8,128)(2,1)}, u32[]{:S(2)}, u32[]{:S(2)}) %collective-permute-start.26) | collective-permute-done | bytes 442400 | tf_op jit(solution)/shard_map/ppermute | solution.py:591
  116.9 9.1 %collective-permute-done.23.refs_1_ = bf16[288,768]{1,0:T(8,128)(2,1)S(1)} collective-permute-done((bf16[288,768]{1,0:T(8,128)(2,1)S(1)}, bf16[288,768]{1,0:T(8,128)(2,1)S(1)}, u32[]{:S(2)}, u32[]{:S(2)}) %collective-permute-start.23) | collective-permute-done | bytes 442400 | tf_op jit(solution)/shard_map/ppermute | solution.py:591
  126.0 2.2 collective-permute-start.25
  131.3 4.0 %collective-permute-done.24.refs_2_ = bf16[288,768]{1,0:T(8,128)(2,1)} collective-permute-done((bf16[288,768]{1,0:T(8,128)(2,1)S(1)}, bf16[288,768]{1,0:T(8,128)(2,1)}, u32[]{:S(2)}, u32[]{:S(2)}) %collective-permute-start.24) | collective-permute-done | bytes 442400 | tf_op jit(solution)/shard_map/ppermute | solution.py:591
  135.3 5.7 %project.6 = (bf16[2,4,4,3,96,384]{5,4,3,2,1,0:T(8,128)(2,1)}, bf16[4,4,3,96,384]{4,3,2,1,0:T(8,128)(2,1)}) custom-call(s32[4]{0:T(128)} %get-tuple-element.158.spot_ref, bf16[288,768]{1,0:T(8,128)(2,1)} %copy-done.10, bf16[288,768]{1,0:T(8,128)(2,1)} %copy-done.12, ...), custom_call_target="tpu_custom_call", output_to_operand_aliasing={{0}: (11, {}), {1}: (12, {})} | custom-call | flops 2038431744 | bytes 12582912 | tf_op jit(solution)/shard_map/project/pallas_call | solution.py:204
  144.5 5.7 %project.7 = (bf16[2,4,4,3,96,384]{5,4,3,2,1,0:T(8,128)(2,1)}, bf16[4,4,3,96,384]{4,3,2,1,0:T(8,128)(2,1)}) custom-call(s32[4]{0:T(128)} %get-tuple-element.189.spot_ref, bf16[288,768]{1,0:T(8,128)(2,1)} %copy-done.11, bf16[288,768]{1,0:T(8,128)(2,1)} %copy-done.14, ...), custom_call_target="tpu_custom_call", output_to_operand_aliasing={{0}: (11, {}), {1}: (12, {})} | custom-call | flops 2038431744 | bytes 12582912 | tf_op jit(solution)/shard_map/project/pallas_call | solution.py:204
  150.3 2.2 constant_dynamic-slice_fusion.5.q_ref
  152.4 13.8 %attend_forward.1 = bf16[4,3,96,256]{3,2,1,0:T(8,128)(2,1)} custom-call(s32[3]{0:T(128)} %copy-done.29, s32[9]{0:T(128)} %max.8.begin_ref, s32[9]{0:T(128)} %reshape_squeeze.18.last_ref, bf16[4,3,96,384]{3,2,1,0:T(8,128)(2,1)} %constant_dynamic-slice_fusion.5.q_ref, bf16[2,16,3,96,384]{4,3,2,1,0:T(8,128)(2,1)} %bitcast.102, ...), custom_call_target="tpu_custom_call" | custom-call | flops 2717908992 | bytes 12582912 | tf_op jit(solution)/shard_map/attend_forward/pallas_call | solution.py:234
  166.3 3.6 all-to-all-start.1
  170.0 9.3 %all-to-all-done.1 = bf16[4,3,96,256]{3,2,1,0:T(8,128)(2,1)S(1)} async-done(((bf16[4,3,96,256]{3,2,1,0:T(8,128)(2,1)}), bf16[4,3,96,256]{3,2,1,0:T(8,128)(2,1)S(1)}, u32[]{:S(2)}, u32[]{:S(2)}) %all-to-all-start.1) | async-done | bytes 589856 | tf_op jit(solution)/shard_map/all_to_all | solution.py:693
  180.1 25.2 %dense_layers.1 = (bf16[288,768]{1,0:T(8,128)(2,1)}, bf16[4,288,256]{2,1,0:T(8,128)(2,1)}, f32[288,768]{1,0:T(8,128)}, bf16[384,7040]{1,0:T(8,128)(2,1)}, bf16[384,7040]{1,0:T(8,128)(2,1)}) custom-call(bf16[4,288,256]{2,1,0:T(8,128)(2,1)} %bitcast.137, bf16[288,768]{1,0:T(8,128)(2,1)} %bitcast.141, bf16[288,768]{1,0:T(8,128)(2,1)} %bitcast.151, ...), custom_call_target="tpu_custom_call" | custom-call | flops 9172942848 | bytes 25165824 | tf_op jit(solution)/shard_map/dense_layers/pallas_call | solution.py:409
  205.4 3.5 all-to-all-start.2
  208.9 5.7 %collective-permute-done.36 = bf16[384,7040]{1,0:T(8,128)(2,1)} collective-permute-done((bf16[384,7040]{1,0:T(8,128)(2,1)}, bf16[384,7040]{1,0:T(8,128)(2,1)}, u32[]{:S(2)}, u32[]{:S(2)}) %collective-permute-start.36) | collective-permute-done | bytes 5406752 | tf_op jit(solution)/shard_map/ppermute | solution.py:580
  214.6 5.9 %add_convert_fusion = (bf16[192,7040]{1,0:T(8,128)(2,1)S(1)}, bf16[192,7040]{1,0:T(8,128)(2,1)}) fusion(bf16[384,7040]{1,0:T(8,128)(2,1)} %collective-permute-done.36, bf16[384,7040]{1,0:T(8,128)(2,1)} %get-tuple-element.80), kind=kLoop, calls=%fused_computation.1 | loop fusion | flops 10813440 | bytes 16220160 | tf_op jit(solution)/shard_map/convert_element_type | solution.py:599
  221.5 2.7 collective-permute-start.35
  227.7 7.2 %attend_key.4.old_ref = f32[4,3,96,384]{3,2,1,0:T(8,128)} custom-call(s32[3]{0:T(128)} %copy-done.29, s32[9]{0:T(128)} %max.8.begin_ref, s32[9]{0:T(128)} %reshape_squeeze.20.reach_ref, s32[3]{0:T(128)} %get-tuple-element.186.place_ref, bf16[16,3,96,384]{3,2,1,0:T(8,128)(2,1)} %bitcast.121, ...), custom_call_target="tpu_custom_call", output_to_operand_aliasing={{}: (10, {})} | custom-call | flops 1358954496 | bytes 8388608 | tf_op jit(solution)/shard_map/attend_key/pallas_call | solution.py:280
  234.9 3.1 collective-permute-done.35.load_ref
  238.0 14.2 %attend_query.1.dq_ref = bf16[4,3,96,192]{3,2,1,0:T(8,128)(2,1)} custom-call(s32[3]{0:T(128)} %copy-done.29, s32[9]{0:T(128)} %max.8.begin_ref, s32[9]{0:T(128)} %reshape_squeeze.18.last_ref, bf16[4,3,96,384]{3,2,1,0:T(8,128)(2,1)} %constant_dynamic-slice_fusion.5.q_ref, bf16[2,16,3,96,384]{4,3,2,1,0:T(8,128)(2,1)} %bitcast.108, ...), custom_call_target="tpu_custom_call" | custom-call | flops 4076863488 | bytes 12582912 | tf_op jit(solution)/shard_map/attend_query/pallas_call | solution.py:255
  252.3 2.1 collective-permute-start.37
  254.4 2.7 add_convert_fusion.5
  258.7 7.2 %attend_key.5.old_ref = f32[4,3,96,384]{3,2,1,0:T(8,128)} custom-call(s32[3]{0:T(128)} %copy-done.29, s32[9]{0:T(128)} %max.8.begin_ref, s32[9]{0:T(128)} %reshape_squeeze.22.reach_ref, s32[3]{0:T(128)} %get-tuple-element.184.place_ref, bf16[16,3,96,384]{3,2,1,0:T(8,128)(2,1)} %bitcast.122, ...), custom_call_target="tpu_custom_call", output_to_operand_aliasing={{}: (10, {})} | custom-call | flops 1358954496 | bytes 8388608 | tf_op jit(solution)/shard_map/attend_key/pallas_call | solution.py:280
  265.9 3.4 collective-permute-done.37.load_ref
  271.5 7.2 %attend_key.6.old_ref = f32[4,3,96,384]{3,2,1,0:T(8,128)} custom-call(s32[3]{0:T(128)} %copy-done.29, s32[9]{0:T(128)} %max.8.begin_ref, s32[9]{0:T(128)} %reshape_squeeze.23.reach_ref, s32[3]{0:T(128)} %get-tuple-element.154.place_ref, bf16[16,3,96,384]{3,2,1,0:T(8,128)(2,1)} %bitcast.123, ...), custom_call_target="tpu_custom_call", output_to_operand_aliasing={{}: (10, {})} | custom-call | flops 1358954496 | bytes 8388608 | tf_op jit(solution)/shard_map/attend_key/pallas_call | solution.py:280
  278.7 6.1 %collective-permute-done.38.load_ref = bf16[4,3,96,256]{3,2,1,0:T(8,128)(2,1)} collective-permute-done((bf16[4,3,96,256]{3,2,1,0:T(8,128)(2,1)S(1)}, bf16[4,3,96,256]{3,2,1,0:T(8,128)(2,1)}, u32[]{:S(2)}, u32[]{:S(2)}) %collective-permute-start.38) | collective-permute-done | bytes 589856 | tf_op jit(solution)/shard_map/ppermute | solution.py:724
  284.9 7.2 %attend_key.7.dkv_ref = f32[4,3,96,384]{3,2,1,0:T(8,128)} custom-call(s32[3]{0:T(128)} %copy-done.29, s32[9]{0:T(128)} %max.8.begin_ref, s32[9]{0:T(128)} %reshape_squeeze.21.reach_ref, s32[3]{0:T(128)} %get-tuple-element.185.place_ref, bf16[16,3,96,384]{3,2,1,0:T(8,128)(2,1)} %bitcast.124, ...), custom_call_target="tpu_custom_call", output_to_operand_aliasing={{}: (10, {})} | custom-call | flops 1358954496 | bytes 8388608 | tf_op jit(solution)/shard_map/attend_key/pallas_call | solution.py:280
  292.1 9.0 %tail.1 = (bf16[2,2,288,768]{3,2,1,0:T(8,128)(2,1)}, bf16[2,2,288,768]{3,2,1,0:T(8,128)(2,1)}, bf16[768,640]{1,0:T(8,128)(2,1)}) custom-call(s32[6]{0:T(128)} %pad_add_fusion.5.spot_ref, bf16[4,3,96,192]{3,2,1,0:T(8,128)(2,1)} %attend_query.1.dq_ref, f32[4,3,96,384]{3,2,1,0:T(8,128)} %attend_key.7.dkv_ref, bf16[768,640]{1,0:T(8,128)(2,1)} %bitcast.130, ...), custom_call_target="tpu_custom_call" | custom-call | flops 1698693120 | bytes 16777216 | tf_op jit(solution)/shard_map/tail/pallas_call | solution.py:485
  301.1 2.3 add_convert_fusion.3
  304.6 5.9 %collective-permute-start.45 = (bf16[24,7040]{1,0:T(8,128)(2,1)}, bf16[24,7040]{1,0:T(8,128)(2,1)}, u32[]{:S(2)}, u32[]{:S(2)}) collective-permute-start(bf16[24,7040]{1,0:T(8,128)(2,1)} %get-tuple-element.164), channel_id=1, source_target_pairs={{0,8},{4,12},{8,0},{12,4},{1,9},{5,13},{9,1},{13,5},{2,10},{6,14},... | collective-permute-start | bytes 1013768 | tf_op jit(solution)/shard_map/ppermute | solution.py:740
  311.9 7.3 %all-to-all-start.3 = ((bf16[32,24,640]{2,1,0:T(8,128)(2,1)}), bf16[32,24,640]{2,1,0:T(8,128)(2,1)S(1)}, u32[]{:S(2)}, u32[]{:S(2)}) async-start(bf16[32,24,640]{2,1,0:T(8,128)(2,1)} %bitcast.135), calls=%async_computation.3 | async-start | bytes 1966080 | tf_op jit(solution)/shard_map/all_to_all | solution.py:745
  319.3 23.9 %collective-permute-done.45 = bf16[24,7040]{1,0:T(8,128)(2,1)} collective-permute-done((bf16[24,7040]{1,0:T(8,128)(2,1)}, bf16[24,7040]{1,0:T(8,128)(2,1)}, u32[]{:S(2)}, u32[]{:S(2)}) %collective-permute-start.45) | collective-permute-done | bytes 337952 | tf_op jit(solution)/shard_map/ppermute | solution.py:740
  343.2 7.8 %collective-permute-done.46 = bf16[24,7040]{1,0:T(8,128)(2,1)} collective-permute-done((bf16[24,7040]{1,0:T(8,128)(2,1)S(1)}, bf16[24,7040]{1,0:T(8,128)(2,1)}, u32[]{:S(2)}, u32[]{:S(2)}) %collective-permute-start.46) | collective-permute-done | bytes 337952 | tf_op jit(solution)/shard_map/ppermute | solution.py:740
  351.0 2.2 convert_add_fusion.3.refs_0_
  354.3 2.6 collective-permute-start.42
  356.9 3.8 finish.1
  364.0 2.4 fusion.2
  367.3 2.1 assemble.1
  (243 shorter events, 59.8 us)
Async XLA Ops:
  7.2 29.1 %collective-permute-start.3 = (bf16[288,768]{1,0:T(8,128)(2,1)}, bf16[288,768]{1,0:T(8,128)(2,1)S(1)}, u32[]{:S(2)}, u32[]{:S(2)}) collective-permute-start(bf16[288,768]{1,0:T(8,128)(2,1)} %bitcast.138), channel_id=1, source_target_pairs={{0,16},{1,3},{2,18},{3,1},{16,0},{17,19},{18,2},{19,17},{4,20},{5,... | collective-permute-start | bytes 1327112 | tf_op jit(solution)/shard_map/ppermute | solution.py:591
  8.7 27.6 %collective-permute-start.4 = (bf16[288,768]{1,0:T(8,128)(2,1)}, bf16[288,768]{1,0:T(8,128)(2,1)S(1)}, u32[]{:S(2)}, u32[]{:S(2)}) collective-permute-start(bf16[288,768]{1,0:T(8,128)(2,1)} %bitcast.139), channel_id=1, source_target_pairs={{0,2},{1,17},{2,0},{3,19},{16,18},{17,1},{18,16},{19,3},{4,6},{5,2... | collective-permute-start | bytes 1327112 | tf_op jit(solution)/shard_map/ppermute | solution.py:591
  16.9 162.3 %all-gather.2.cloned.1.call-start = ((), (), s32[]{:S(2)}) async-start(), calls=%async_computation.4 | async-start | bytes 11151360 | tf_op jit(solution)/shard_map/all_gather | solution.py:644
  21.9 10.3 %collective-permute-start = (bf16[4,24,640]{2,1,0:T(8,128)(2,1)S(1)}, bf16[4,24,640]{2,1,0:T(8,128)(2,1)S(1)}, u32[]{:S(2)}, u32[]{:S(2)}) collective-permute-start(bf16[4,24,640]{2,1,0:T(8,128)(2,1)S(1)} %all-to-all-done), channel_id=1, source_target_pairs={{0,4},{4,8},{8,12},{12,0},{1,5},{5,9},{9,13},{13,1},{2,6},{6,10},{... | collective-permute-start | bytes 368648 | tf_op jit(solution)/shard_map/ppermute | solution.py:640
  23.5 11.1 %collective-permute-start.1 = (bf16[4,24,640]{2,1,0:T(8,128)(2,1)S(1)}, bf16[4,24,640]{2,1,0:T(8,128)(2,1)S(1)}, u32[]{:S(2)}, u32[]{:S(2)}) collective-permute-start(bf16[4,24,640]{2,1,0:T(8,128)(2,1)S(1)} %all-to-all-done), channel_id=1, source_target_pairs={{0,8},{4,12},{8,0},{12,4},{1,9},{5,13},{9,1},{13,5},{2,10},{6,14},... | collective-permute-start | bytes 368648 | tf_op jit(solution)/shard_map/ppermute | solution.py:640
  24.7 11.6 %collective-permute-start.2 = (bf16[4,24,640]{2,1,0:T(8,128)(2,1)S(1)}, bf16[4,24,640]{2,1,0:T(8,128)(2,1)S(1)}, u32[]{:S(2)}, u32[]{:S(2)}) collective-permute-start(bf16[4,24,640]{2,1,0:T(8,128)(2,1)S(1)} %all-to-all-done), channel_id=1, source_target_pairs={{0,12},{4,0},{8,4},{12,8},{1,13},{5,1},{9,5},{13,9},{2,14},{6,2},{... | collective-permute-start | bytes 368648 | tf_op jit(solution)/shard_map/ppermute | solution.py:640
  36.4 21.4 %collective-permute-start.8 = (bf16[288,768]{1,0:T(8,128)(2,1)S(1)}, bf16[288,768]{1,0:T(8,128)(2,1)}, u32[]{:S(2)}, u32[]{:S(2)}) collective-permute-start(bf16[288,768]{1,0:T(8,128)(2,1)S(1)} %bitcast.143), channel_id=1, source_target_pairs={{0,1},{1,0},{2,3},{3,2},{4,5},{5,4},{6,7},{7,6},{8,9},{9,8},{10,11... | collective-permute-start | bytes 1327112 | tf_op jit(solution)/shard_map/ppermute | solution.py:580
  36.5 21.0 %collective-permute-start.12 = (bf16[4,4,24,640]{3,2,1,0:T(8,128)(2,1)S(1)}, bf16[4,4,24,640]{3,2,1,0:T(8,128)(2,1)S(1)}, u32[]{:S(2)}, u32[]{:S(2)}) collective-permute-start(bf16[4,4,24,640]{3,2,1,0:T(8,128)(2,1)S(1)} %bitcast_dynamic-update-slice_fusion.2), channel_id=1, source_target_pairs={{0,16},{16,0},{1,17},{17,1},{2,18},{18,2},{3,19},{19,3},{4,20},{20... | collective-permute-start | bytes 1474568 | tf_op jit(solution)/shard_map/ppermute | solution.py:580
  37.6 19.8 %collective-permute-start.5 = (bf16[288,768]{1,0:T(8,128)(2,1)S(1)}, bf16[288,768]{1,0:T(8,128)(2,1)}, u32[]{:S(2)}, u32[]{:S(2)}) collective-permute-start(bf16[288,768]{1,0:T(8,128)(2,1)S(1)} %bitcast.144), channel_id=1, source_target_pairs={{0,4},{4,8},{8,12},{12,0},{1,5},{5,9},{9,13},{13,1},{2,6},{6,10},{... | collective-permute-start | bytes 1327112 | tf_op jit(solution)/shard_map/ppermute | solution.py:660
  37.7 8.4 %collective-permute-start.7 = (bf16[288,768]{1,0:T(8,128)(2,1)S(1)}, bf16[288,768]{1,0:T(8,128)(2,1)}, u32[]{:S(2)}, u32[]{:S(2)}) collective-permute-start(bf16[288,768]{1,0:T(8,128)(2,1)S(1)} %collective-permute-done.3.refs_1_), channel_id=1, source_target_pairs={{0,2},{1,17},{2,0},{3,19},{16,18},{17,1},{18,16},{19,3},{4,6},{5,2... | collective-permute-start | bytes 1327112 | tf_op jit(solution)/shard_map/ppermute | solution.py:591
  40.1 18.8 %collective-permute-start.9 = (bf16[288,768]{1,0:T(8,128)(2,1)S(1)}, bf16[288,768]{1,0:T(8,128)(2,1)}, u32[]{:S(2)}, u32[]{:S(2)}) collective-permute-start(bf16[288,768]{1,0:T(8,128)(2,1)S(1)} %collective-permute-done.3.refs_1_), channel_id=1, source_target_pairs={{0,1},{1,0},{2,3},{3,2},{4,5},{5,4},{6,7},{7,6},{8,9},{9,8},{10,11... | collective-permute-start | bytes 1327112 | tf_op jit(solution)/shard_map/ppermute | solution.py:580
  46.1 14.5 %collective-permute-start.10 = (bf16[288,768]{1,0:T(8,128)(2,1)S(1)}, bf16[288,768]{1,0:T(8,128)(2,1)}, u32[]{:S(2)}, u32[]{:S(2)}) collective-permute-start(bf16[288,768]{1,0:T(8,128)(2,1)S(1)} %collective-permute-done.4.refs_2_), channel_id=1, source_target_pairs={{0,1},{1,0},{2,3},{3,2},{4,5},{5,4},{6,7},{7,6},{8,9},{9,8},{10,11... | collective-permute-start | bytes 1327112 | tf_op jit(solution)/shard_map/ppermute | solution.py:580
  57.5 16.9 %collective-permute-start.6 = (bf16[288,768]{1,0:T(8,128)(2,1)}, bf16[288,768]{1,0:T(8,128)(2,1)S(1)}, u32[]{:S(2)}, u32[]{:S(2)}) collective-permute-start(bf16[288,768]{1,0:T(8,128)(2,1)} %collective-permute-done.5.refs_0_), channel_id=1, source_target_pairs={{0,4},{4,8},{8,12},{12,0},{1,5},{5,9},{9,13},{13,1},{2,6},{6,10},{... | collective-permute-start | bytes 1327112 | tf_op jit(solution)/shard_map/ppermute | solution.py:660
  57.8 16.6 %collective-permute-start.16 = (bf16[288,768]{1,0:T(8,128)(2,1)}, bf16[288,768]{1,0:T(8,128)(2,1)}, u32[]{:S(2)}, u32[]{:S(2)}) collective-permute-start(bf16[288,768]{1,0:T(8,128)(2,1)} %collective-permute-done.5.refs_0_), channel_id=1, source_target_pairs={{0,16},{1,3},{2,18},{3,1},{16,0},{17,19},{18,2},{19,17},{4,20},{5,... | collective-permute-start | bytes 1327112 | tf_op jit(solution)/shard_map/ppermute | solution.py:591
  58.9 18.2 %collective-permute-start.17 = (bf16[288,768]{1,0:T(8,128)(2,1)}, bf16[288,768]{1,0:T(8,128)(2,1)}, u32[]{:S(2)}, u32[]{:S(2)}) collective-permute-start(bf16[288,768]{1,0:T(8,128)(2,1)} %collective-permute-done.5.refs_0_), channel_id=1, source_target_pairs={{0,2},{1,17},{2,0},{3,19},{16,18},{17,1},{18,16},{19,3},{4,6},{5,2... | collective-permute-start | bytes 1327112 | tf_op jit(solution)/shard_map/ppermute | solution.py:591
  60.5 19.3 %collective-permute-start.19 = (bf16[288,768]{1,0:T(8,128)(2,1)}, bf16[288,768]{1,0:T(8,128)(2,1)}, u32[]{:S(2)}, u32[]{:S(2)}) collective-permute-start(bf16[288,768]{1,0:T(8,128)(2,1)} %collective-permute-done.5.refs_0_), channel_id=1, source_target_pairs={{0,1},{1,0},{2,3},{3,2},{4,5},{5,4},{6,7},{7,6},{8,9},{9,8},{10,11... | collective-permute-start | bytes 1327112 | tf_op jit(solution)/shard_map/ppermute | solution.py:580
  74.4 11.0 %collective-permute-start.18 = (bf16[288,768]{1,0:T(8,128)(2,1)}, bf16[288,768]{1,0:T(8,128)(2,1)S(1)}, u32[]{:S(2)}, u32[]{:S(2)}) collective-permute-start(bf16[288,768]{1,0:T(8,128)(2,1)} %collective-permute-done.16.refs_1_), channel_id=1, source_target_pairs={{0,2},{1,17},{2,0},{3,19},{16,18},{17,1},{18,16},{19,3},{4,6},{5,2... | collective-permute-start | bytes 1327112 | tf_op jit(solution)/shard_map/ppermute | solution.py:591
  76.4 13.9 %collective-permute-start.14 = (bf16[288,768]{1,0:T(8,128)(2,1)S(1)}, bf16[288,768]{1,0:T(8,128)(2,1)S(1)}, u32[]{:S(2)}, u32[]{:S(2)}) collective-permute-start(bf16[288,768]{1,0:T(8,128)(2,1)S(1)} %collective-permute-done.6.refs_0_), channel_id=1, source_target_pairs={{0,16},{1,3},{2,18},{3,1},{16,0},{17,19},{18,2},{19,17},{4,20},{5,... | collective-permute-start | bytes 1327112 | tf_op jit(solution)/shard_map/ppermute | solution.py:591
  77.0 22.7 %collective-permute-start.20 = (bf16[288,768]{1,0:T(8,128)(2,1)}, bf16[288,768]{1,0:T(8,128)(2,1)S(1)}, u32[]{:S(2)}, u32[]{:S(2)}) collective-permute-start(bf16[288,768]{1,0:T(8,128)(2,1)} %collective-permute-done.16.refs_1_), channel_id=1, source_target_pairs={{0,1},{1,0},{2,3},{3,2},{4,5},{5,4},{6,7},{7,6},{8,9},{9,8},{10,11... | collective-permute-start | bytes 1327112 | tf_op jit(solution)/shard_map/ppermute | solution.py:580
  77.1 29.2 %collective-permute-start.13 = (bf16[288,768]{1,0:T(8,128)(2,1)S(1)}, bf16[288,768]{1,0:T(8,128)(2,1)S(1)}, u32[]{:S(2)}, u32[]{:S(2)}) collective-permute-start(bf16[288,768]{1,0:T(8,128)(2,1)S(1)} %collective-permute-done.6.refs_0_), channel_id=1, source_target_pairs={{0,4},{4,8},{8,12},{12,0},{1,5},{5,9},{9,13},{13,1},{2,6},{6,10},{... | collective-permute-start | bytes 1327112 | tf_op jit(solution)/shard_map/ppermute | solution.py:660
  79.8 20.3 %collective-permute-start.21 = (bf16[288,768]{1,0:T(8,128)(2,1)}, bf16[288,768]{1,0:T(8,128)(2,1)}, u32[]{:S(2)}, u32[]{:S(2)}) collective-permute-start(bf16[288,768]{1,0:T(8,128)(2,1)} %collective-permute-done.17.refs_2_), channel_id=1, source_target_pairs={{0,1},{1,0},{2,3},{3,2},{4,5},{5,4},{6,7},{7,6},{8,9},{9,8},{10,11... | collective-permute-start | bytes 1327112 | tf_op jit(solution)/shard_map/ppermute | solution.py:580
  85.4 14.9 %collective-permute-start.22 = (bf16[288,768]{1,0:T(8,128)(2,1)S(1)}, bf16[288,768]{1,0:T(8,128)(2,1)}, u32[]{:S(2)}, u32[]{:S(2)}) collective-permute-start(bf16[288,768]{1,0:T(8,128)(2,1)S(1)} %collective-permute-done.18.refs_3_), channel_id=1, source_target_pairs={{0,1},{1,0},{2,3},{3,2},{4,5},{5,4},{6,7},{7,6},{8,9},{9,8},{10,11... | collective-permute-start | bytes 1327112 | tf_op jit(solution)/shard_map/ppermute | solution.py:580
  90.2 16.0 %collective-permute-start.15 = (bf16[288,768]{1,0:T(8,128)(2,1)S(1)}, bf16[288,768]{1,0:T(8,128)(2,1)S(1)}, u32[]{:S(2)}, u32[]{:S(2)}) collective-permute-start(bf16[288,768]{1,0:T(8,128)(2,1)S(1)} %collective-permute-done.14.refs_1_), channel_id=1, source_target_pairs={{0,2},{1,17},{2,0},{3,19},{16,18},{17,1},{18,16},{19,3},{4,6},{5,2... | collective-permute-start | bytes 1327112 | tf_op jit(solution)/shard_map/ppermute | solution.py:591
  99.7 15.7 %collective-permute-start.26 = (bf16[288,768]{1,0:T(8,128)(2,1)S(1)}, bf16[288,768]{1,0:T(8,128)(2,1)}, u32[]{:S(2)}, u32[]{:S(2)}) collective-permute-start(bf16[288,768]{1,0:T(8,128)(2,1)S(1)} %collective-permute-done.6.refs_0_), channel_id=1, source_target_pairs={{0,2},{1,17},{2,0},{3,19},{16,18},{17,1},{18,16},{19,3},{4,6},{5,2... | collective-permute-start | bytes 1327112 | tf_op jit(solution)/shard_map/ppermute | solution.py:591
  100.2 15.3 %collective-permute-start.27 = (bf16[288,768]{1,0:T(8,128)(2,1)S(1)}, bf16[288,768]{1,0:T(8,128)(2,1)S(1)}, u32[]{:S(2)}, u32[]{:S(2)}) collective-permute-start(bf16[288,768]{1,0:T(8,128)(2,1)S(1)} %collective-permute-done.6.refs_0_), channel_id=1, source_target_pairs={{0,1},{1,0},{2,3},{3,2},{4,5},{5,4},{6,7},{7,6},{8,9},{9,8},{10,11... | collective-permute-start | bytes 1327112 | tf_op jit(solution)/shard_map/ppermute | solution.py:580
  106.3 19.7 %collective-permute-start.23 = (bf16[288,768]{1,0:T(8,128)(2,1)S(1)}, bf16[288,768]{1,0:T(8,128)(2,1)S(1)}, u32[]{:S(2)}, u32[]{:S(2)}) collective-permute-start(bf16[288,768]{1,0:T(8,128)(2,1)S(1)} %collective-permute-done.13.refs_0_), channel_id=1, source_target_pairs={{0,16},{1,3},{2,18},{3,1},{16,0},{17,19},{18,2},{19,17},{4,20},{5,... | collective-permute-start | bytes 1327112 | tf_op jit(solution)/shard_map/ppermute | solution.py:591
  107.0 23.8 %collective-permute-start.28 = (bf16[288,768]{1,0:T(8,128)(2,1)S(1)}, bf16[288,768]{1,0:T(8,128)(2,1)}, u32[]{:S(2)}, u32[]{:S(2)}) collective-permute-start(bf16[288,768]{1,0:T(8,128)(2,1)S(1)} %collective-permute-done.14.refs_1_), channel_id=1, source_target_pairs={{0,1},{1,0},{2,3},{3,2},{4,5},{5,4},{6,7},{7,6},{8,9},{9,8},{10,11... | collective-permute-start | bytes 1327112 | tf_op jit(solution)/shard_map/ppermute | solution.py:580
  115.4 15.3 %collective-permute-start.29 = (bf16[288,768]{1,0:T(8,128)(2,1)}, bf16[288,768]{1,0:T(8,128)(2,1)}, u32[]{:S(2)}, u32[]{:S(2)}) collective-permute-start(bf16[288,768]{1,0:T(8,128)(2,1)} %collective-permute-done.26.refs_2_), channel_id=1, source_target_pairs={{0,1},{1,0},{2,3},{3,2},{4,5},{5,4},{6,7},{7,6},{8,9},{9,8},{10,11... | collective-permute-start | bytes 1327112 | tf_op jit(solution)/shard_map/ppermute | solution.py:580
  115.4 19.9 %collective-permute-start.24 = (bf16[288,768]{1,0:T(8,128)(2,1)S(1)}, bf16[288,768]{1,0:T(8,128)(2,1)}, u32[]{:S(2)}, u32[]{:S(2)}) collective-permute-start(bf16[288,768]{1,0:T(8,128)(2,1)S(1)} %collective-permute-done.13.refs_0_), channel_id=1, source_target_pairs={{0,2},{1,17},{2,0},{3,19},{16,18},{17,1},{18,16},{19,3},{4,6},{5,2... | collective-permute-start | bytes 1327112 | tf_op jit(solution)/shard_map/ppermute | solution.py:591
  115.5 19.8 %collective-permute-start.30 = (bf16[288,768]{1,0:T(8,128)(2,1)S(1)}, bf16[288,768]{1,0:T(8,128)(2,1)}, u32[]{:S(2)}, u32[]{:S(2)}) collective-permute-start(bf16[288,768]{1,0:T(8,128)(2,1)S(1)} %collective-permute-done.15.refs_3_), channel_id=1, source_target_pairs={{0,1},{1,0},{2,3},{3,2},{4,5},{5,4},{6,7},{7,6},{8,9},{9,8},{10,11... | collective-permute-start | bytes 1327112 | tf_op jit(solution)/shard_map/ppermute | solution.py:580
  126.0 15.8 %collective-permute-start.25 = (bf16[288,768]{1,0:T(8,128)(2,1)S(1)}, bf16[288,768]{1,0:T(8,128)(2,1)}, u32[]{:S(2)}, u32[]{:S(2)}) collective-permute-start(bf16[288,768]{1,0:T(8,128)(2,1)S(1)} %collective-permute-done.23.refs_1_), channel_id=1, source_target_pairs={{0,2},{1,17},{2,0},{3,19},{16,18},{17,1},{18,16},{19,3},{4,6},{5,2... | collective-permute-start | bytes 1327112 | tf_op jit(solution)/shard_map/ppermute | solution.py:591
  130.8 11.7 %collective-permute-start.31 = (bf16[288,768]{1,0:T(8,128)(2,1)S(1)}, bf16[288,768]{1,0:T(8,128)(2,1)S(1)}, u32[]{:S(2)}, u32[]{:S(2)}) collective-permute-start(bf16[288,768]{1,0:T(8,128)(2,1)S(1)} %collective-permute-done.13.refs_0_), channel_id=1, source_target_pairs={{0,1},{1,0},{2,3},{3,2},{4,5},{5,4},{6,7},{7,6},{8,9},{9,8},{10,11... | collective-permute-start | bytes 1327112 | tf_op jit(solution)/shard_map/ppermute | solution.py:580
  130.8 11.7 %collective-permute-start.32 = (bf16[288,768]{1,0:T(8,128)(2,1)S(1)}, bf16[288,768]{1,0:T(8,128)(2,1)S(1)}, u32[]{:S(2)}, u32[]{:S(2)}) collective-permute-start(bf16[288,768]{1,0:T(8,128)(2,1)S(1)} %collective-permute-done.23.refs_1_), channel_id=1, source_target_pairs={{0,1},{1,0},{2,3},{3,2},{4,5},{5,4},{6,7},{7,6},{8,9},{9,8},{10,11... | collective-permute-start | bytes 1327112 | tf_op jit(solution)/shard_map/ppermute | solution.py:580
  166.3 13.0 %all-to-all-start.1 = ((bf16[4,3,96,256]{3,2,1,0:T(8,128)(2,1)}), bf16[4,3,96,256]{3,2,1,0:T(8,128)(2,1)S(1)}, u32[]{:S(2)}, u32[]{:S(2)}) async-start(bf16[4,3,96,256]{3,2,1,0:T(8,128)(2,1)} %attend_forward.1), calls=%async_computation.1 | async-start | bytes 1179648 | tf_op jit(solution)/shard_map/all_to_all | solution.py:693
  205.3 9.3 %collective-permute-start.36 = (bf16[384,7040]{1,0:T(8,128)(2,1)}, bf16[384,7040]{1,0:T(8,128)(2,1)}, u32[]{:S(2)}, u32[]{:S(2)}) collective-permute-start(bf16[384,7040]{1,0:T(8,128)(2,1)} %get-tuple-element.81), channel_id=1, source_target_pairs={{0,1},{1,0},{2,3},{3,2},{4,5},{5,4},{6,7},{7,6},{8,9},{9,8},{10,11... | collective-permute-start | bytes 16220168 | tf_op jit(solution)/shard_map/ppermute | solution.py:580
  205.4 15.2 %all-to-all-start.2 = ((bf16[4,3,96,256]{3,2,1,0:T(8,128)(2,1)}), bf16[4,3,96,256]{3,2,1,0:T(8,128)(2,1)S(1)}, u32[]{:S(2)}, u32[]{:S(2)}) async-start(bf16[4,3,96,256]{3,2,1,0:T(8,128)(2,1)} %bitcast.136), calls=%async_computation.2 | async-start | bytes 1179648 | tf_op jit(solution)/shard_map/all_to_all | solution.py:712
  220.6 33.9 %collective-permute-start.39 = (bf16[192,7040]{1,0:T(8,128)(2,1)}, bf16[192,7040]{1,0:T(8,128)(2,1)}, u32[]{:S(2)}, u32[]{:S(2)}) collective-permute-start(bf16[192,7040]{1,0:T(8,128)(2,1)} %get-tuple-element.86), channel_id=1, source_target_pairs={{0,16},{1,3},{2,18},{3,1},{16,0},{17,19},{18,2},{19,17},{4,20},{5,... | collective-permute-start | bytes 8110088 | tf_op jit(solution)/shard_map/ppermute | solution.py:591
  221.5 16.5 %collective-permute-start.35 = (bf16[4,3,96,256]{3,2,1,0:T(8,128)(2,1)S(1)}, bf16[4,3,96,256]{3,2,1,0:T(8,128)(2,1)}, u32[]{:S(2)}, u32[]{:S(2)}) collective-permute-start(bf16[4,3,96,256]{3,2,1,0:T(8,128)(2,1)S(1)} %all-to-all-done.2.load_ref), channel_id=1, source_target_pairs={{0,4},{4,8},{8,12},{12,0},{1,5},{5,9},{9,13},{13,1},{2,6},{6,10},{... | collective-permute-start | bytes 1769480 | tf_op jit(solution)/shard_map/ppermute | solution.py:724
  252.3 17.0 %collective-permute-start.37 = (bf16[4,3,96,256]{3,2,1,0:T(8,128)(2,1)}, bf16[4,3,96,256]{3,2,1,0:T(8,128)(2,1)S(1)}, u32[]{:S(2)}, u32[]{:S(2)}) collective-permute-start(bf16[4,3,96,256]{3,2,1,0:T(8,128)(2,1)} %collective-permute-done.35.load_ref), channel_id=1, source_target_pairs={{0,4},{4,8},{8,12},{12,0},{1,5},{5,9},{9,13},{13,1},{2,6},{6,10},{... | collective-permute-start | bytes 1769480 | tf_op jit(solution)/shard_map/ppermute | solution.py:724
  257.1 44.0 %collective-permute-start.43 = (bf16[96,7040]{1,0:T(8,128)(2,1)}, bf16[96,7040]{1,0:T(8,128)(2,1)}, u32[]{:S(2)}, u32[]{:S(2)}) collective-permute-start(bf16[96,7040]{1,0:T(8,128)(2,1)} %add_convert_fusion.5), channel_id=1, source_target_pairs={{0,2},{1,17},{2,0},{3,19},{16,18},{17,1},{18,16},{19,3},{4,6},{5,2... | collective-permute-start | bytes 4055048 | tf_op jit(solution)/shard_map/ppermute | solution.py:591
  269.3 15.6 %collective-permute-start.38 = (bf16[4,3,96,256]{3,2,1,0:T(8,128)(2,1)S(1)}, bf16[4,3,96,256]{3,2,1,0:T(8,128)(2,1)}, u32[]{:S(2)}, u32[]{:S(2)}) collective-permute-start(bf16[4,3,96,256]{3,2,1,0:T(8,128)(2,1)S(1)} %collective-permute-done.37.load_ref), channel_id=1, source_target_pairs={{0,4},{4,8},{8,12},{12,0},{1,5},{5,9},{9,13},{13,1},{2,6},{6,10},{... | collective-permute-start | bytes 1769480 | tf_op jit(solution)/shard_map/ppermute | solution.py:724
  301.1 9.4 %collective-permute-start.40 = (bf16[2,2,288,768]{3,2,1,0:T(8,128)(2,1)}, bf16[2,2,288,768]{3,2,1,0:T(8,128)(2,1)S(1)}, u32[]{:S(2)}, u32[]{:S(2)}) collective-permute-start(bf16[2,2,288,768]{3,2,1,0:T(8,128)(2,1)} %get-tuple-element.89), channel_id=1, source_target_pairs={{0,1},{1,0},{2,3},{3,2},{4,5},{5,4},{6,7},{7,6},{8,9},{9,8},{10,11... | collective-permute-start | bytes 5308424 | tf_op jit(solution)/shard_map/ppermute | solution.py:580
  304.6 14.7 %collective-permute-start.44 = (bf16[24,7040]{1,0:T(8,128)(2,1)}, bf16[24,7040]{1,0:T(8,128)(2,1)S(1)}, u32[]{:S(2)}, u32[]{:S(2)}) collective-permute-start(bf16[24,7040]{1,0:T(8,128)(2,1)} %get-tuple-element.162), channel_id=1, source_target_pairs={{0,4},{4,8},{8,12},{12,0},{1,5},{5,9},{9,13},{13,1},{2,6},{6,10},{... | collective-permute-start | bytes 1013768 | tf_op jit(solution)/shard_map/ppermute | solution.py:740
  304.6 38.6 %collective-permute-start.45 = (bf16[24,7040]{1,0:T(8,128)(2,1)}, bf16[24,7040]{1,0:T(8,128)(2,1)}, u32[]{:S(2)}, u32[]{:S(2)}) collective-permute-start(bf16[24,7040]{1,0:T(8,128)(2,1)} %get-tuple-element.164), channel_id=1, source_target_pairs={{0,8},{4,12},{8,0},{12,4},{1,9},{5,13},{9,1},{13,5},{2,10},{6,14},... | collective-permute-start | bytes 1013768 | tf_op jit(solution)/shard_map/ppermute | solution.py:740
  310.5 40.5 %collective-permute-start.46 = (bf16[24,7040]{1,0:T(8,128)(2,1)S(1)}, bf16[24,7040]{1,0:T(8,128)(2,1)}, u32[]{:S(2)}, u32[]{:S(2)}) collective-permute-start(bf16[24,7040]{1,0:T(8,128)(2,1)S(1)} %get-tuple-element.163), channel_id=1, source_target_pairs={{0,12},{4,0},{8,4},{12,8},{1,13},{5,1},{9,5},{13,9},{2,14},{6,2},{... | collective-permute-start | bytes 1013768 | tf_op jit(solution)/shard_map/ppermute | solution.py:740
  311.9 41.2 %collective-permute-start.41 = (bf16[2,288,768]{2,1,0:T(8,128)(2,1)}, bf16[2,288,768]{2,1,0:T(8,128)(2,1)}, u32[]{:S(2)}, u32[]{:S(2)}) collective-permute-start(bf16[2,288,768]{2,1,0:T(8,128)(2,1)} %slice_bitcast_fusion), channel_id=1, source_target_pairs={{0,16},{1,3},{2,18},{3,1},{16,0},{17,19},{18,2},{19,17},{4,20},{5,... | collective-permute-start | bytes 2654216 | tf_op jit(solution)/shard_map/ppermute | solution.py:591
  311.9 54.4 %all-to-all-start.3 = ((bf16[32,24,640]{2,1,0:T(8,128)(2,1)}), bf16[32,24,640]{2,1,0:T(8,128)(2,1)S(1)}, u32[]{:S(2)}, u32[]{:S(2)}) async-start(bf16[32,24,640]{2,1,0:T(8,128)(2,1)} %bitcast.135), calls=%async_computation.3 | async-start | bytes 1966080 | tf_op jit(solution)/shard_map/all_to_all | solution.py:745
  354.3 9.7 %collective-permute-start.42 = (bf16[288,768]{1,0:T(8,128)(2,1)S(1)}, bf16[288,768]{1,0:T(8,128)(2,1)}, u32[]{:S(2)}, u32[]{:S(2)}) collective-permute-start(bf16[288,768]{1,0:T(8,128)(2,1)S(1)} %fusion), channel_id=1, source_target_pairs={{0,2},{1,17},{2,0},{3,19},{16,18},{17,1},{18,16},{19,3},{4,6},{5,2... | collective-permute-start | bytes 1327112 | tf_op jit(solution)/shard_map/ppermute | solution.py:591
  (39 other events, 471.6 us)
Sparse Core Ops, SparseCore 0:
  36.5 116.1 all-gather.1

commit v4 on v3

--- a/solution.py
+++ b/solution.py
@@ -226,10 +226,10 @@
     return pl.BlockSpec((1, shards, 1, rows, 128), lambda s, pair, *_: (pair[h], 0, s, 0, h))
 
 
-def attend_forward(q_loc, kv, pair, begin, last, end_row_own):
+def attend_forward(q_all, kv, pair, begin, last, end_row_own):
     _, shards, seqs, rows, _ = kv.shape
     nq = TP * rows
-    row_spec = pl.BlockSpec((TP, 1, rows, 384), lambda s, *_: (0, s, 0, 0))
+    row_spec = pl.BlockSpec((TP, 1, rows, 384), lambda s, pair, begin, last: (last[seqs * HG], s, 0, 0))
     end_spec = pl.BlockSpec((1, HG, 1, nq), lambda s, *_: (s, 0, 0, 0))
     return pl.pallas_call(
         functools.partial(forward_kernel, rows, shards),
@@ -244,13 +244,13 @@
         compiler_params=pltpu.CompilerParams(vmem_limit_bytes=VMEM_LIMIT),
         cost_estimate=pl.CostEstimate(flops=4 * 9 * nq * shards * rows * 128, bytes_accessed=12 << 20, transcendentals=0),
         name="attend_forward",
-    )(pair, begin, last, q_loc, kv, kv, kv, end_row_own)
-
-
-def attend_query(q_loc, kv, pair, begin, last, end_row_own, load):
+    )(pair, begin, last, q_all, kv, kv, kv, end_row_own)
+
+
+def attend_query(q_all, kv, pair, begin, last, end_row_own, load):
     _, shards, seqs, rows, _ = kv.shape
     nq = TP * rows
-    row_spec = pl.BlockSpec((TP, 1, rows, 384), lambda s, *_: (0, s, 0, 0))
+    row_spec = pl.BlockSpec((TP, 1, rows, 384), lambda s, pair, begin, last: (last[seqs * HG], s, 0, 0))
     end_spec = pl.BlockSpec((1, HG, 1, nq), lambda s, *_: (s, 0, 0, 0))
     return pl.pallas_call(
         functools.partial(query_kernel, rows, shards),
@@ -267,7 +267,7 @@
         compiler_params=pltpu.CompilerParams(vmem_limit_bytes=VMEM_LIMIT),
         cost_estimate=pl.CostEstimate(flops=6 * 9 * nq * shards * rows * 128, bytes_accessed=12 << 20, transcendentals=0),
         name="attend_query",
-    )(pair, begin, last, q_loc, kv, kv, kv, end_row_own, load)
+    )(pair, begin, last, q_all, kv, kv, kv, end_row_own, load)
 
 
 def attend_key(q_all, load, kv, pair, begin, reach, place, end_row, old):
@@ -675,7 +675,6 @@
     buffers = stages[-1]
     kv = buffers[0].reshape(2, shards, seqs, rows, HG * 128)
     q_all = buffers[1].reshape(shards, seqs, rows, HG * 128)
-    q_loc = lax.dynamic_slice_in_dim(q_all, me_r * TP, TP, 0)
 
     pair = lax.dynamic_slice_in_dim(pick(pairing, me_u, 1), me_t * HG, HG, 0)
     ids = block_ids.reshape(seqs, 2, half)
@@ -684,12 +683,12 @@
     end_all = jnp.where((pair == 0)[None, :, None], ends[:, 0:1], ends[:, 1:2])
     end_loc = lax.dynamic_slice_in_dim(end_all, me_r * TP * rows, TP * rows, 2)
     begin = jnp.maximum(offsets[:, None] - pair[None, :] * half, 0).reshape(-1)
-    last = end_loc[:, :, -1].reshape(-1)
+    last = jnp.concatenate([end_loc[:, :, -1].reshape(-1), me_r[None].astype(jnp.int32)])
     start = me_r * TP * rows
     end_ring = end_all.reshape(seqs, HG, ring, TP * rows)
     end_row_own = end_loc[:, :, None]
 
-    att = attend_forward(q_loc, kv, pair, begin, last, end_row_own)
+    att = attend_forward(q_all, kv, pair, begin, last, end_row_own)
     att = lax.all_to_all(att, ("y", "c"), split_axis=0, concat_axis=0, tiled=True).reshape(TP, tokens, 256)
 
     index = jnp.arange(width, dtype=jnp.int32)
@@ -718,21 +717,22 @@
     for k in range(ring):
         if k >= 2:
             moving, done[k - 2] = lax.optimization_barrier((moving, done[k - 2]))
-        if k == 2:
-            moving, dq = lax.optimization_barrier((moving, dq))
         if k:
             moving = lax.ppermute(moving, "r", forward)
         source = (me_r - k) % ring
         ends_k = pick(end_ring, source, 2)
         where = jnp.concatenate([place, source[None]]).astype(jnp.int32)
         before = done[-1] if done else dkv
+        if k == 2:
+            dq = attend_query(q_all, kv, pair, begin, last, end_row_own, after(load, high_first, moving))
+        if k == ring - 1:
+            before = after(before, dq)
         if k == ring - 2:
+            came = after(came, done[1], moving)
             high2, low2 = add(low[cut:], came[cut:]), add(low[:cut], came[:cut])
             stay = add(low2, cross_two(high2))
             before = after(before, high2)
         done.append(attend_key(q_all, moving, kv, pair, begin, ends_k[:, :, -1].reshape(-1), where, ends_k[:, :, None], before))
-        if k == 0:
-            dq = attend_query(q_loc, kv, pair, begin, last, end_row_own, after(load, high))
 
     summed = stay[:part].astype(F32)
     for j in range(1, ring):

time: 385 us -> 382 us (level)
  starting transfers between devices: 73 us -> 69 us
  transfers between devices with their start and end apart: 52 -> 52, of which waited for: 20 -> 18; matrix products, arithmetic and copies ran while one was open for 14% -> 13% of each run, Pallas kernels for 25% -> 25%
where the time goes in v4:
time: 382 us; the launch traced here: 376 us
  Pallas kernels  120 us (31%)
  waiting for transfers between devices  114 us (30%)
  starting transfers between devices  69 us (18%)
  other arithmetic  31.5 us (8%)
  local copies, waits for them, and re-layouts  25.9 us (7%)
  between operations  15.1 us (4%)
    ppermute x16, waiting for transfers between devices, crossing(): return lambda v: lax.ppermute(v, ('u', 'y', 'c'), pairs)  37 us
    ppermute x3, waiting for transfers between devices, per_device(): lax.ppermute(stay[j * part:(j + 1) * part], 'r', along).astype(F32)  33.8 us
    pallas_call x4, Pallas kernels, attend_key(): pl.pallas_call(functools.partial(key_kernel, rows), grid_spec=pltpu.Prefe...  28.9 us
    pallas_call x1, Pallas kernels, dense_layers(): pl.pallas_call(functools.partial(dense_kernel, fold), in_specs=[local, lo...  25.2 us
    pallas_call x4, Pallas kernels, project(): pl.pallas_call(functools.partial(project_kernel, seqs, rows, not extra),...  23 us
    ppermute x19, starting transfers between devices, swap_on(): return lambda v: lax.ppermute(v, axis, [(0, 1), (1, 0)])  18.6 us
    ppermute x16, starting transfers between devices, crossing(): return lambda v: lax.ppermute(v, ('u', 'y', 'c'), pairs)  17.3 us
    pallas_call x1, Pallas kernels, attend_query(): pl.pallas_call(functools.partial(query_kernel, rows, shards), grid_spec=p...  14.7 us
  transfers between devices with their start and end apart: 52, of which 18 were waited for; matrix products, arithmetic and copies ran while one was open for 13% of the time, Pallas kernels for 25%

profile of v4, /device:TPU:8, one launch (start us, length us, event | category | flops | bytes accessed | tf_op | source)
XLA Modules:
  0.0 375.5 jit_solution(12278060091542917032)
XLA Ops:
  13.6 3.3 all-to-all-start
  24.7 1.8 collective-permute-start.2
  26.6 5.7 %collective-permute-done = bf16[4,24,640]{2,1,0:T(8,128)(2,1)S(1)} collective-permute-done((bf16[4,24,640]{2,1,0:T(8,128)(2,1)S(1)}, bf16[4,24,640]{2,1,0:T(8,128)(2,1)S(1)}, u32[]{:S(2)}, u32[]{:S(2)}) %collective-permute-start) | collective-permute-done | bytes 122912 | tf_op jit(solution)/shard_map/ppermute | solution.py:640
  32.3 2.3 collective-permute-done.1
  34.6 1.7 collective-permute-done.2
  40.2 5.9 %collective-permute-done.7.refs_3_ = bf16[288,768]{1,0:T(8,128)(2,1)} collective-permute-done((bf16[288,768]{1,0:T(8,128)(2,1)S(1)}, bf16[288,768]{1,0:T(8,128)(2,1)}, u32[]{:S(2)}, u32[]{:S(2)}) %collective-permute-start.7) | collective-permute-done | bytes 442400 | tf_op jit(solution)/shard_map/ppermute | solution.py:591
  46.1 11.4 %collective-permute-start.10 = (bf16[288,768]{1,0:T(8,128)(2,1)S(1)}, bf16[288,768]{1,0:T(8,128)(2,1)}, u32[]{:S(2)}, u32[]{:S(2)}) collective-permute-start(bf16[288,768]{1,0:T(8,128)(2,1)S(1)} %collective-permute-done.4.refs_2_), channel_id=1, source_target_pairs={{0,1},{1,0},{2,3},{3,2},{4,5},{5,4},{6,7},{7,6},{8,9},{9,8},{10,11... | collective-permute-start | bytes 1327112 | tf_op jit(solution)/shard_map/ppermute | solution.py:580
  61.2 5.7 %project.4 = (bf16[2,4,4,3,96,384]{5,4,3,2,1,0:T(8,128)(2,1)}, bf16[4,4,3,96,384]{4,3,2,1,0:T(8,128)(2,1)}) custom-call(s32[4]{0:T(128)} %get-tuple-element.188.spot_ref, bf16[288,768]{1,0:T(8,128)(2,1)} %bitcast.141, bf16[288,768]{1,0:T(8,128)(2,1)} %copy-done.9, bf16[288,768]{1,0:T(8,128)(2,1)} %copy-done.10, ...), custom_call_target="tpu_custom_call" | custom-call | flops 2038431744 | bytes 12582912 | tf_op jit(solution)/shard_map/project/pallas_call | solution.py:204
  66.9 7.5 %collective-permute-done.6.refs_0_ = bf16[288,768]{1,0:T(8,128)(2,1)S(1)} collective-permute-done((bf16[288,768]{1,0:T(8,128)(2,1)}, bf16[288,768]{1,0:T(8,128)(2,1)S(1)}, u32[]{:S(2)}, u32[]{:S(2)}) %collective-permute-start.6) | collective-permute-done | bytes 442400 | tf_op jit(solution)/shard_map/ppermute | solution.py:660
  74.4 2.0 collective-permute-start.18
  77.1 2.8 collective-permute-start.13
  80.0 5.4 %collective-permute-done.18.refs_3_ = bf16[288,768]{1,0:T(8,128)(2,1)S(1)} collective-permute-done((bf16[288,768]{1,0:T(8,128)(2,1)}, bf16[288,768]{1,0:T(8,128)(2,1)S(1)}, u32[]{:S(2)}, u32[]{:S(2)}) %collective-permute-start.18) | collective-permute-done | bytes 442400 | tf_op jit(solution)/shard_map/ppermute | solution.py:591
  85.4 3.8 %collective-permute-start.22 = (bf16[288,768]{1,0:T(8,128)(2,1)S(1)}, bf16[288,768]{1,0:T(8,128)(2,1)}, u32[]{:S(2)}, u32[]{:S(2)}) collective-permute-start(bf16[288,768]{1,0:T(8,128)(2,1)S(1)} %collective-permute-done.18.refs_3_), channel_id=1, source_target_pairs={{0,1},{1,0},{2,3},{3,2},{4,5},{5,4},{6,7},{7,6},{8,9},{9,8},{10,11... | collective-permute-start | bytes 1327112 | tf_op jit(solution)/shard_map/ppermute | solution.py:580
  91.9 7.8 %convert_reduce_fusion = s32[3,2,1536]{2,1,0:T(2,128)S(1)} fusion(s32[3,1536]{1,0:T(4,128)S(1)} %bitcast.151, s32[3,2,1536]{2,1,0:T(2,128)S(1)} %le.17), kind=kLoop, calls=%fused_computation | loop fusion | flops 42458112 | bytes 92160 | tf_op jit(solution)/shard_map/reduce_sum | solution.py:682
  100.5 5.7 %project.5 = (bf16[2,4,4,3,96,384]{5,4,3,2,1,0:T(8,128)(2,1)}, bf16[4,4,3,96,384]{4,3,2,1,0:T(8,128)(2,1)}) custom-call(s32[4]{0:T(128)} %get-tuple-element.187.spot_ref, bf16[288,768]{1,0:T(8,128)(2,1)} %collective-permute-done.5.refs_0_, bf16[288,768]{1,0:T(8,128)(2,1)} %collective-permute-done.16.refs_1_, ...), custom_call_target="tpu_custom_call", output_to_operand_aliasing={{0}: (11, {}), {1}: (12, {})} | custom-call | flops 2038431744 | bytes 12582912 | tf_op jit(solution)/shard_map/project/pallas_call | solution.py:204
  108.2 7.3 %collective-permute-done.26.refs_2_ = bf16[288,768]{1,0:T(8,128)(2,1)} collective-permute-done((bf16[288,768]{1,0:T(8,128)(2,1)S(1)}, bf16[288,768]{1,0:T(8,128)(2,1)}, u32[]{:S(2)}, u32[]{:S(2)}) %collective-permute-start.26) | collective-permute-done | bytes 442400 | tf_op jit(solution)/shard_map/ppermute | solution.py:591
  116.9 9.1 %collective-permute-done.23.refs_1_ = bf16[288,768]{1,0:T(8,128)(2,1)S(1)} collective-permute-done((bf16[288,768]{1,0:T(8,128)(2,1)S(1)}, bf16[288,768]{1,0:T(8,128)(2,1)S(1)}, u32[]{:S(2)}, u32[]{:S(2)}) %collective-permute-start.23) | collective-permute-done | bytes 442400 | tf_op jit(solution)/shard_map/ppermute | solution.py:591
  126.0 2.2 collective-permute-start.25
  129.9 5.4 %collective-permute-done.24.refs_2_ = bf16[288,768]{1,0:T(8,128)(2,1)} collective-permute-done((bf16[288,768]{1,0:T(8,128)(2,1)S(1)}, bf16[288,768]{1,0:T(8,128)(2,1)}, u32[]{:S(2)}, u32[]{:S(2)}) %collective-permute-start.24) | collective-permute-done | bytes 442400 | tf_op jit(solution)/shard_map/ppermute | solution.py:591
  135.3 5.7 %project.6 = (bf16[2,4,4,3,96,384]{5,4,3,2,1,0:T(8,128)(2,1)}, bf16[4,4,3,96,384]{4,3,2,1,0:T(8,128)(2,1)}) custom-call(s32[4]{0:T(128)} %get-tuple-element.158.spot_ref, bf16[288,768]{1,0:T(8,128)(2,1)} %copy-done.11, bf16[288,768]{1,0:T(8,128)(2,1)} %copy-done.13, ...), custom_call_target="tpu_custom_call", output_to_operand_aliasing={{0}: (11, {}), {1}: (12, {})} | custom-call | flops 2038431744 | bytes 12582912 | tf_op jit(solution)/shard_map/project/pallas_call | solution.py:204
  144.8 5.8 %project.7 = (bf16[2,4,4,3,96,384]{5,4,3,2,1,0:T(8,128)(2,1)}, bf16[4,4,3,96,384]{4,3,2,1,0:T(8,128)(2,1)}) custom-call(s32[4]{0:T(128)} %get-tuple-element.189.spot_ref, bf16[288,768]{1,0:T(8,128)(2,1)} %copy-done.12, bf16[288,768]{1,0:T(8,128)(2,1)} %copy-done.15, ...), custom_call_target="tpu_custom_call", output_to_operand_aliasing={{0}: (11, {}), {1}: (12, {})} | custom-call | flops 2038431744 | bytes 12582912 | tf_op jit(solution)/shard_map/project/pallas_call | solution.py:204
  150.6 13.8 %attend_forward.1 = bf16[4,3,96,256]{3,2,1,0:T(8,128)(2,1)} custom-call(s32[3]{0:T(128)} %copy-done.29, s32[9]{0:T(128)} %max.8.begin_ref, s32[10]{0:T(128)} %pad_add_fusion.last_ref, bf16[16,3,96,384]{3,2,1,0:T(8,128)(2,1)} %bitcast.120, bf16[2,16,3,96,384]{4,3,2,1,0:T(8,128)(2,1)} %bitcast.102, bf16[2,16,3,96,384]{4,3,2,1,0:T(8,128)(2,1)} %bitcast.103, ...), custom_call_target="tpu_custom_call" | custom-call | flops 2717908992 | bytes 12582912 | tf_op jit(solution)/shard_map/attend_forward/pallas_call | solution.py:234
  164.4 3.6 all-to-all-start.1
  168.1 9.3 %all-to-all-done.1 = bf16[4,3,96,256]{3,2,1,0:T(8,128)(2,1)S(1)} async-done(((bf16[4,3,96,256]{3,2,1,0:T(8,128)(2,1)}), bf16[4,3,96,256]{3,2,1,0:T(8,128)(2,1)S(1)}, u32[]{:S(2)}, u32[]{:S(2)}) %all-to-all-start.1) | async-done | bytes 589856 | tf_op jit(solution)/shard_map/all_to_all | solution.py:692
  178.3 25.2 %dense_layers.1 = (bf16[288,768]{1,0:T(8,128)(2,1)}, bf16[4,288,256]{2,1,0:T(8,128)(2,1)}, f32[288,768]{1,0:T(8,128)}, bf16[384,7040]{1,0:T(8,128)(2,1)}, bf16[384,7040]{1,0:T(8,128)(2,1)}) custom-call(bf16[4,288,256]{2,1,0:T(8,128)(2,1)} %bitcast.138, bf16[288,768]{1,0:T(8,128)(2,1)} %bitcast.142, bf16[288,768]{1,0:T(8,128)(2,1)} %bitcast.152, ...), custom_call_target="tpu_custom_call" | custom-call | flops 9172942848 | bytes 25165824 | tf_op jit(solution)/shard_map/dense_layers/pallas_call | solution.py:409
  203.5 3.5 all-to-all-start.2
  207.0 5.7 %collective-permute-done.35 = bf16[384,7040]{1,0:T(8,128)(2,1)} collective-permute-done((bf16[384,7040]{1,0:T(8,128)(2,1)}, bf16[384,7040]{1,0:T(8,128)(2,1)}, u32[]{:S(2)}, u32[]{:S(2)}) %collective-permute-start.35) | collective-permute-done | bytes 5406752 | tf_op jit(solution)/shard_map/ppermute | solution.py:580
  212.8 5.9 %add_convert_fusion = (bf16[192,7040]{1,0:T(8,128)(2,1)S(1)}, bf16[192,7040]{1,0:T(8,128)(2,1)}) fusion(bf16[384,7040]{1,0:T(8,128)(2,1)} %collective-permute-done.35, bf16[384,7040]{1,0:T(8,128)(2,1)} %get-tuple-element.79), kind=kLoop, calls=%fused_computation.1 | loop fusion | flops 10813440 | bytes 16220160 | tf_op jit(solution)/shard_map/convert_element_type | solution.py:599
  219.5 2.8 collective-permute-start.36
  225.7 7.2 %attend_key.4.old_ref = f32[4,3,96,384]{3,2,1,0:T(8,128)} custom-call(s32[3]{0:T(128)} %copy-done.29, s32[9]{0:T(128)} %max.8.begin_ref, s32[9]{0:T(128)} %reshape_squeeze.20.reach_ref, s32[3]{0:T(128)} %get-tuple-element.186.place_ref, bf16[16,3,96,384]{3,2,1,0:T(8,128)(2,1)} %bitcast.121, ...), custom_call_target="tpu_custom_call", output_to_operand_aliasing={{}: (10, {})} | custom-call | flops 1358954496 | bytes 8388608 | tf_op jit(solution)/shard_map/attend_key/pallas_call | solution.py:280
  233.0 3.4 collective-permute-done.36.load_ref
  238.6 7.2 %attend_key.5.old_ref = f32[4,3,96,384]{3,2,1,0:T(8,128)} custom-call(s32[3]{0:T(128)} %copy-done.29, s32[9]{0:T(128)} %max.8.begin_ref, s32[9]{0:T(128)} %reshape_squeeze.22.reach_ref, s32[3]{0:T(128)} %get-tuple-element.184.place_ref, bf16[16,3,96,384]{3,2,1,0:T(8,128)(2,1)} %bitcast.122, ...), custom_call_target="tpu_custom_call", output_to_operand_aliasing={{}: (10, {})} | custom-call | flops 1358954496 | bytes 8388608 | tf_op jit(solution)/shard_map/attend_key/pallas_call | solution.py:280
  245.9 7.1 %collective-permute-done.37.load_ref = bf16[4,3,96,256]{3,2,1,0:T(8,128)(2,1)S(1)} collective-permute-done((bf16[4,3,96,256]{3,2,1,0:T(8,128)(2,1)}, bf16[4,3,96,256]{3,2,1,0:T(8,128)(2,1)S(1)}, u32[]{:S(2)}, u32[]{:S(2)}) %collective-permute-start.37) | collective-permute-done | bytes 589856 | tf_op jit(solution)/shard_map/ppermute | solution.py:721
  253.0 2.9 add_convert_fusion.5
  260.1 14.7 %attend_query.1.dq_ref = bf16[4,3,96,192]{3,2,1,0:T(8,128)(2,1)} custom-call(s32[3]{0:T(128)} %copy-done.29, s32[9]{0:T(128)} %max.8.begin_ref, s32[10]{0:T(128)} %pad_add_fusion.last_ref, bf16[16,3,96,384]{3,2,1,0:T(8,128)(2,1)} %bitcast.123, bf16[2,16,3,96,384]{4,3,2,1,0:T(8,128)(2,1)} %bitcast.111, bf16[2,16,3,96,384]{4,3,2,1,0:T(8,128)(2,1)} %bitcast.112, ...), custom_call_target="tpu_custom_call" | custom-call | flops 4076863488 | bytes 12582912 | tf_op jit(solution)/shard_map/attend_query/pallas_call | solution.py:255
  274.8 7.2 %attend_key.6.old_ref = f32[4,3,96,384]{3,2,1,0:T(8,128)} custom-call(s32[3]{0:T(128)} %copy-done.29, s32[9]{0:T(128)} %max.8.begin_ref, s32[9]{0:T(128)} %reshape_squeeze.23.reach_ref, s32[3]{0:T(128)} %get-tuple-element.154.place_ref, bf16[16,3,96,384]{3,2,1,0:T(8,128)(2,1)} %bitcast.124, ...), custom_call_target="tpu_custom_call", output_to_operand_aliasing={{}: (10, {})} | custom-call | flops 1358954496 | bytes 8388608 | tf_op jit(solution)/shard_map/attend_key/pallas_call | solution.py:280
  282.9 7.2 %attend_key.7.dkv_ref = f32[4,3,96,384]{3,2,1,0:T(8,128)} custom-call(s32[3]{0:T(128)} %copy-done.29, s32[9]{0:T(128)} %max.8.begin_ref, s32[9]{0:T(128)} %reshape_squeeze.21.reach_ref, s32[3]{0:T(128)} %get-tuple-element.185.place_ref, bf16[16,3,96,384]{3,2,1,0:T(8,128)(2,1)} %bitcast.125, ...), custom_call_target="tpu_custom_call", output_to_operand_aliasing={{}: (10, {})} | custom-call | flops 1358954496 | bytes 8388608 | tf_op jit(solution)/shard_map/attend_key/pallas_call | solution.py:280
  290.1 9.0 %tail.1 = (bf16[2,2,288,768]{3,2,1,0:T(8,128)(2,1)}, bf16[2,2,288,768]{3,2,1,0:T(8,128)(2,1)}, bf16[768,640]{1,0:T(8,128)(2,1)}) custom-call(s32[6]{0:T(128)} %pad_add_fusion.6.spot_ref, bf16[4,3,96,192]{3,2,1,0:T(8,128)(2,1)} %attend_query.1.dq_ref, f32[4,3,96,384]{3,2,1,0:T(8,128)} %attend_key.7.dkv_ref, bf16[768,640]{1,0:T(8,128)(2,1)} %bitcast.131, ...), custom_call_target="tpu_custom_call" | custom-call | flops 1698693120 | bytes 16777216 | tf_op jit(solution)/shard_map/tail/pallas_call | solution.py:485
  299.1 2.3 add_convert_fusion.3
  302.5 5.5 %collective-permute-start.45 = (bf16[24,7040]{1,0:T(8,128)(2,1)}, bf16[24,7040]{1,0:T(8,128)(2,1)}, u32[]{:S(2)}, u32[]{:S(2)}) collective-permute-start(bf16[24,7040]{1,0:T(8,128)(2,1)} %get-tuple-element.164), channel_id=1, source_target_pairs={{0,8},{4,12},{8,0},{12,4},{1,9},{5,13},{9,1},{13,5},{2,10},{6,14},... | collective-permute-start | bytes 1013768 | tf_op jit(solution)/shard_map/ppermute | solution.py:740
  309.8 4.9 %all-to-all-start.3 = ((bf16[32,24,640]{2,1,0:T(8,128)(2,1)}), bf16[32,24,640]{2,1,0:T(8,128)(2,1)S(1)}, u32[]{:S(2)}, u32[]{:S(2)}) async-start(bf16[32,24,640]{2,1,0:T(8,128)(2,1)} %bitcast.136), calls=%async_computation.3 | async-start | bytes 1966080 | tf_op jit(solution)/shard_map/all_to_all | solution.py:745
  314.7 28.1 %collective-permute-done.45 = bf16[24,7040]{1,0:T(8,128)(2,1)} collective-permute-done((bf16[24,7040]{1,0:T(8,128)(2,1)}, bf16[24,7040]{1,0:T(8,128)(2,1)}, u32[]{:S(2)}, u32[]{:S(2)}) %collective-permute-start.45) | collective-permute-done | bytes 337952 | tf_op jit(solution)/shard_map/ppermute | solution.py:740
  342.8 5.8 %collective-permute-done.46 = bf16[24,7040]{1,0:T(8,128)(2,1)} collective-permute-done((bf16[24,7040]{1,0:T(8,128)(2,1)S(1)}, bf16[24,7040]{1,0:T(8,128)(2,1)}, u32[]{:S(2)}, u32[]{:S(2)}) %collective-permute-start.46) | collective-permute-done | bytes 337952 | tf_op jit(solution)/shard_map/ppermute | solution.py:740
  348.5 2.2 convert_add_fusion.3.refs_0_
  352.5 3.8 %finish.1 = (f32[24,3072]{1,0:T(8,128)}, f32[4,24,768]{2,1,0:T(8,128)}, f32[24,768]{1,0:T(8,128)}, f32[24,128]{1,0:T(8,128)}) custom-call(f32[24,7040]{1,0:T(8,128)} %convert_add_fusion.3.refs_0_), custom_call_target="tpu_custom_call" | custom-call | flops 134217728 | bytes 2097152 | tf_op jit(solution)/shard_map/finish/pallas_call | solution.py:532
  359.1 2.3 collective-permute-done.42
  361.4 2.4 fusion.2
  364.7 2.1 assemble.1
  (243 shorter events, 57.1 us)
Async XLA Ops:
  7.2 29.1 %collective-permute-start.3 = (bf16[288,768]{1,0:T(8,128)(2,1)}, bf16[288,768]{1,0:T(8,128)(2,1)S(1)}, u32[]{:S(2)}, u32[]{:S(2)}) collective-permute-start(bf16[288,768]{1,0:T(8,128)(2,1)} %bitcast.139), channel_id=1, source_target_pairs={{0,16},{1,3},{2,18},{3,1},{16,0},{17,19},{18,2},{19,17},{4,20},{5,... | collective-permute-start | bytes 1327112 | tf_op jit(solution)/shard_map/ppermute | solution.py:591
  8.7 27.6 %collective-permute-start.4 = (bf16[288,768]{1,0:T(8,128)(2,1)}, bf16[288,768]{1,0:T(8,128)(2,1)S(1)}, u32[]{:S(2)}, u32[]{:S(2)}) collective-permute-start(bf16[288,768]{1,0:T(8,128)(2,1)} %bitcast.140), channel_id=1, source_target_pairs={{0,2},{1,17},{2,0},{3,19},{16,18},{17,1},{18,16},{19,3},{4,6},{5,2... | collective-permute-start | bytes 1327112 | tf_op jit(solution)/shard_map/ppermute | solution.py:591
  16.9 160.5 %all-gather.2.cloned.1.call-start = ((), (), s32[]{:S(2)}) async-start(), calls=%async_computation.4 | async-start | bytes 11151360 | tf_op jit(solution)/shard_map/all_gather | solution.py:644
  21.9 10.3 %collective-permute-start = (bf16[4,24,640]{2,1,0:T(8,128)(2,1)S(1)}, bf16[4,24,640]{2,1,0:T(8,128)(2,1)S(1)}, u32[]{:S(2)}, u32[]{:S(2)}) collective-permute-start(bf16[4,24,640]{2,1,0:T(8,128)(2,1)S(1)} %all-to-all-done), channel_id=1, source_target_pairs={{0,4},{4,8},{8,12},{12,0},{1,5},{5,9},{9,13},{13,1},{2,6},{6,10},{... | collective-permute-start | bytes 368648 | tf_op jit(solution)/shard_map/ppermute | solution.py:640
  23.5 11.1 %collective-permute-start.1 = (bf16[4,24,640]{2,1,0:T(8,128)(2,1)S(1)}, bf16[4,24,640]{2,1,0:T(8,128)(2,1)S(1)}, u32[]{:S(2)}, u32[]{:S(2)}) collective-permute-start(bf16[4,24,640]{2,1,0:T(8,128)(2,1)S(1)} %all-to-all-done), channel_id=1, source_target_pairs={{0,8},{4,12},{8,0},{12,4},{1,9},{5,13},{9,1},{13,5},{2,10},{6,14},... | collective-permute-start | bytes 368648 | tf_op jit(solution)/shard_map/ppermute | solution.py:640
  24.7 11.6 %collective-permute-start.2 = (bf16[4,24,640]{2,1,0:T(8,128)(2,1)S(1)}, bf16[4,24,640]{2,1,0:T(8,128)(2,1)S(1)}, u32[]{:S(2)}, u32[]{:S(2)}) collective-permute-start(bf16[4,24,640]{2,1,0:T(8,128)(2,1)S(1)} %all-to-all-done), channel_id=1, source_target_pairs={{0,12},{4,0},{8,4},{12,8},{1,13},{5,1},{9,5},{13,9},{2,14},{6,2},{... | collective-permute-start | bytes 368648 | tf_op jit(solution)/shard_map/ppermute | solution.py:640
  36.4 21.4 %collective-permute-start.8 = (bf16[288,768]{1,0:T(8,128)(2,1)S(1)}, bf16[288,768]{1,0:T(8,128)(2,1)}, u32[]{:S(2)}, u32[]{:S(2)}) collective-permute-start(bf16[288,768]{1,0:T(8,128)(2,1)S(1)} %bitcast.144), channel_id=1, source_target_pairs={{0,1},{1,0},{2,3},{3,2},{4,5},{5,4},{6,7},{7,6},{8,9},{9,8},{10,11... | collective-permute-start | bytes 1327112 | tf_op jit(solution)/shard_map/ppermute | solution.py:580
  36.5 21.0 %collective-permute-start.12 = (bf16[4,4,24,640]{3,2,1,0:T(8,128)(2,1)S(1)}, bf16[4,4,24,640]{3,2,1,0:T(8,128)(2,1)S(1)}, u32[]{:S(2)}, u32[]{:S(2)}) collective-permute-start(bf16[4,4,24,640]{3,2,1,0:T(8,128)(2,1)S(1)} %bitcast_dynamic-update-slice_fusion.2), channel_id=1, source_target_pairs={{0,16},{16,0},{1,17},{17,1},{2,18},{18,2},{3,19},{19,3},{4,20},{20... | collective-permute-start | bytes 1474568 | tf_op jit(solution)/shard_map/ppermute | solution.py:580
  37.7 19.8 %collective-permute-start.5 = (bf16[288,768]{1,0:T(8,128)(2,1)S(1)}, bf16[288,768]{1,0:T(8,128)(2,1)}, u32[]{:S(2)}, u32[]{:S(2)}) collective-permute-start(bf16[288,768]{1,0:T(8,128)(2,1)S(1)} %bitcast.145), channel_id=1, source_target_pairs={{0,4},{4,8},{8,12},{12,0},{1,5},{5,9},{9,13},{13,1},{2,6},{6,10},{... | collective-permute-start | bytes 1327112 | tf_op jit(solution)/shard_map/ppermute | solution.py:660
  40.1 18.8 %collective-permute-start.9 = (bf16[288,768]{1,0:T(8,128)(2,1)S(1)}, bf16[288,768]{1,0:T(8,128)(2,1)}, u32[]{:S(2)}, u32[]{:S(2)}) collective-permute-start(bf16[288,768]{1,0:T(8,128)(2,1)S(1)} %collective-permute-done.3.refs_1_), channel_id=1, source_target_pairs={{0,1},{1,0},{2,3},{3,2},{4,5},{5,4},{6,7},{7,6},{8,9},{9,8},{10,11... | collective-permute-start | bytes 1327112 | tf_op jit(solution)/shard_map/ppermute | solution.py:580
  46.1 14.5 %collective-permute-start.10 = (bf16[288,768]{1,0:T(8,128)(2,1)S(1)}, bf16[288,768]{1,0:T(8,128)(2,1)}, u32[]{:S(2)}, u32[]{:S(2)}) collective-permute-start(bf16[288,768]{1,0:T(8,128)(2,1)S(1)} %collective-permute-done.4.refs_2_), channel_id=1, source_target_pairs={{0,1},{1,0},{2,3},{3,2},{4,5},{5,4},{6,7},{7,6},{8,9},{9,8},{10,11... | collective-permute-start | bytes 1327112 | tf_op jit(solution)/shard_map/ppermute | solution.py:580
  57.5 16.9 %collective-permute-start.6 = (bf16[288,768]{1,0:T(8,128)(2,1)}, bf16[288,768]{1,0:T(8,128)(2,1)S(1)}, u32[]{:S(2)}, u32[]{:S(2)}) collective-permute-start(bf16[288,768]{1,0:T(8,128)(2,1)} %collective-permute-done.5.refs_0_), channel_id=1, source_target_pairs={{0,4},{4,8},{8,12},{12,0},{1,5},{5,9},{9,13},{13,1},{2,6},{6,10},{... | collective-permute-start | bytes 1327112 | tf_op jit(solution)/shard_map/ppermute | solution.py:660
  57.8 16.6 %collective-permute-start.16 = (bf16[288,768]{1,0:T(8,128)(2,1)}, bf16[288,768]{1,0:T(8,128)(2,1)}, u32[]{:S(2)}, u32[]{:S(2)}) collective-permute-start(bf16[288,768]{1,0:T(8,128)(2,1)} %collective-permute-done.5.refs_0_), channel_id=1, source_target_pairs={{0,16},{1,3},{2,18},{3,1},{16,0},{17,19},{18,2},{19,17},{4,20},{5,... | collective-permute-start | bytes 1327112 | tf_op jit(solution)/shard_map/ppermute | solution.py:591
  58.9 18.2 %collective-permute-start.17 = (bf16[288,768]{1,0:T(8,128)(2,1)}, bf16[288,768]{1,0:T(8,128)(2,1)}, u32[]{:S(2)}, u32[]{:S(2)}) collective-permute-start(bf16[288,768]{1,0:T(8,128)(2,1)} %collective-permute-done.5.refs_0_), channel_id=1, source_target_pairs={{0,2},{1,17},{2,0},{3,19},{16,18},{17,1},{18,16},{19,3},{4,6},{5,2... | collective-permute-start | bytes 1327112 | tf_op jit(solution)/shard_map/ppermute | solution.py:591
  60.5 19.3 %collective-permute-start.19 = (bf16[288,768]{1,0:T(8,128)(2,1)}, bf16[288,768]{1,0:T(8,128)(2,1)}, u32[]{:S(2)}, u32[]{:S(2)}) collective-permute-start(bf16[288,768]{1,0:T(8,128)(2,1)} %collective-permute-done.5.refs_0_), channel_id=1, source_target_pairs={{0,1},{1,0},{2,3},{3,2},{4,5},{5,4},{6,7},{7,6},{8,9},{9,8},{10,11... | collective-permute-start | bytes 1327112 | tf_op jit(solution)/shard_map/ppermute | solution.py:580
  74.4 11.0 %collective-permute-start.18 = (bf16[288,768]{1,0:T(8,128)(2,1)}, bf16[288,768]{1,0:T(8,128)(2,1)S(1)}, u32[]{:S(2)}, u32[]{:S(2)}) collective-permute-start(bf16[288,768]{1,0:T(8,128)(2,1)} %collective-permute-done.16.refs_1_), channel_id=1, source_target_pairs={{0,2},{1,17},{2,0},{3,19},{16,18},{17,1},{18,16},{19,3},{4,6},{5,2... | collective-permute-start | bytes 1327112 | tf_op jit(solution)/shard_map/ppermute | solution.py:591
  76.4 13.9 %collective-permute-start.14 = (bf16[288,768]{1,0:T(8,128)(2,1)S(1)}, bf16[288,768]{1,0:T(8,128)(2,1)S(1)}, u32[]{:S(2)}, u32[]{:S(2)}) collective-permute-start(bf16[288,768]{1,0:T(8,128)(2,1)S(1)} %collective-permute-done.6.refs_0_), channel_id=1, source_target_pairs={{0,16},{1,3},{2,18},{3,1},{16,0},{17,19},{18,2},{19,17},{4,20},{5,... | collective-permute-start | bytes 1327112 | tf_op jit(solution)/shard_map/ppermute | solution.py:591
  77.0 22.7 %collective-permute-start.20 = (bf16[288,768]{1,0:T(8,128)(2,1)}, bf16[288,768]{1,0:T(8,128)(2,1)S(1)}, u32[]{:S(2)}, u32[]{:S(2)}) collective-permute-start(bf16[288,768]{1,0:T(8,128)(2,1)} %collective-permute-done.16.refs_1_), channel_id=1, source_target_pairs={{0,1},{1,0},{2,3},{3,2},{4,5},{5,4},{6,7},{7,6},{8,9},{9,8},{10,11... | collective-permute-start | bytes 1327112 | tf_op jit(solution)/shard_map/ppermute | solution.py:580
  77.1 29.2 %collective-permute-start.13 = (bf16[288,768]{1,0:T(8,128)(2,1)S(1)}, bf16[288,768]{1,0:T(8,128)(2,1)S(1)}, u32[]{:S(2)}, u32[]{:S(2)}) collective-permute-start(bf16[288,768]{1,0:T(8,128)(2,1)S(1)} %collective-permute-done.6.refs_0_), channel_id=1, source_target_pairs={{0,4},{4,8},{8,12},{12,0},{1,5},{5,9},{9,13},{13,1},{2,6},{6,10},{... | collective-permute-start | bytes 1327112 | tf_op jit(solution)/shard_map/ppermute | solution.py:660
  79.9 20.3 %collective-permute-start.21 = (bf16[288,768]{1,0:T(8,128)(2,1)}, bf16[288,768]{1,0:T(8,128)(2,1)}, u32[]{:S(2)}, u32[]{:S(2)}) collective-permute-start(bf16[288,768]{1,0:T(8,128)(2,1)} %collective-permute-done.17.refs_2_), channel_id=1, source_target_pairs={{0,1},{1,0},{2,3},{3,2},{4,5},{5,4},{6,7},{7,6},{8,9},{9,8},{10,11... | collective-permute-start | bytes 1327112 | tf_op jit(solution)/shard_map/ppermute | solution.py:580
  85.4 14.9 %collective-permute-start.22 = (bf16[288,768]{1,0:T(8,128)(2,1)S(1)}, bf16[288,768]{1,0:T(8,128)(2,1)}, u32[]{:S(2)}, u32[]{:S(2)}) collective-permute-start(bf16[288,768]{1,0:T(8,128)(2,1)S(1)} %collective-permute-done.18.refs_3_), channel_id=1, source_target_pairs={{0,1},{1,0},{2,3},{3,2},{4,5},{5,4},{6,7},{7,6},{8,9},{9,8},{10,11... | collective-permute-start | bytes 1327112 | tf_op jit(solution)/shard_map/ppermute | solution.py:580
  90.3 16.0 %collective-permute-start.15 = (bf16[288,768]{1,0:T(8,128)(2,1)S(1)}, bf16[288,768]{1,0:T(8,128)(2,1)S(1)}, u32[]{:S(2)}, u32[]{:S(2)}) collective-permute-start(bf16[288,768]{1,0:T(8,128)(2,1)S(1)} %collective-permute-done.14.refs_1_), channel_id=1, source_target_pairs={{0,2},{1,17},{2,0},{3,19},{16,18},{17,1},{18,16},{19,3},{4,6},{5,2... | collective-permute-start | bytes 1327112 | tf_op jit(solution)/shard_map/ppermute | solution.py:591
  99.8 15.7 %collective-permute-start.26 = (bf16[288,768]{1,0:T(8,128)(2,1)S(1)}, bf16[288,768]{1,0:T(8,128)(2,1)}, u32[]{:S(2)}, u32[]{:S(2)}) collective-permute-start(bf16[288,768]{1,0:T(8,128)(2,1)S(1)} %collective-permute-done.6.refs_0_), channel_id=1, source_target_pairs={{0,2},{1,17},{2,0},{3,19},{16,18},{17,1},{18,16},{19,3},{4,6},{5,2... | collective-permute-start | bytes 1327112 | tf_op jit(solution)/shard_map/ppermute | solution.py:591
  100.2 15.3 %collective-permute-start.27 = (bf16[288,768]{1,0:T(8,128)(2,1)S(1)}, bf16[288,768]{1,0:T(8,128)(2,1)S(1)}, u32[]{:S(2)}, u32[]{:S(2)}) collective-permute-start(bf16[288,768]{1,0:T(8,128)(2,1)S(1)} %collective-permute-done.6.refs_0_), channel_id=1, source_target_pairs={{0,1},{1,0},{2,3},{3,2},{4,5},{5,4},{6,7},{7,6},{8,9},{9,8},{10,11... | collective-permute-start | bytes 1327112 | tf_op jit(solution)/shard_map/ppermute | solution.py:580
  106.3 19.7 %collective-permute-start.23 = (bf16[288,768]{1,0:T(8,128)(2,1)S(1)}, bf16[288,768]{1,0:T(8,128)(2,1)S(1)}, u32[]{:S(2)}, u32[]{:S(2)}) collective-permute-start(bf16[288,768]{1,0:T(8,128)(2,1)S(1)} %collective-permute-done.13.refs_0_), channel_id=1, source_target_pairs={{0,16},{1,3},{2,18},{3,1},{16,0},{17,19},{18,2},{19,17},{4,20},{5,... | collective-permute-start | bytes 1327112 | tf_op jit(solution)/shard_map/ppermute | solution.py:591
  107.0 22.3 %collective-permute-start.28 = (bf16[288,768]{1,0:T(8,128)(2,1)S(1)}, bf16[288,768]{1,0:T(8,128)(2,1)}, u32[]{:S(2)}, u32[]{:S(2)}) collective-permute-start(bf16[288,768]{1,0:T(8,128)(2,1)S(1)} %collective-permute-done.14.refs_1_), channel_id=1, source_target_pairs={{0,1},{1,0},{2,3},{3,2},{4,5},{5,4},{6,7},{7,6},{8,9},{9,8},{10,11... | collective-permute-start | bytes 1327112 | tf_op jit(solution)/shard_map/ppermute | solution.py:580
  115.5 13.9 %collective-permute-start.29 = (bf16[288,768]{1,0:T(8,128)(2,1)}, bf16[288,768]{1,0:T(8,128)(2,1)}, u32[]{:S(2)}, u32[]{:S(2)}) collective-permute-start(bf16[288,768]{1,0:T(8,128)(2,1)} %collective-permute-done.26.refs_2_), channel_id=1, source_target_pairs={{0,1},{1,0},{2,3},{3,2},{4,5},{5,4},{6,7},{7,6},{8,9},{9,8},{10,11... | collective-permute-start | bytes 1327112 | tf_op jit(solution)/shard_map/ppermute | solution.py:580
  115.5 19.8 %collective-permute-start.24 = (bf16[288,768]{1,0:T(8,128)(2,1)S(1)}, bf16[288,768]{1,0:T(8,128)(2,1)}, u32[]{:S(2)}, u32[]{:S(2)}) collective-permute-start(bf16[288,768]{1,0:T(8,128)(2,1)S(1)} %collective-permute-done.13.refs_0_), channel_id=1, source_target_pairs={{0,2},{1,17},{2,0},{3,19},{16,18},{17,1},{18,16},{19,3},{4,6},{5,2... | collective-permute-start | bytes 1327112 | tf_op jit(solution)/shard_map/ppermute | solution.py:591
  115.5 19.8 %collective-permute-start.30 = (bf16[288,768]{1,0:T(8,128)(2,1)S(1)}, bf16[288,768]{1,0:T(8,128)(2,1)}, u32[]{:S(2)}, u32[]{:S(2)}) collective-permute-start(bf16[288,768]{1,0:T(8,128)(2,1)S(1)} %collective-permute-done.15.refs_3_), channel_id=1, source_target_pairs={{0,1},{1,0},{2,3},{3,2},{4,5},{5,4},{6,7},{7,6},{8,9},{9,8},{10,11... | collective-permute-start | bytes 1327112 | tf_op jit(solution)/shard_map/ppermute | solution.py:580
  126.0 15.7 %collective-permute-start.25 = (bf16[288,768]{1,0:T(8,128)(2,1)S(1)}, bf16[288,768]{1,0:T(8,128)(2,1)S(1)}, u32[]{:S(2)}, u32[]{:S(2)}) collective-permute-start(bf16[288,768]{1,0:T(8,128)(2,1)S(1)} %collective-permute-done.23.refs_1_), channel_id=1, source_target_pairs={{0,2},{1,17},{2,0},{3,19},{16,18},{17,1},{18,16},{19,3},{4,6},{5,2... | collective-permute-start | bytes 1327112 | tf_op jit(solution)/shard_map/ppermute | solution.py:591
  129.3 14.6 %collective-permute-start.31 = (bf16[288,768]{1,0:T(8,128)(2,1)S(1)}, bf16[288,768]{1,0:T(8,128)(2,1)S(1)}, u32[]{:S(2)}, u32[]{:S(2)}) collective-permute-start(bf16[288,768]{1,0:T(8,128)(2,1)S(1)} %collective-permute-done.13.refs_0_), channel_id=1, source_target_pairs={{0,1},{1,0},{2,3},{3,2},{4,5},{5,4},{6,7},{7,6},{8,9},{9,8},{10,11... | collective-permute-start | bytes 1327112 | tf_op jit(solution)/shard_map/ppermute | solution.py:580
  129.4 14.5 %collective-permute-start.32 = (bf16[288,768]{1,0:T(8,128)(2,1)S(1)}, bf16[288,768]{1,0:T(8,128)(2,1)}, u32[]{:S(2)}, u32[]{:S(2)}) collective-permute-start(bf16[288,768]{1,0:T(8,128)(2,1)S(1)} %collective-permute-done.23.refs_1_), channel_id=1, source_target_pairs={{0,1},{1,0},{2,3},{3,2},{4,5},{5,4},{6,7},{7,6},{8,9},{9,8},{10,11... | collective-permute-start | bytes 1327112 | tf_op jit(solution)/shard_map/ppermute | solution.py:580
  135.3 8.6 %collective-permute-start.33 = (bf16[288,768]{1,0:T(8,128)(2,1)}, bf16[288,768]{1,0:T(8,128)(2,1)}, u32[]{:S(2)}, u32[]{:S(2)}) collective-permute-start(bf16[288,768]{1,0:T(8,128)(2,1)} %collective-permute-done.24.refs_2_), channel_id=1, source_target_pairs={{0,1},{1,0},{2,3},{3,2},{4,5},{5,4},{6,7},{7,6},{8,9},{9,8},{10,11... | collective-permute-start | bytes 1327112 | tf_op jit(solution)/shard_map/ppermute | solution.py:580
  164.4 13.0 %all-to-all-start.1 = ((bf16[4,3,96,256]{3,2,1,0:T(8,128)(2,1)}), bf16[4,3,96,256]{3,2,1,0:T(8,128)(2,1)S(1)}, u32[]{:S(2)}, u32[]{:S(2)}) async-start(bf16[4,3,96,256]{3,2,1,0:T(8,128)(2,1)} %attend_forward.1), calls=%async_computation.1 | async-start | bytes 1179648 | tf_op jit(solution)/shard_map/all_to_all | solution.py:692
  203.5 9.3 %collective-permute-start.35 = (bf16[384,7040]{1,0:T(8,128)(2,1)}, bf16[384,7040]{1,0:T(8,128)(2,1)}, u32[]{:S(2)}, u32[]{:S(2)}) collective-permute-start(bf16[384,7040]{1,0:T(8,128)(2,1)} %get-tuple-element.80), channel_id=1, source_target_pairs={{0,1},{1,0},{2,3},{3,2},{4,5},{5,4},{6,7},{7,6},{8,9},{9,8},{10,11... | collective-permute-start | bytes 16220168 | tf_op jit(solution)/shard_map/ppermute | solution.py:580
  203.5 15.2 %all-to-all-start.2 = ((bf16[4,3,96,256]{3,2,1,0:T(8,128)(2,1)}), bf16[4,3,96,256]{3,2,1,0:T(8,128)(2,1)S(1)}, u32[]{:S(2)}, u32[]{:S(2)}) async-start(bf16[4,3,96,256]{3,2,1,0:T(8,128)(2,1)} %bitcast.137), calls=%async_computation.2 | async-start | bytes 1179648 | tf_op jit(solution)/shard_map/all_to_all | solution.py:711
  218.7 34.3 %collective-permute-start.39 = (bf16[192,7040]{1,0:T(8,128)(2,1)}, bf16[192,7040]{1,0:T(8,128)(2,1)}, u32[]{:S(2)}, u32[]{:S(2)}) collective-permute-start(bf16[192,7040]{1,0:T(8,128)(2,1)} %get-tuple-element.84), channel_id=1, source_target_pairs={{0,16},{1,3},{2,18},{3,1},{16,0},{17,19},{18,2},{19,17},{4,20},{5,... | collective-permute-start | bytes 8110088 | tf_op jit(solution)/shard_map/ppermute | solution.py:591
  219.5 16.9 %collective-permute-start.36 = (bf16[4,3,96,256]{3,2,1,0:T(8,128)(2,1)S(1)}, bf16[4,3,96,256]{3,2,1,0:T(8,128)(2,1)}, u32[]{:S(2)}, u32[]{:S(2)}) collective-permute-start(bf16[4,3,96,256]{3,2,1,0:T(8,128)(2,1)S(1)} %all-to-all-done.2.load_ref), channel_id=1, source_target_pairs={{0,4},{4,8},{8,12},{12,0},{1,5},{5,9},{9,13},{13,1},{2,6},{6,10},{... | collective-permute-start | bytes 1769480 | tf_op jit(solution)/shard_map/ppermute | solution.py:721
  236.3 16.6 %collective-permute-start.37 = (bf16[4,3,96,256]{3,2,1,0:T(8,128)(2,1)}, bf16[4,3,96,256]{3,2,1,0:T(8,128)(2,1)S(1)}, u32[]{:S(2)}, u32[]{:S(2)}) collective-permute-start(bf16[4,3,96,256]{3,2,1,0:T(8,128)(2,1)} %collective-permute-done.36.load_ref), channel_id=1, source_target_pairs={{0,4},{4,8},{8,12},{12,0},{1,5},{5,9},{9,13},{13,1},{2,6},{6,10},{... | collective-permute-start | bytes 1769480 | tf_op jit(solution)/shard_map/ppermute | solution.py:721
  255.9 43.2 %collective-permute-start.43 = (bf16[96,7040]{1,0:T(8,128)(2,1)}, bf16[96,7040]{1,0:T(8,128)(2,1)}, u32[]{:S(2)}, u32[]{:S(2)}) collective-permute-start(bf16[96,7040]{1,0:T(8,128)(2,1)} %add_convert_fusion.5), channel_id=1, source_target_pairs={{0,2},{1,17},{2,0},{3,19},{16,18},{17,1},{18,16},{19,3},{4,6},{5,2... | collective-permute-start | bytes 4055048 | tf_op jit(solution)/shard_map/ppermute | solution.py:591
  259.2 22.9 %collective-permute-start.38 = (bf16[4,3,96,256]{3,2,1,0:T(8,128)(2,1)S(1)}, bf16[4,3,96,256]{3,2,1,0:T(8,128)(2,1)S(1)}, u32[]{:S(2)}, u32[]{:S(2)}) collective-permute-start(bf16[4,3,96,256]{3,2,1,0:T(8,128)(2,1)S(1)} %collective-permute-done.37.load_ref), channel_id=1, source_target_pairs={{0,4},{4,8},{8,12},{12,0},{1,5},{5,9},{9,13},{13,1},{2,6},{6,10},{... | collective-permute-start | bytes 1769480 | tf_op jit(solution)/shard_map/ppermute | solution.py:721
  299.1 9.1 %collective-permute-start.40 = (bf16[2,2,288,768]{3,2,1,0:T(8,128)(2,1)}, bf16[2,2,288,768]{3,2,1,0:T(8,128)(2,1)S(1)}, u32[]{:S(2)}, u32[]{:S(2)}) collective-permute-start(bf16[2,2,288,768]{3,2,1,0:T(8,128)(2,1)} %get-tuple-element.89), channel_id=1, source_target_pairs={{0,1},{1,0},{2,3},{3,2},{4,5},{5,4},{6,7},{7,6},{8,9},{9,8},{10,11... | collective-permute-start | bytes 5308424 | tf_op jit(solution)/shard_map/ppermute | solution.py:580
  302.5 12.2 %collective-permute-start.44 = (bf16[24,7040]{1,0:T(8,128)(2,1)}, bf16[24,7040]{1,0:T(8,128)(2,1)S(1)}, u32[]{:S(2)}, u32[]{:S(2)}) collective-permute-start(bf16[24,7040]{1,0:T(8,128)(2,1)} %get-tuple-element.162), channel_id=1, source_target_pairs={{0,4},{4,8},{8,12},{12,0},{1,5},{5,9},{9,13},{13,1},{2,6},{6,10},{... | collective-permute-start | bytes 1013768 | tf_op jit(solution)/shard_map/ppermute | solution.py:740
  302.5 40.2 %collective-permute-start.45 = (bf16[24,7040]{1,0:T(8,128)(2,1)}, bf16[24,7040]{1,0:T(8,128)(2,1)}, u32[]{:S(2)}, u32[]{:S(2)}) collective-permute-start(bf16[24,7040]{1,0:T(8,128)(2,1)} %get-tuple-element.164), channel_id=1, source_target_pairs={{0,8},{4,12},{8,0},{12,4},{1,9},{5,13},{9,1},{13,5},{2,10},{6,14},... | collective-permute-start | bytes 1013768 | tf_op jit(solution)/shard_map/ppermute | solution.py:740
  308.0 40.5 %collective-permute-start.46 = (bf16[24,7040]{1,0:T(8,128)(2,1)S(1)}, bf16[24,7040]{1,0:T(8,128)(2,1)}, u32[]{:S(2)}, u32[]{:S(2)}) collective-permute-start(bf16[24,7040]{1,0:T(8,128)(2,1)S(1)} %get-tuple-element.163), channel_id=1, source_target_pairs={{0,12},{4,0},{8,4},{12,8},{1,13},{5,1},{9,5},{13,9},{2,14},{6,2},{... | collective-permute-start | bytes 1013768 | tf_op jit(solution)/shard_map/ppermute | solution.py:740
  309.7 41.1 %collective-permute-start.41 = (bf16[2,288,768]{2,1,0:T(8,128)(2,1)}, bf16[2,288,768]{2,1,0:T(8,128)(2,1)}, u32[]{:S(2)}, u32[]{:S(2)}) collective-permute-start(bf16[2,288,768]{2,1,0:T(8,128)(2,1)} %slice_bitcast_fusion), channel_id=1, source_target_pairs={{0,16},{1,3},{2,18},{3,1},{16,0},{17,19},{18,2},{19,17},{4,20},{5,... | collective-permute-start | bytes 2654216 | tf_op jit(solution)/shard_map/ppermute | solution.py:591
  309.8 53.9 %all-to-all-start.3 = ((bf16[32,24,640]{2,1,0:T(8,128)(2,1)}), bf16[32,24,640]{2,1,0:T(8,128)(2,1)S(1)}, u32[]{:S(2)}, u32[]{:S(2)}) async-start(bf16[32,24,640]{2,1,0:T(8,128)(2,1)} %bitcast.136), calls=%async_computation.3 | async-start | bytes 1966080 | tf_op jit(solution)/shard_map/all_to_all | solution.py:745
  351.9 9.5 %collective-permute-start.42 = (bf16[288,768]{1,0:T(8,128)(2,1)S(1)}, bf16[288,768]{1,0:T(8,128)(2,1)}, u32[]{:S(2)}, u32[]{:S(2)}) collective-permute-start(bf16[288,768]{1,0:T(8,128)(2,1)S(1)} %fusion), channel_id=1, source_target_pairs={{0,2},{1,17},{2,0},{3,19},{16,18},{17,1},{18,16},{19,3},{4,6},{5,2... | collective-permute-start | bytes 1327112 | tf_op jit(solution)/shard_map/ppermute | solution.py:591
  (39 other events, 457.2 us)
Sparse Core Ops, SparseCore 0:
  36.5 116.1 all-gather.1

commit v5 on v4

--- a/solution.py
+++ b/solution.py
@@ -734,17 +734,20 @@
             before = after(before, high2)
         done.append(attend_key(q_all, moving, kv, pair, begin, ends_k[:, :, -1].reshape(-1), where, ends_k[:, :, None], before))
 
-    summed = stay[:part].astype(F32)
+    moved = []
     for j in range(1, ring):
         along = [(i, (i + j) % ring) for i in range(ring)]
-        summed = summed + lax.ppermute(stay[j * part : (j + 1) * part], "r", along).astype(F32)
+        moved.append(lax.ppermute(stay[j * part : (j + 1) * part], "r", along))
     spot = jnp.concatenate([jnp.stack([me_u, me_y, me_c]), (pair == me_u).astype(jnp.int32)])
     keep, send, dw = tail(spot.astype(jnp.int32), dq, done[-1], w_here, x_near[0] + x_near[1], part)
     keep = add(keep, swap_c(send))
-    dw = after(dw, keep)
+    dw = after(dw, keep, moved[0])
     got = lax.all_to_all(dw.reshape(devices, part, 640), ALL, split_axis=0, concat_axis=0, tiled=True)
     came = cross_one(keep[1])
     onward = add(keep[0, 1], came[1])
+    summed = stay[:part].astype(F32) + moved[0].astype(F32)
+    for m in moved[1:]:
+        summed = summed + after(m, onward).astype(F32)
     final = cross_two(onward)
     grad_w_in, grad_w_down, grad_w_out, flat = finish([after(summed, onward)], fold, width)
     grad_w_down = grad_w_down.reshape(fold * part, width)

time: 382 us -> 384 us (level)
  the two profiles are of different devices: /device:TPU:8 before, /device:TPU:0 now
where the time goes in v5:
time: 384 us; the launch traced here: 376 us
  Pallas kernels  122 us (32%)
  waiting for transfers between devices  105 us (27%)
  starting transfers between devices  76.8 us (20%)
  other arithmetic  31.5 us (8%)
  local copies, waits for them, and re-layouts  26.1 us (7%)
  between operations  15.2 us (4%)
    ppermute x16, waiting for transfers between devices, crossing(): return lambda v: lax.ppermute(v, ('u', 'y', 'c'), pairs)  40.7 us
    pallas_call x4, Pallas kernels, attend_key(): pl.pallas_call(functools.partial(key_kernel, rows), grid_spec=pltpu.Prefe...  29 us
    pallas_call x1, Pallas kernels, dense_layers(): pl.pallas_call(functools.partial(dense_kernel, fold), in_specs=[local, lo...  25.2 us
    pallas_call x4, Pallas kernels, project(): pl.pallas_call(functools.partial(project_kernel, seqs, rows, not extra),...  24.1 us
    ppermute x16, starting transfers between devices, crossing(): return lambda v: lax.ppermute(v, ('u', 'y', 'c'), pairs)  20.7 us
    ppermute x19, starting transfers between devices, swap_on(): return lambda v: lax.ppermute(v, axis, [(0, 1), (1, 0)])  15.8 us
    ppermute x3, waiting for transfers between devices, per_device(): moving = lax.ppermute(moving, 'r', forward)  15.2 us
    pallas_call x1, Pallas kernels, attend_query(): pl.pallas_call(functools.partial(query_kernel, rows, shards), grid_spec=p...  14.7 us
  transfers between devices with their start and end apart: 52, of which 18 were waited for; matrix products, arithmetic and copies ran while one was open for 13% of the time, Pallas kernels for 25%

profile of v5, /device:TPU:0, one launch (start us, length us, event | category | flops | bytes accessed | tf_op | source)
XLA Modules:
  0.0 376.2 jit_solution(8291602492626976591)
XLA Ops:
  7.2 3.0 collective-permute-start.3
  15.0 3.3 all-to-all-start
  24.9 2.6 collective-permute-start.1
  28.9 2.4 collective-permute-done
  31.4 4.8 %collective-permute-done.1 = bf16[4,24,640]{2,1,0:T(8,128)(2,1)S(1)} collective-permute-done((bf16[4,24,640]{2,1,0:T(8,128)(2,1)S(1)}, bf16[4,24,640]{2,1,0:T(8,128)(2,1)S(1)}, u32[]{:S(2)}, u32[]{:S(2)}) %collective-permute-start.1) | collective-permute-done | bytes 122912 | tf_op jit(solution)/shard_map/ppermute | solution.py:640
  37.6 3.1 collective-permute-start.5
  43.2 7.4 %collective-permute-done.7.refs_3_ = bf16[288,768]{1,0:T(8,128)(2,1)} collective-permute-done((bf16[288,768]{1,0:T(8,128)(2,1)S(1)}, bf16[288,768]{1,0:T(8,128)(2,1)}, u32[]{:S(2)}, u32[]{:S(2)}) %collective-permute-start.7) | collective-permute-done | bytes 442400 | tf_op jit(solution)/shard_map/ppermute | solution.py:591
  50.6 6.6 %collective-permute-start.10 = (bf16[288,768]{1,0:T(8,128)(2,1)S(1)}, bf16[288,768]{1,0:T(8,128)(2,1)}, u32[]{:S(2)}, u32[]{:S(2)}) collective-permute-start(bf16[288,768]{1,0:T(8,128)(2,1)S(1)} %collective-permute-done.4.refs_2_), channel_id=1, source_target_pairs={{0,1},{1,0},{2,3},{3,2},{4,5},{5,4},{6,7},{7,6},{8,9},{9,8},{10,11... | collective-permute-start | bytes 1327112 | tf_op jit(solution)/shard_map/ppermute | solution.py:580
  57.2 3.3 collective-permute-start.6
  64.2 5.7 %project.4 = (bf16[2,4,4,3,96,384]{5,4,3,2,1,0:T(8,128)(2,1)}, bf16[4,4,3,96,384]{4,3,2,1,0:T(8,128)(2,1)}) custom-call(s32[4]{0:T(128)} %get-tuple-element.192.spot_ref, bf16[288,768]{1,0:T(8,128)(2,1)} %bitcast.141, bf16[288,768]{1,0:T(8,128)(2,1)} %copy-done.9, bf16[288,768]{1,0:T(8,128)(2,1)} %copy-done.10, ...), custom_call_target="tpu_custom_call" | custom-call | flops 2038431744 | bytes 12582912 | tf_op jit(solution)/shard_map/project/pallas_call | solution.py:204
  69.9 5.1 %collective-permute-done.6.refs_0_ = bf16[288,768]{1,0:T(8,128)(2,1)S(1)} collective-permute-done((bf16[288,768]{1,0:T(8,128)(2,1)}, bf16[288,768]{1,0:T(8,128)(2,1)S(1)}, u32[]{:S(2)}, u32[]{:S(2)}) %collective-permute-start.6) | collective-permute-done | bytes 442400 | tf_op jit(solution)/shard_map/ppermute | solution.py:660
  75.0 1.8 collective-permute-done.16.refs_1_
  76.9 4.0 %collective-permute-start.18 = (bf16[288,768]{1,0:T(8,128)(2,1)}, bf16[288,768]{1,0:T(8,128)(2,1)S(1)}, u32[]{:S(2)}, u32[]{:S(2)}) collective-permute-start(bf16[288,768]{1,0:T(8,128)(2,1)} %collective-permute-done.16.refs_1_), channel_id=1, source_target_pairs={{0,2},{1,17},{2,0},{3,19},{16,18},{17,1},{18,16},{19,3},{4,6},{5,2... | collective-permute-start | bytes 1327112 | tf_op jit(solution)/shard_map/ppermute | solution.py:591
  82.1 5.5 %collective-permute-done.18.refs_3_ = bf16[288,768]{1,0:T(8,128)(2,1)S(1)} collective-permute-done((bf16[288,768]{1,0:T(8,128)(2,1)}, bf16[288,768]{1,0:T(8,128)(2,1)S(1)}, u32[]{:S(2)}, u32[]{:S(2)}) %collective-permute-start.18) | collective-permute-done | bytes 442400 | tf_op jit(solution)/shard_map/ppermute | solution.py:591
  87.6 4.4 %collective-permute-start.22 = (bf16[288,768]{1,0:T(8,128)(2,1)S(1)}, bf16[288,768]{1,0:T(8,128)(2,1)}, u32[]{:S(2)}, u32[]{:S(2)}) collective-permute-start(bf16[288,768]{1,0:T(8,128)(2,1)S(1)} %collective-permute-done.18.refs_3_), channel_id=1, source_target_pairs={{0,1},{1,0},{2,3},{3,2},{4,5},{5,4},{6,7},{7,6},{8,9},{9,8},{10,11... | collective-permute-start | bytes 1327112 | tf_op jit(solution)/shard_map/ppermute | solution.py:580
  94.7 7.8 %convert_reduce_fusion = s32[3,2,1536]{2,1,0:T(2,128)S(1)} fusion(s32[3,1536]{1,0:T(4,128)S(1)} %bitcast.151, s32[3,2,1536]{2,1,0:T(2,128)S(1)} %le.17), kind=kLoop, calls=%fused_computation | loop fusion | flops 42458112 | bytes 92160 | tf_op jit(solution)/shard_map/reduce_sum | solution.py:682
  103.3 6.6 %project.5 = (bf16[2,4,4,3,96,384]{5,4,3,2,1,0:T(8,128)(2,1)}, bf16[4,4,3,96,384]{4,3,2,1,0:T(8,128)(2,1)}) custom-call(s32[4]{0:T(128)} %get-tuple-element.191.spot_ref, bf16[288,768]{1,0:T(8,128)(2,1)} %collective-permute-done.5.refs_0_, bf16[288,768]{1,0:T(8,128)(2,1)} %collective-permute-done.16.refs_1_, ...), custom_call_target="tpu_custom_call", output_to_operand_aliasing={{0}: (11, {}), {1}: (12, {})} | custom-call | flops 2038431744 | bytes 12582912 | tf_op jit(solution)/shard_map/project/pallas_call | solution.py:204
  111.7 9.5 %collective-permute-done.26.refs_2_ = bf16[288,768]{1,0:T(8,128)(2,1)} collective-permute-done((bf16[288,768]{1,0:T(8,128)(2,1)S(1)}, bf16[288,768]{1,0:T(8,128)(2,1)}, u32[]{:S(2)}, u32[]{:S(2)}) %collective-permute-start.26) | collective-permute-done | bytes 442400 | tf_op jit(solution)/shard_map/ppermute | solution.py:591
  123.8 5.2 %collective-permute-done.23.refs_1_ = bf16[288,768]{1,0:T(8,128)(2,1)S(1)} collective-permute-done((bf16[288,768]{1,0:T(8,128)(2,1)S(1)}, bf16[288,768]{1,0:T(8,128)(2,1)S(1)}, u32[]{:S(2)}, u32[]{:S(2)}) %collective-permute-start.23) | collective-permute-done | bytes 442400 | tf_op jit(solution)/shard_map/ppermute | solution.py:591
  132.6 7.2 %collective-permute-done.24.refs_2_ = bf16[288,768]{1,0:T(8,128)(2,1)} collective-permute-done((bf16[288,768]{1,0:T(8,128)(2,1)S(1)}, bf16[288,768]{1,0:T(8,128)(2,1)}, u32[]{:S(2)}, u32[]{:S(2)}) %collective-permute-start.24) | collective-permute-done | bytes 442400 | tf_op jit(solution)/shard_map/ppermute | solution.py:591
  139.8 6.0 %project.6 = (bf16[2,4,4,3,96,384]{5,4,3,2,1,0:T(8,128)(2,1)}, bf16[4,4,3,96,384]{4,3,2,1,0:T(8,128)(2,1)}) custom-call(s32[4]{0:T(128)} %get-tuple-element.162.spot_ref, bf16[288,768]{1,0:T(8,128)(2,1)} %copy-done.11, bf16[288,768]{1,0:T(8,128)(2,1)} %copy-done.13, ...), custom_call_target="tpu_custom_call", output_to_operand_aliasing={{0}: (11, {}), {1}: (12, {})} | custom-call | flops 2038431744 | bytes 12582912 | tf_op jit(solution)/shard_map/project/pallas_call | solution.py:204
  149.3 5.7 %project.7 = (bf16[2,4,4,3,96,384]{5,4,3,2,1,0:T(8,128)(2,1)}, bf16[4,4,3,96,384]{4,3,2,1,0:T(8,128)(2,1)}) custom-call(s32[4]{0:T(128)} %get-tuple-element.193.spot_ref, bf16[288,768]{1,0:T(8,128)(2,1)} %copy-done.12, bf16[288,768]{1,0:T(8,128)(2,1)} %copy-done.15, ...), custom_call_target="tpu_custom_call", output_to_operand_aliasing={{0}: (11, {}), {1}: (12, {})} | custom-call | flops 2038431744 | bytes 12582912 | tf_op jit(solution)/shard_map/project/pallas_call | solution.py:204
  155.1 13.8 %attend_forward.1 = bf16[4,3,96,256]{3,2,1,0:T(8,128)(2,1)} custom-call(s32[3]{0:T(128)} %copy-done.29, s32[9]{0:T(128)} %max.8.begin_ref, s32[10]{0:T(128)} %pad_add_fusion.last_ref, bf16[16,3,96,384]{3,2,1,0:T(8,128)(2,1)} %bitcast.120, bf16[2,16,3,96,384]{4,3,2,1,0:T(8,128)(2,1)} %bitcast.102, bf16[2,16,3,96,384]{4,3,2,1,0:T(8,128)(2,1)} %bitcast.103, ...), custom_call_target="tpu_custom_call" | custom-call | flops 2717908992 | bytes 12582912 | tf_op jit(solution)/shard_map/attend_forward/pallas_call | solution.py:234
  168.9 3.6 all-to-all-start.1
  172.6 9.3 %all-to-all-done.1 = bf16[4,3,96,256]{3,2,1,0:T(8,128)(2,1)S(1)} async-done(((bf16[4,3,96,256]{3,2,1,0:T(8,128)(2,1)}), bf16[4,3,96,256]{3,2,1,0:T(8,128)(2,1)S(1)}, u32[]{:S(2)}, u32[]{:S(2)}) %all-to-all-start.1) | async-done | bytes 589856 | tf_op jit(solution)/shard_map/all_to_all | solution.py:692
  182.8 25.2 %dense_layers.1 = (bf16[288,768]{1,0:T(8,128)(2,1)}, bf16[4,288,256]{2,1,0:T(8,128)(2,1)}, f32[288,768]{1,0:T(8,128)}, bf16[384,7040]{1,0:T(8,128)(2,1)}, bf16[384,7040]{1,0:T(8,128)(2,1)}) custom-call(bf16[4,288,256]{2,1,0:T(8,128)(2,1)} %bitcast.138, bf16[288,768]{1,0:T(8,128)(2,1)} %bitcast.142, bf16[288,768]{1,0:T(8,128)(2,1)} %bitcast.152, ...), custom_call_target="tpu_custom_call" | custom-call | flops 9172942848 | bytes 25165824 | tf_op jit(solution)/shard_map/dense_layers/pallas_call | solution.py:409
  208.0 3.5 all-to-all-start.2
  211.5 5.7 %collective-permute-done.35 = bf16[384,7040]{1,0:T(8,128)(2,1)} collective-permute-done((bf16[384,7040]{1,0:T(8,128)(2,1)}, bf16[384,7040]{1,0:T(8,128)(2,1)}, u32[]{:S(2)}, u32[]{:S(2)}) %collective-permute-start.35) | collective-permute-done | bytes 5406752 | tf_op jit(solution)/shard_map/ppermute | solution.py:580
  217.2 5.9 %add_convert_fusion = (bf16[192,7040]{1,0:T(8,128)(2,1)S(1)}, bf16[192,7040]{1,0:T(8,128)(2,1)}) fusion(bf16[384,7040]{1,0:T(8,128)(2,1)} %collective-permute-done.35, bf16[384,7040]{1,0:T(8,128)(2,1)} %get-tuple-element.81), kind=kLoop, calls=%fused_computation.1 | loop fusion | flops 10813440 | bytes 16220160 | tf_op jit(solution)/shard_map/convert_element_type | solution.py:599
  227.0 7.2 %attend_key.4.old_ref = f32[4,3,96,384]{3,2,1,0:T(8,128)} custom-call(s32[3]{0:T(128)} %copy-done.29, s32[9]{0:T(128)} %max.8.begin_ref, s32[9]{0:T(128)} %reshape_squeeze.20.reach_ref, s32[3]{0:T(128)} %get-tuple-element.190.place_ref, bf16[16,3,96,384]{3,2,1,0:T(8,128)(2,1)} %bitcast.121, ...), custom_call_target="tpu_custom_call", output_to_operand_aliasing={{}: (10, {})} | custom-call | flops 1358954496 | bytes 8388608 | tf_op jit(solution)/shard_map/attend_key/pallas_call | solution.py:280
  234.3 6.6 %collective-permute-done.36.load_ref = bf16[4,3,96,256]{3,2,1,0:T(8,128)(2,1)} collective-permute-done((bf16[4,3,96,256]{3,2,1,0:T(8,128)(2,1)S(1)}, bf16[4,3,96,256]{3,2,1,0:T(8,128)(2,1)}, u32[]{:S(2)}, u32[]{:S(2)}) %collective-permute-start.36) | collective-permute-done | bytes 589856 | tf_op jit(solution)/shard_map/ppermute | solution.py:721
  241.7 7.2 %attend_key.5.old_ref = f32[4,3,96,384]{3,2,1,0:T(8,128)} custom-call(s32[3]{0:T(128)} %copy-done.29, s32[9]{0:T(128)} %max.8.begin_ref, s32[9]{0:T(128)} %reshape_squeeze.22.reach_ref, s32[3]{0:T(128)} %get-tuple-element.188.place_ref, bf16[16,3,96,384]{3,2,1,0:T(8,128)(2,1)} %bitcast.122, ...), custom_call_target="tpu_custom_call", output_to_operand_aliasing={{}: (10, {})} | custom-call | flops 1358954496 | bytes 8388608 | tf_op jit(solution)/shard_map/attend_key/pallas_call | solution.py:280
  248.9 8.6 %collective-permute-done.37.load_ref = bf16[4,3,96,256]{3,2,1,0:T(8,128)(2,1)S(1)} collective-permute-done((bf16[4,3,96,256]{3,2,1,0:T(8,128)(2,1)}, bf16[4,3,96,256]{3,2,1,0:T(8,128)(2,1)S(1)}, u32[]{:S(2)}, u32[]{:S(2)}) %collective-permute-start.37) | collective-permute-done | bytes 589856 | tf_op jit(solution)/shard_map/ppermute | solution.py:721
  257.5 2.9 add_convert_fusion.5
  264.3 14.7 %attend_query.1.dq_ref = bf16[4,3,96,192]{3,2,1,0:T(8,128)(2,1)} custom-call(s32[3]{0:T(128)} %copy-done.29, s32[9]{0:T(128)} %max.8.begin_ref, s32[10]{0:T(128)} %pad_add_fusion.last_ref, bf16[16,3,96,384]{3,2,1,0:T(8,128)(2,1)} %bitcast.123, bf16[2,16,3,96,384]{4,3,2,1,0:T(8,128)(2,1)} %bitcast.111, bf16[2,16,3,96,384]{4,3,2,1,0:T(8,128)(2,1)} %bitcast.112, ...), custom_call_target="tpu_custom_call" | custom-call | flops 4076863488 | bytes 12582912 | tf_op jit(solution)/shard_map/attend_query/pallas_call | solution.py:255
  278.9 7.2 %attend_key.6.old_ref = f32[4,3,96,384]{3,2,1,0:T(8,128)} custom-call(s32[3]{0:T(128)} %copy-done.29, s32[9]{0:T(128)} %max.8.begin_ref, s32[9]{0:T(128)} %reshape_squeeze.23.reach_ref, s32[3]{0:T(128)} %get-tuple-element.158.place_ref, bf16[16,3,96,384]{3,2,1,0:T(8,128)(2,1)} %bitcast.124, ...), custom_call_target="tpu_custom_call", output_to_operand_aliasing={{}: (10, {})} | custom-call | flops 1358954496 | bytes 8388608 | tf_op jit(solution)/shard_map/attend_key/pallas_call | solution.py:280
  287.0 7.4 %attend_key.7.dkv_ref = f32[4,3,96,384]{3,2,1,0:T(8,128)} custom-call(s32[3]{0:T(128)} %copy-done.29, s32[9]{0:T(128)} %max.8.begin_ref, s32[9]{0:T(128)} %reshape_squeeze.21.reach_ref, s32[3]{0:T(128)} %get-tuple-element.189.place_ref, bf16[16,3,96,384]{3,2,1,0:T(8,128)(2,1)} %bitcast.125, ...), custom_call_target="tpu_custom_call", output_to_operand_aliasing={{}: (10, {})} | custom-call | flops 1358954496 | bytes 8388608 | tf_op jit(solution)/shard_map/attend_key/pallas_call | solution.py:280
  294.4 9.0 %tail.1 = (bf16[2,2,288,768]{3,2,1,0:T(8,128)(2,1)}, bf16[2,2,288,768]{3,2,1,0:T(8,128)(2,1)}, bf16[768,640]{1,0:T(8,128)(2,1)}) custom-call(s32[6]{0:T(128)} %pad_add_fusion.6.spot_ref, bf16[4,3,96,192]{3,2,1,0:T(8,128)(2,1)} %attend_query.1.dq_ref, f32[4,3,96,384]{3,2,1,0:T(8,128)} %attend_key.7.dkv_ref, bf16[768,640]{1,0:T(8,128)(2,1)} %bitcast.131, ...), custom_call_target="tpu_custom_call" | custom-call | flops 1698693120 | bytes 16777216 | tf_op jit(solution)/shard_map/tail/pallas_call | solution.py:485
  303.4 2.3 add_convert_fusion.3
  309.6 2.3 collective-permute-start.45
  313.5 8.9 %collective-permute-done.44 = bf16[24,7040]{1,0:T(8,128)(2,1)S(1)} collective-permute-done((bf16[24,7040]{1,0:T(8,128)(2,1)S(1)}, bf16[24,7040]{1,0:T(8,128)(2,1)S(1)}, u32[]{:S(2)}, u32[]{:S(2)}) %collective-permute-start.44) | collective-permute-done | bytes 337952 | tf_op jit(solution)/shard_map/ppermute | solution.py:740
  322.3 13.9 %all-to-all-start.3 = ((bf16[32,24,640]{2,1,0:T(8,128)(2,1)}), bf16[32,24,640]{2,1,0:T(8,128)(2,1)S(1)}, u32[]{:S(2)}, u32[]{:S(2)}) async-start(bf16[32,24,640]{2,1,0:T(8,128)(2,1)} %bitcast.136), calls=%async_computation.3 | async-start | bytes 1966080 | tf_op jit(solution)/shard_map/all_to_all | solution.py:745
  339.2 2.2 convert_add_fusion.3.refs_0_
  341.4 3.8 %finish.1 = (f32[24,3072]{1,0:T(8,128)}, f32[4,24,768]{2,1,0:T(8,128)}, f32[24,768]{1,0:T(8,128)}, f32[24,128]{1,0:T(8,128)}) custom-call(f32[24,7040]{1,0:T(8,128)} %convert_add_fusion.3.refs_0_), custom_call_target="tpu_custom_call" | custom-call | flops 134217728 | bytes 2097152 | tf_op jit(solution)/shard_map/finish/pallas_call | solution.py:532
  348.1 2.8 collective-permute-done.42
  350.9 2.4 fusion.2
  353.2 11.2 %all-to-all-done.3 = bf16[32,24,640]{2,1,0:T(8,128)(2,1)S(1)} async-done(((bf16[32,24,640]{2,1,0:T(8,128)(2,1)}), bf16[32,24,640]{2,1,0:T(8,128)(2,1)S(1)}, u32[]{:S(2)}, u32[]{:S(2)}) %all-to-all-start.3) | async-done | bytes 983072 | tf_op jit(solution)/shard_map/all_to_all | solution.py:745
  365.4 2.1 assemble.1
  (243 shorter events, 60.1 us)
Async XLA Ops:
  7.2 29.1 %collective-permute-start.3 = (bf16[288,768]{1,0:T(8,128)(2,1)}, bf16[288,768]{1,0:T(8,128)(2,1)S(1)}, u32[]{:S(2)}, u32[]{:S(2)}) collective-permute-start(bf16[288,768]{1,0:T(8,128)(2,1)} %bitcast.139), channel_id=1, source_target_pairs={{0,16},{1,3},{2,18},{3,1},{16,0},{17,19},{18,2},{19,17},{4,20},{5,... | collective-permute-start | bytes 1327112 | tf_op jit(solution)/shard_map/ppermute | solution.py:591
  10.2 26.1 %collective-permute-start.4 = (bf16[288,768]{1,0:T(8,128)(2,1)}, bf16[288,768]{1,0:T(8,128)(2,1)S(1)}, u32[]{:S(2)}, u32[]{:S(2)}) collective-permute-start(bf16[288,768]{1,0:T(8,128)(2,1)} %bitcast.140), channel_id=1, source_target_pairs={{0,2},{1,17},{2,0},{3,19},{16,18},{17,1},{18,16},{19,3},{4,6},{5,2... | collective-permute-start | bytes 1327112 | tf_op jit(solution)/shard_map/ppermute | solution.py:591
  15.0 8.3 %all-to-all-start = ((bf16[4,24,640]{2,1,0:T(8,128)(2,1)}), bf16[4,24,640]{2,1,0:T(8,128)(2,1)S(1)}, u32[]{:S(2)}, u32[]{:S(2)}) async-start(bf16[4,24,640]{2,1,0:T(8,128)(2,1)} %pad_maximum_fusion), calls=%async_computation | async-start | bytes 245760 | tf_op jit(solution)/shard_map/all_to_all | solution.py:637
  18.4 163.6 %all-gather.2.cloned.1.call-start = ((), (), s32[]{:S(2)}) async-start(), calls=%async_computation.4 | async-start | bytes 11151360 | tf_op jit(solution)/shard_map/all_gather | solution.py:644
  24.9 11.3 %collective-permute-start.1 = (bf16[4,24,640]{2,1,0:T(8,128)(2,1)S(1)}, bf16[4,24,640]{2,1,0:T(8,128)(2,1)S(1)}, u32[]{:S(2)}, u32[]{:S(2)}) collective-permute-start(bf16[4,24,640]{2,1,0:T(8,128)(2,1)S(1)} %all-to-all-done), channel_id=1, source_target_pairs={{0,8},{4,12},{8,0},{12,4},{1,9},{5,13},{9,1},{13,5},{2,10},{6,14},... | collective-permute-start | bytes 368648 | tf_op jit(solution)/shard_map/ppermute | solution.py:640
  27.5 8.7 %collective-permute-start.2 = (bf16[4,24,640]{2,1,0:T(8,128)(2,1)S(1)}, bf16[4,24,640]{2,1,0:T(8,128)(2,1)S(1)}, u32[]{:S(2)}, u32[]{:S(2)}) collective-permute-start(bf16[4,24,640]{2,1,0:T(8,128)(2,1)S(1)} %all-to-all-done), channel_id=1, source_target_pairs={{0,12},{4,0},{8,4},{12,8},{1,13},{5,1},{9,5},{13,9},{2,14},{6,2},{... | collective-permute-start | bytes 368648 | tf_op jit(solution)/shard_map/ppermute | solution.py:640
  36.3 24.5 %collective-permute-start.8 = (bf16[288,768]{1,0:T(8,128)(2,1)S(1)}, bf16[288,768]{1,0:T(8,128)(2,1)}, u32[]{:S(2)}, u32[]{:S(2)}) collective-permute-start(bf16[288,768]{1,0:T(8,128)(2,1)S(1)} %bitcast.144), channel_id=1, source_target_pairs={{0,1},{1,0},{2,3},{3,2},{4,5},{5,4},{6,7},{7,6},{8,9},{9,8},{10,11... | collective-permute-start | bytes 1327112 | tf_op jit(solution)/shard_map/ppermute | solution.py:580
  36.4 20.8 %collective-permute-start.12 = (bf16[4,4,24,640]{3,2,1,0:T(8,128)(2,1)S(1)}, bf16[4,4,24,640]{3,2,1,0:T(8,128)(2,1)S(1)}, u32[]{:S(2)}, u32[]{:S(2)}) collective-permute-start(bf16[4,4,24,640]{3,2,1,0:T(8,128)(2,1)S(1)} %bitcast_dynamic-update-slice_fusion.2), channel_id=1, source_target_pairs={{0,16},{16,0},{1,17},{17,1},{2,18},{18,2},{3,19},{19,3},{4,20},{20... | collective-permute-start | bytes 1474568 | tf_op jit(solution)/shard_map/ppermute | solution.py:580
  37.6 19.6 %collective-permute-start.5 = (bf16[288,768]{1,0:T(8,128)(2,1)S(1)}, bf16[288,768]{1,0:T(8,128)(2,1)}, u32[]{:S(2)}, u32[]{:S(2)}) collective-permute-start(bf16[288,768]{1,0:T(8,128)(2,1)S(1)} %bitcast.145), channel_id=1, source_target_pairs={{0,4},{4,8},{8,12},{12,0},{1,5},{5,9},{9,13},{13,1},{2,6},{6,10},{... | collective-permute-start | bytes 1327112 | tf_op jit(solution)/shard_map/ppermute | solution.py:660
  40.7 9.9 %collective-permute-start.7 = (bf16[288,768]{1,0:T(8,128)(2,1)S(1)}, bf16[288,768]{1,0:T(8,128)(2,1)}, u32[]{:S(2)}, u32[]{:S(2)}) collective-permute-start(bf16[288,768]{1,0:T(8,128)(2,1)S(1)} %collective-permute-done.3.refs_1_), channel_id=1, source_target_pairs={{0,2},{1,17},{2,0},{3,19},{16,18},{17,1},{18,16},{19,3},{4,6},{5,2... | collective-permute-start | bytes 1327112 | tf_op jit(solution)/shard_map/ppermute | solution.py:591
  43.1 18.8 %collective-permute-start.9 = (bf16[288,768]{1,0:T(8,128)(2,1)S(1)}, bf16[288,768]{1,0:T(8,128)(2,1)}, u32[]{:S(2)}, u32[]{:S(2)}) collective-permute-start(bf16[288,768]{1,0:T(8,128)(2,1)S(1)} %collective-permute-done.3.refs_1_), channel_id=1, source_target_pairs={{0,1},{1,0},{2,3},{3,2},{4,5},{5,4},{6,7},{7,6},{8,9},{9,8},{10,11... | collective-permute-start | bytes 1327112 | tf_op jit(solution)/shard_map/ppermute | solution.py:580
  50.6 13.0 %collective-permute-start.10 = (bf16[288,768]{1,0:T(8,128)(2,1)S(1)}, bf16[288,768]{1,0:T(8,128)(2,1)}, u32[]{:S(2)}, u32[]{:S(2)}) collective-permute-start(bf16[288,768]{1,0:T(8,128)(2,1)S(1)} %collective-permute-done.4.refs_2_), channel_id=1, source_target_pairs={{0,1},{1,0},{2,3},{3,2},{4,5},{5,4},{6,7},{7,6},{8,9},{9,8},{10,11... | collective-permute-start | bytes 1327112 | tf_op jit(solution)/shard_map/ppermute | solution.py:580
  57.2 17.8 %collective-permute-start.6 = (bf16[288,768]{1,0:T(8,128)(2,1)}, bf16[288,768]{1,0:T(8,128)(2,1)S(1)}, u32[]{:S(2)}, u32[]{:S(2)}) collective-permute-start(bf16[288,768]{1,0:T(8,128)(2,1)} %collective-permute-done.5.refs_0_), channel_id=1, source_target_pairs={{0,4},{4,8},{8,12},{12,0},{1,5},{5,9},{9,13},{13,1},{2,6},{6,10},{... | collective-permute-start | bytes 1327112 | tf_op jit(solution)/shard_map/ppermute | solution.py:660
  60.8 16.1 %collective-permute-start.16 = (bf16[288,768]{1,0:T(8,128)(2,1)}, bf16[288,768]{1,0:T(8,128)(2,1)}, u32[]{:S(2)}, u32[]{:S(2)}) collective-permute-start(bf16[288,768]{1,0:T(8,128)(2,1)} %collective-permute-done.5.refs_0_), channel_id=1, source_target_pairs={{0,16},{1,3},{2,18},{3,1},{16,0},{17,19},{18,2},{19,17},{4,20},{5,... | collective-permute-start | bytes 1327112 | tf_op jit(solution)/shard_map/ppermute | solution.py:591
  61.9 19.7 %collective-permute-start.17 = (bf16[288,768]{1,0:T(8,128)(2,1)}, bf16[288,768]{1,0:T(8,128)(2,1)}, u32[]{:S(2)}, u32[]{:S(2)}) collective-permute-start(bf16[288,768]{1,0:T(8,128)(2,1)} %collective-permute-done.5.refs_0_), channel_id=1, source_target_pairs={{0,2},{1,17},{2,0},{3,19},{16,18},{17,1},{18,16},{19,3},{4,6},{5,2... | collective-permute-start | bytes 1327112 | tf_op jit(solution)/shard_map/ppermute | solution.py:591
  63.5 18.1 %collective-permute-start.19 = (bf16[288,768]{1,0:T(8,128)(2,1)}, bf16[288,768]{1,0:T(8,128)(2,1)}, u32[]{:S(2)}, u32[]{:S(2)}) collective-permute-start(bf16[288,768]{1,0:T(8,128)(2,1)} %collective-permute-done.5.refs_0_), channel_id=1, source_target_pairs={{0,1},{1,0},{2,3},{3,2},{4,5},{5,4},{6,7},{7,6},{8,9},{9,8},{10,11... | collective-permute-start | bytes 1327112 | tf_op jit(solution)/shard_map/ppermute | solution.py:580
  76.9 10.7 %collective-permute-start.18 = (bf16[288,768]{1,0:T(8,128)(2,1)}, bf16[288,768]{1,0:T(8,128)(2,1)S(1)}, u32[]{:S(2)}, u32[]{:S(2)}) collective-permute-start(bf16[288,768]{1,0:T(8,128)(2,1)} %collective-permute-done.16.refs_1_), channel_id=1, source_target_pairs={{0,2},{1,17},{2,0},{3,19},{16,18},{17,1},{18,16},{19,3},{4,6},{5,2... | collective-permute-start | bytes 1327112 | tf_op jit(solution)/shard_map/ppermute | solution.py:591
  80.9 12.4 %collective-permute-start.14 = (bf16[288,768]{1,0:T(8,128)(2,1)S(1)}, bf16[288,768]{1,0:T(8,128)(2,1)S(1)}, u32[]{:S(2)}, u32[]{:S(2)}) collective-permute-start(bf16[288,768]{1,0:T(8,128)(2,1)S(1)} %collective-permute-done.6.refs_0_), channel_id=1, source_target_pairs={{0,16},{1,3},{2,18},{3,1},{16,0},{17,19},{18,2},{19,17},{4,20},{5,... | collective-permute-start | bytes 1327112 | tf_op jit(solution)/shard_map/ppermute | solution.py:591
  81.5 21.0 %collective-permute-start.20 = (bf16[288,768]{1,0:T(8,128)(2,1)}, bf16[288,768]{1,0:T(8,128)(2,1)S(1)}, u32[]{:S(2)}, u32[]{:S(2)}) collective-permute-start(bf16[288,768]{1,0:T(8,128)(2,1)} %collective-permute-done.16.refs_1_), channel_id=1, source_target_pairs={{0,1},{1,0},{2,3},{3,2},{4,5},{5,4},{6,7},{7,6},{8,9},{9,8},{10,11... | collective-permute-start | bytes 1327112 | tf_op jit(solution)/shard_map/ppermute | solution.py:580
  81.6 28.4 %collective-permute-start.13 = (bf16[288,768]{1,0:T(8,128)(2,1)S(1)}, bf16[288,768]{1,0:T(8,128)(2,1)S(1)}, u32[]{:S(2)}, u32[]{:S(2)}) collective-permute-start(bf16[288,768]{1,0:T(8,128)(2,1)S(1)} %collective-permute-done.6.refs_0_), channel_id=1, source_target_pairs={{0,4},{4,8},{8,12},{12,0},{1,5},{5,9},{9,13},{13,1},{2,6},{6,10},{... | collective-permute-start | bytes 1327112 | tf_op jit(solution)/shard_map/ppermute | solution.py:660
  81.6 21.5 %collective-permute-start.21 = (bf16[288,768]{1,0:T(8,128)(2,1)}, bf16[288,768]{1,0:T(8,128)(2,1)}, u32[]{:S(2)}, u32[]{:S(2)}) collective-permute-start(bf16[288,768]{1,0:T(8,128)(2,1)} %collective-permute-done.17.refs_2_), channel_id=1, source_target_pairs={{0,1},{1,0},{2,3},{3,2},{4,5},{5,4},{6,7},{7,6},{8,9},{9,8},{10,11... | collective-permute-start | bytes 1327112 | tf_op jit(solution)/shard_map/ppermute | solution.py:580
  87.6 15.7 %collective-permute-start.22 = (bf16[288,768]{1,0:T(8,128)(2,1)S(1)}, bf16[288,768]{1,0:T(8,128)(2,1)}, u32[]{:S(2)}, u32[]{:S(2)}) collective-permute-start(bf16[288,768]{1,0:T(8,128)(2,1)S(1)} %collective-permute-done.18.refs_3_), channel_id=1, source_target_pairs={{0,1},{1,0},{2,3},{3,2},{4,5},{5,4},{6,7},{7,6},{8,9},{9,8},{10,11... | collective-permute-start | bytes 1327112 | tf_op jit(solution)/shard_map/ppermute | solution.py:580
  93.3 16.7 %collective-permute-start.15 = (bf16[288,768]{1,0:T(8,128)(2,1)S(1)}, bf16[288,768]{1,0:T(8,128)(2,1)S(1)}, u32[]{:S(2)}, u32[]{:S(2)}) collective-permute-start(bf16[288,768]{1,0:T(8,128)(2,1)S(1)} %collective-permute-done.14.refs_1_), channel_id=1, source_target_pairs={{0,2},{1,17},{2,0},{3,19},{16,18},{17,1},{18,16},{19,3},{4,6},{5,2... | collective-permute-start | bytes 1327112 | tf_op jit(solution)/shard_map/ppermute | solution.py:591
  102.5 18.7 %collective-permute-start.26 = (bf16[288,768]{1,0:T(8,128)(2,1)S(1)}, bf16[288,768]{1,0:T(8,128)(2,1)}, u32[]{:S(2)}, u32[]{:S(2)}) collective-permute-start(bf16[288,768]{1,0:T(8,128)(2,1)S(1)} %collective-permute-done.6.refs_0_), channel_id=1, source_target_pairs={{0,2},{1,17},{2,0},{3,19},{16,18},{17,1},{18,16},{19,3},{4,6},{5,2... | collective-permute-start | bytes 1327112 | tf_op jit(solution)/shard_map/ppermute | solution.py:591
  103.2 19.2 %collective-permute-start.27 = (bf16[288,768]{1,0:T(8,128)(2,1)S(1)}, bf16[288,768]{1,0:T(8,128)(2,1)S(1)}, u32[]{:S(2)}, u32[]{:S(2)}) collective-permute-start(bf16[288,768]{1,0:T(8,128)(2,1)S(1)} %collective-permute-done.6.refs_0_), channel_id=1, source_target_pairs={{0,1},{1,0},{2,3},{3,2},{4,5},{5,4},{6,7},{7,6},{8,9},{9,8},{10,11... | collective-permute-start | bytes 1327112 | tf_op jit(solution)/shard_map/ppermute | solution.py:580
  110.0 19.0 %collective-permute-start.23 = (bf16[288,768]{1,0:T(8,128)(2,1)S(1)}, bf16[288,768]{1,0:T(8,128)(2,1)S(1)}, u32[]{:S(2)}, u32[]{:S(2)}) collective-permute-start(bf16[288,768]{1,0:T(8,128)(2,1)S(1)} %collective-permute-done.13.refs_0_), channel_id=1, source_target_pairs={{0,16},{1,3},{2,18},{3,1},{16,0},{17,19},{18,2},{19,17},{4,20},{5,... | collective-permute-start | bytes 1327112 | tf_op jit(solution)/shard_map/ppermute | solution.py:591
  110.2 20.9 %collective-permute-start.28 = (bf16[288,768]{1,0:T(8,128)(2,1)S(1)}, bf16[288,768]{1,0:T(8,128)(2,1)}, u32[]{:S(2)}, u32[]{:S(2)}) collective-permute-start(bf16[288,768]{1,0:T(8,128)(2,1)S(1)} %collective-permute-done.14.refs_1_), channel_id=1, source_target_pairs={{0,1},{1,0},{2,3},{3,2},{4,5},{5,4},{6,7},{7,6},{8,9},{9,8},{10,11... | collective-permute-start | bytes 1327112 | tf_op jit(solution)/shard_map/ppermute | solution.py:580
  121.3 11.3 %collective-permute-start.29 = (bf16[288,768]{1,0:T(8,128)(2,1)}, bf16[288,768]{1,0:T(8,128)(2,1)}, u32[]{:S(2)}, u32[]{:S(2)}) collective-permute-start(bf16[288,768]{1,0:T(8,128)(2,1)} %collective-permute-done.26.refs_2_), channel_id=1, source_target_pairs={{0,1},{1,0},{2,3},{3,2},{4,5},{5,4},{6,7},{7,6},{8,9},{9,8},{10,11... | collective-permute-start | bytes 1327112 | tf_op jit(solution)/shard_map/ppermute | solution.py:580
  121.3 18.5 %collective-permute-start.24 = (bf16[288,768]{1,0:T(8,128)(2,1)S(1)}, bf16[288,768]{1,0:T(8,128)(2,1)}, u32[]{:S(2)}, u32[]{:S(2)}) collective-permute-start(bf16[288,768]{1,0:T(8,128)(2,1)S(1)} %collective-permute-done.13.refs_0_), channel_id=1, source_target_pairs={{0,2},{1,17},{2,0},{3,19},{16,18},{17,1},{18,16},{19,3},{4,6},{5,2... | collective-permute-start | bytes 1327112 | tf_op jit(solution)/shard_map/ppermute | solution.py:591
  122.4 17.4 %collective-permute-start.30 = (bf16[288,768]{1,0:T(8,128)(2,1)S(1)}, bf16[288,768]{1,0:T(8,128)(2,1)}, u32[]{:S(2)}, u32[]{:S(2)}) collective-permute-start(bf16[288,768]{1,0:T(8,128)(2,1)S(1)} %collective-permute-done.15.refs_3_), channel_id=1, source_target_pairs={{0,1},{1,0},{2,3},{3,2},{4,5},{5,4},{6,7},{7,6},{8,9},{9,8},{10,11... | collective-permute-start | bytes 1327112 | tf_op jit(solution)/shard_map/ppermute | solution.py:580
  129.0 16.8 %collective-permute-start.25 = (bf16[288,768]{1,0:T(8,128)(2,1)S(1)}, bf16[288,768]{1,0:T(8,128)(2,1)S(1)}, u32[]{:S(2)}, u32[]{:S(2)}) collective-permute-start(bf16[288,768]{1,0:T(8,128)(2,1)S(1)} %collective-permute-done.23.refs_1_), channel_id=1, source_target_pairs={{0,2},{1,17},{2,0},{3,19},{16,18},{17,1},{18,16},{19,3},{4,6},{5,2... | collective-permute-start | bytes 1327112 | tf_op jit(solution)/shard_map/ppermute | solution.py:591
  131.1 17.4 %collective-permute-start.31 = (bf16[288,768]{1,0:T(8,128)(2,1)S(1)}, bf16[288,768]{1,0:T(8,128)(2,1)S(1)}, u32[]{:S(2)}, u32[]{:S(2)}) collective-permute-start(bf16[288,768]{1,0:T(8,128)(2,1)S(1)} %collective-permute-done.13.refs_0_), channel_id=1, source_target_pairs={{0,1},{1,0},{2,3},{3,2},{4,5},{5,4},{6,7},{7,6},{8,9},{9,8},{10,11... | collective-permute-start | bytes 1327112 | tf_op jit(solution)/shard_map/ppermute | solution.py:580
  132.5 15.9 %collective-permute-start.32 = (bf16[288,768]{1,0:T(8,128)(2,1)S(1)}, bf16[288,768]{1,0:T(8,128)(2,1)}, u32[]{:S(2)}, u32[]{:S(2)}) collective-permute-start(bf16[288,768]{1,0:T(8,128)(2,1)S(1)} %collective-permute-done.23.refs_1_), channel_id=1, source_target_pairs={{0,1},{1,0},{2,3},{3,2},{4,5},{5,4},{6,7},{7,6},{8,9},{9,8},{10,11... | collective-permute-start | bytes 1327112 | tf_op jit(solution)/shard_map/ppermute | solution.py:580
  139.8 8.7 %collective-permute-start.33 = (bf16[288,768]{1,0:T(8,128)(2,1)}, bf16[288,768]{1,0:T(8,128)(2,1)}, u32[]{:S(2)}, u32[]{:S(2)}) collective-permute-start(bf16[288,768]{1,0:T(8,128)(2,1)} %collective-permute-done.24.refs_2_), channel_id=1, source_target_pairs={{0,1},{1,0},{2,3},{3,2},{4,5},{5,4},{6,7},{7,6},{8,9},{9,8},{10,11... | collective-permute-start | bytes 1327112 | tf_op jit(solution)/shard_map/ppermute | solution.py:580
  168.9 13.0 %all-to-all-start.1 = ((bf16[4,3,96,256]{3,2,1,0:T(8,128)(2,1)}), bf16[4,3,96,256]{3,2,1,0:T(8,128)(2,1)S(1)}, u32[]{:S(2)}, u32[]{:S(2)}) async-start(bf16[4,3,96,256]{3,2,1,0:T(8,128)(2,1)} %attend_forward.1), calls=%async_computation.1 | async-start | bytes 1179648 | tf_op jit(solution)/shard_map/all_to_all | solution.py:692
  207.9 9.3 %collective-permute-start.35 = (bf16[384,7040]{1,0:T(8,128)(2,1)}, bf16[384,7040]{1,0:T(8,128)(2,1)}, u32[]{:S(2)}, u32[]{:S(2)}) collective-permute-start(bf16[384,7040]{1,0:T(8,128)(2,1)} %get-tuple-element.82), channel_id=1, source_target_pairs={{0,1},{1,0},{2,3},{3,2},{4,5},{5,4},{6,7},{7,6},{8,9},{9,8},{10,11... | collective-permute-start | bytes 16220168 | tf_op jit(solution)/shard_map/ppermute | solution.py:580
  208.0 15.2 %all-to-all-start.2 = ((bf16[4,3,96,256]{3,2,1,0:T(8,128)(2,1)}), bf16[4,3,96,256]{3,2,1,0:T(8,128)(2,1)S(1)}, u32[]{:S(2)}, u32[]{:S(2)}) async-start(bf16[4,3,96,256]{3,2,1,0:T(8,128)(2,1)} %bitcast.137), calls=%async_computation.2 | async-start | bytes 1179648 | tf_op jit(solution)/shard_map/all_to_all | solution.py:711
  223.2 34.3 %collective-permute-start.39 = (bf16[192,7040]{1,0:T(8,128)(2,1)}, bf16[192,7040]{1,0:T(8,128)(2,1)}, u32[]{:S(2)}, u32[]{:S(2)}) collective-permute-start(bf16[192,7040]{1,0:T(8,128)(2,1)} %get-tuple-element.86), channel_id=1, source_target_pairs={{0,16},{1,3},{2,18},{3,1},{16,0},{17,19},{18,2},{19,17},{4,20},{5,... | collective-permute-start | bytes 8110088 | tf_op jit(solution)/shard_map/ppermute | solution.py:591
  223.5 17.4 %collective-permute-start.36 = (bf16[4,3,96,256]{3,2,1,0:T(8,128)(2,1)S(1)}, bf16[4,3,96,256]{3,2,1,0:T(8,128)(2,1)}, u32[]{:S(2)}, u32[]{:S(2)}) collective-permute-start(bf16[4,3,96,256]{3,2,1,0:T(8,128)(2,1)S(1)} %all-to-all-done.2.load_ref), channel_id=1, source_target_pairs={{0,4},{4,8},{8,12},{12,0},{1,5},{5,9},{9,13},{13,1},{2,6},{6,10},{... | collective-permute-start | bytes 1769480 | tf_op jit(solution)/shard_map/ppermute | solution.py:721
  240.9 16.6 %collective-permute-start.37 = (bf16[4,3,96,256]{3,2,1,0:T(8,128)(2,1)}, bf16[4,3,96,256]{3,2,1,0:T(8,128)(2,1)S(1)}, u32[]{:S(2)}, u32[]{:S(2)}) collective-permute-start(bf16[4,3,96,256]{3,2,1,0:T(8,128)(2,1)} %collective-permute-done.36.load_ref), channel_id=1, source_target_pairs={{0,4},{4,8},{8,12},{12,0},{1,5},{5,9},{9,13},{13,1},{2,6},{6,10},{... | collective-permute-start | bytes 1769480 | tf_op jit(solution)/shard_map/ppermute | solution.py:721
  260.4 43.0 %collective-permute-start.43 = (bf16[96,7040]{1,0:T(8,128)(2,1)}, bf16[96,7040]{1,0:T(8,128)(2,1)}, u32[]{:S(2)}, u32[]{:S(2)}) collective-permute-start(bf16[96,7040]{1,0:T(8,128)(2,1)} %add_convert_fusion.5), channel_id=1, source_target_pairs={{0,2},{1,17},{2,0},{3,19},{16,18},{17,1},{18,16},{19,3},{4,6},{5,2... | collective-permute-start | bytes 4055048 | tf_op jit(solution)/shard_map/ppermute | solution.py:591
  263.7 22.5 %collective-permute-start.38 = (bf16[4,3,96,256]{3,2,1,0:T(8,128)(2,1)S(1)}, bf16[4,3,96,256]{3,2,1,0:T(8,128)(2,1)S(1)}, u32[]{:S(2)}, u32[]{:S(2)}) collective-permute-start(bf16[4,3,96,256]{3,2,1,0:T(8,128)(2,1)S(1)} %collective-permute-done.37.load_ref), channel_id=1, source_target_pairs={{0,4},{4,8},{8,12},{12,0},{1,5},{5,9},{9,13},{13,1},{2,6},{6,10},{... | collective-permute-start | bytes 1769480 | tf_op jit(solution)/shard_map/ppermute | solution.py:721
  308.7 27.5 %collective-permute-start.41 = (bf16[2,288,768]{2,1,0:T(8,128)(2,1)}, bf16[2,288,768]{2,1,0:T(8,128)(2,1)}, u32[]{:S(2)}, u32[]{:S(2)}) collective-permute-start(bf16[2,288,768]{2,1,0:T(8,128)(2,1)} %slice_bitcast_fusion), channel_id=1, source_target_pairs={{0,16},{1,3},{2,18},{3,1},{16,0},{17,19},{18,2},{19,17},{4,20},{5,... | collective-permute-start | bytes 2654216 | tf_op jit(solution)/shard_map/ppermute | solution.py:591
  309.6 12.7 %collective-permute-start.44 = (bf16[24,7040]{1,0:T(8,128)(2,1)S(1)}, bf16[24,7040]{1,0:T(8,128)(2,1)S(1)}, u32[]{:S(2)}, u32[]{:S(2)}) collective-permute-start(bf16[24,7040]{1,0:T(8,128)(2,1)S(1)} %get-tuple-element.168), channel_id=1, source_target_pairs={{0,4},{4,8},{8,12},{12,0},{1,5},{5,9},{9,13},{13,1},{2,6},{6,10},{... | collective-permute-start | bytes 1013768 | tf_op jit(solution)/shard_map/ppermute | solution.py:740
  309.6 29.6 %collective-permute-start.45 = (bf16[24,7040]{1,0:T(8,128)(2,1)}, bf16[24,7040]{1,0:T(8,128)(2,1)}, u32[]{:S(2)}, u32[]{:S(2)}) collective-permute-start(bf16[24,7040]{1,0:T(8,128)(2,1)} %get-tuple-element.166), channel_id=1, source_target_pairs={{0,8},{4,12},{8,0},{12,4},{1,9},{5,13},{9,1},{13,5},{2,10},{6,14},... | collective-permute-start | bytes 1013768 | tf_op jit(solution)/shard_map/ppermute | solution.py:740
  312.0 27.2 %collective-permute-start.46 = (bf16[24,7040]{1,0:T(8,128)(2,1)}, bf16[24,7040]{1,0:T(8,128)(2,1)}, u32[]{:S(2)}, u32[]{:S(2)}) collective-permute-start(bf16[24,7040]{1,0:T(8,128)(2,1)} %get-tuple-element.167), channel_id=1, source_target_pairs={{0,12},{4,0},{8,4},{12,8},{1,13},{5,1},{9,5},{13,9},{2,14},{6,2},{... | collective-permute-start | bytes 1013768 | tf_op jit(solution)/shard_map/ppermute | solution.py:740
  322.3 42.1 %all-to-all-start.3 = ((bf16[32,24,640]{2,1,0:T(8,128)(2,1)}), bf16[32,24,640]{2,1,0:T(8,128)(2,1)S(1)}, u32[]{:S(2)}, u32[]{:S(2)}) async-start(bf16[32,24,640]{2,1,0:T(8,128)(2,1)} %bitcast.136), calls=%async_computation.3 | async-start | bytes 1966080 | tf_op jit(solution)/shard_map/all_to_all | solution.py:745
  337.4 13.5 %collective-permute-start.42 = (bf16[288,768]{1,0:T(8,128)(2,1)S(1)}, bf16[288,768]{1,0:T(8,128)(2,1)}, u32[]{:S(2)}, u32[]{:S(2)}) collective-permute-start(bf16[288,768]{1,0:T(8,128)(2,1)S(1)} %fusion), channel_id=1, source_target_pairs={{0,2},{1,17},{2,0},{3,19},{16,18},{17,1},{18,16},{19,3},{4,6},{5,2... | collective-permute-start | bytes 1327112 | tf_op jit(solution)/shard_map/ppermute | solution.py:591
  (39 other events, 453.0 us)
Sparse Core Ops, SparseCore 0:
  36.4 118.4 all-gather.1
